TPU v7x, 32 devices: a whole 2x2x4 slice. The times are simulated.
32 devices in a mesh: wide: 8 (over y, x, core), narrow: 4 (over z).
Axes of the slice: x: 2, y: 2, z: 4, core: 2. Of those that a mesh axis runs over, the one named last changes fastest.
Arguments:
- features: bfloat16 [32768, 512], P(('wide', 'narrow')), may hold values from -240 to 240
- presence: int32 [32768, 8], P(('wide', 'narrow')), may hold values 0 or 1
- first_params: bfloat16 [1196032], P(('wide', 'narrow')), may hold values from -4 to 4
- second_params: bfloat16 [880640], P(('wide', 'narrow')), may hold values from -4 to 4
- cotangent: bfloat16 [32768, 128], P(('wide', 'narrow')), may hold values from -6 to 6
Outputs:
- towers: float32 [32768, 128], P(('wide', 'narrow'))
- input_grad: float32 [32768, 512], P(('wide', 'narrow'))
- first_grad: float32 [1196032], P(('wide', 'narrow'))
- second_grad: float32 [880640], P(('wide', 'narrow'))
All inputs are finite; a program needn't handle non-finite values. No bound on the sum of `presence` on one device may be relied on, other than what follows from the above.
Results may differ from a plain program's by a relative error of at most 0.0093.
Values may be sent and summed in bfloat16 or wider, within the bound.
No kernel may reach another device: no remote copies, remote signals or barrier semaphores. Data moves between devices by JAX's collectives and lax.ppermute only.
A program may use at most 192 MiB of HBM per device.

v0:
```python
import math

import jax
import jax.numpy as jnp
from jax import lax
from jax.sharding import PartitionSpec as P

H = 256
TOWER1 = 128
TOWER2 = 64


EPSILON = 1e-05


def cut_pieces(flat_vector, shapes):
    pieces = []
    offset = 0
    for shape_now in shapes:
        amount = math.prod(shape_now)
        pieces.append(flat_vector[offset : offset + amount].reshape(shape_now))
        offset += amount
    return pieces


def pack_flat(pieces, length):
    joined = jnp.concatenate([piece.reshape(-1) for piece in pieces])
    return jnp.pad(joined, (0, length - joined.shape[0]))


def silu_slope(values):
    sigmoid_part = jax.nn.sigmoid(values)
    return sigmoid_part * (1.0 + values * (1.0 - sigmoid_part))


def softmax_back(probabilities, gradients):
    return probabilities * (gradients - jnp.sum(probabilities * gradients, axis=-1, keepdims=True))


def mix_parts(weights, parts):
    running = weights[:, 0:1] * parts[0]
    for position in range(1, len(parts)):
        running = running + weights[:, position : position + 1] * parts[position]
    return running


def add_into(targets, member, value):
    if targets[member] is None:
        targets[member] = value
    else:
        targets[member] = targets[member] + value


def expert_forward(inputs, expert_in, in_bias, expert_out, out_bias, norm_gain, norm_bias):
    groups = inputs.shape[0]
    per_group = 6 // groups
    row_count = inputs.shape[1]
    hidden = expert_in.shape[2]
    weight_in = expert_in.reshape(groups, per_group, expert_in.shape[1], hidden)
    weight_out = expert_out.reshape(groups, per_group, hidden, hidden)
    pre_act = jnp.einsum("grd,gedh->gerh", inputs, weight_in, preferred_element_type=jnp.float32)
    pre_act = pre_act + in_bias.astype(jnp.float32).reshape(groups, per_group, 1, hidden)
    active = jax.nn.silu(pre_act).astype(jnp.bfloat16)
    post_act = jnp.einsum("gerh,gehk->gerk", active, weight_out, preferred_element_type=jnp.float32)
    post_act = post_act + out_bias.astype(jnp.float32).reshape(groups, per_group, 1, hidden)
    centred = post_act - jnp.mean(post_act, axis=-1, keepdims=True)
    norm_scale = lax.rsqrt(jnp.mean(centred * centred, axis=-1, keepdims=True) + EPSILON)
    normal_out = centred * norm_scale
    gain_full = norm_gain.astype(jnp.float32).reshape(groups, per_group, 1, hidden)
    outputs = normal_out * gain_full + norm_bias.astype(jnp.float32).reshape(
        groups, per_group, 1, hidden
    )
    saved = (pre_act, active, normal_out, norm_scale, weight_in, weight_out, gain_full)
    return (outputs.reshape(6, row_count, hidden), saved)


def expert_backward(inputs, out_grads, saved):
    pre_act, active, normal_out, norm_scale, weight_in, weight_out, gain_full = saved
    groups = active.shape[0]
    per_group = active.shape[1]
    out_grads = out_grads.reshape(groups, per_group, out_grads.shape[1], out_grads.shape[2])
    grad_gain = jnp.sum(out_grads * normal_out, axis=2)
    grad_bias = jnp.sum(out_grads, axis=2)
    scaled = out_grads * gain_full
    post_grad = norm_scale * (
        scaled
        - jnp.mean(scaled, axis=-1, keepdims=True)
        - normal_out * jnp.mean(scaled * normal_out, axis=-1, keepdims=True)
    )
    post_low = post_grad.astype(jnp.bfloat16)
    grad_out = jnp.einsum("gerh,gerk->gehk", active, post_low, preferred_element_type=jnp.float32)
    grad_out_bias = jnp.sum(post_low.astype(jnp.float32), axis=2)
    act_grad = jnp.einsum(
        "gerk,gehk->gerh", post_low, weight_out, preferred_element_type=jnp.float32
    )
    pre_low = (act_grad * silu_slope(pre_act)).astype(jnp.bfloat16)
    grad_in = jnp.einsum("grd,gerh->gedh", inputs, pre_low, preferred_element_type=jnp.float32)
    grad_in_bias = jnp.sum(pre_low.astype(jnp.float32), axis=2)
    input_grads = jnp.einsum(
        "gerh,gedh->grd", pre_low, weight_in, preferred_element_type=jnp.float32
    )
    return (input_grads, [grad_in, grad_in_bias, grad_out, grad_out_bias, grad_gain, grad_bias])


def per_device(features, presence, first_params, second_params, cotangent):
    row_count = features.shape[0]
    feature_width = features.shape[1]
    devices_all = lax.axis_size(("wide", "narrow"))
    total_rows = row_count * devices_all
    mask_full = jnp.repeat(presence.astype(jnp.float32), feature_width // presence.shape[1], axis=1)
    masked = features.astype(jnp.float32) * mask_full
    column_mean = lax.psum(jnp.sum(masked, axis=0), ("wide", "narrow")) / total_rows
    variance = (
        lax.psum(jnp.sum(jnp.square(masked - column_mean), axis=0), ("wide", "narrow")) / total_rows
    )
    inv_scale = lax.rsqrt(variance + EPSILON)
    first_full = lax.all_gather(first_params, ("wide", "narrow"), axis=0, tiled=True)
    second_full = lax.all_gather(second_params, ("wide", "narrow"), axis=0, tiled=True)
    (
        in_gain,
        in_bias,
        expert_in,
        expert_in_bias,
        expert_out,
        expert_out_bias,
        norm_gain,
        norm_bias,
        gate_table,
    ) = cut_pieces(
        first_full,
        [
            (feature_width,),
            (feature_width,),
            (6, feature_width, H),
            (6, H),
            (6, H, H),
            (6, H),
            (6, H),
            (6, H),
            (feature_width, 14),
        ],
    )
    (
        expert_in_two,
        in_bias_two,
        expert_out_two,
        out_bias_two,
        norm_gain_two,
        norm_bias_two,
        gate_table_two,
        tower_in,
        tower_in_bias,
        tower_out,
        tower_out_bias,
    ) = cut_pieces(
        second_full,
        [
            (6, H, H),
            (6, H),
            (6, H, H),
            (6, H),
            (6, H),
            (6, H),
            (2, H, 4),
            (2, H, TOWER1),
            (2, TOWER1),
            (2, TOWER1, TOWER2),
            (2, TOWER2),
        ],
    )
    normed = (masked - column_mean) * inv_scale
    level_input = (normed * in_gain.astype(jnp.float32) + in_bias.astype(jnp.float32)).astype(
        jnp.bfloat16
    )
    outputs_one, saved_one = expert_forward(
        level_input[None],
        expert_in,
        expert_in_bias,
        expert_out,
        expert_out_bias,
        norm_gain,
        norm_bias,
    )
    logits_one = jnp.dot(level_input, gate_table, preferred_element_type=jnp.float32)
    probs_one = [
        jax.nn.softmax(logits_one[:, 0:4], axis=-1),
        jax.nn.softmax(logits_one[:, 4:8], axis=-1),
        jax.nn.softmax(logits_one[:, 8:14], axis=-1),
    ]
    groups_one = [[0, 1, 4, 5], [2, 3, 4, 5], [0, 1, 2, 3, 4, 5]]
    mixed = [
        mix_parts(
            probs_one[group_index], [outputs_one[member] for member in groups_one[group_index]]
        )
        for group_index in range(3)
    ]
    second_input = jnp.stack(mixed).astype(jnp.bfloat16)
    outputs_two, saved_two = expert_forward(
        second_input,
        expert_in_two,
        in_bias_two,
        expert_out_two,
        out_bias_two,
        norm_gain_two,
        norm_bias_two,
    )
    logits_two = jnp.einsum(
        "trh,thk->trk", second_input[0:2], gate_table_two, preferred_element_type=jnp.float32
    )
    probs_two = jax.nn.softmax(logits_two, axis=-1)
    groups_two = [[0, 1, 4, 5], [2, 3, 4, 5]]
    combined = jnp.stack(
        [
            mix_parts(
                probs_two[task_index], [outputs_two[member] for member in groups_two[task_index]]
            )
            for task_index in range(2)
        ]
    ).astype(jnp.bfloat16)
    tower_pre = jnp.einsum("trh,thk->trk", combined, tower_in, preferred_element_type=jnp.float32)
    tower_pre = tower_pre + tower_in_bias.astype(jnp.float32)[:, None, :]
    tower_act = jax.nn.silu(tower_pre).astype(jnp.bfloat16)
    task_out = jnp.einsum("trk,tkj->trj", tower_act, tower_out, preferred_element_type=jnp.float32)
    task_out = task_out + tower_out_bias.astype(jnp.float32)[:, None, :]
    towers = jnp.concatenate([task_out[0], task_out[1]], axis=1)
    out_grad = jnp.stack([cotangent[:, :TOWER2], cotangent[:, TOWER2:]])
    grad_tower_out = jnp.einsum(
        "trk,trj->tkj", tower_act, out_grad, preferred_element_type=jnp.float32
    )
    grad_tower_out_bias = jnp.sum(out_grad.astype(jnp.float32), axis=1)
    act_grad = jnp.einsum("trj,tkj->trk", out_grad, tower_out, preferred_element_type=jnp.float32)
    tower_pre_low = (act_grad * silu_slope(tower_pre)).astype(jnp.bfloat16)
    grad_tower_in = jnp.einsum(
        "trh,trk->thk", combined, tower_pre_low, preferred_element_type=jnp.float32
    )
    grad_tower_in_bias = jnp.sum(tower_pre_low.astype(jnp.float32), axis=1)
    combined_grad = jnp.einsum(
        "trk,thk->trh", tower_pre_low, tower_in, preferred_element_type=jnp.float32
    )
    expert_grads_two = [None] * 6
    logit_grads_two = []
    for task_index in range(2):
        members = groups_two[task_index]
        gate_grad = jnp.stack(
            [
                jnp.sum(combined_grad[task_index] * outputs_two[member], axis=-1)
                for member in members
            ],
            axis=-1,
        )
        logit_grads_two.append(softmax_back(probs_two[task_index], gate_grad))
        for position, member in enumerate(members):
            add_into(
                expert_grads_two,
                member,
                probs_two[task_index][:, position : position + 1] * combined_grad[task_index],
            )
    logit_low_two = jnp.stack(logit_grads_two).astype(jnp.bfloat16)
    grad_gate_two = jnp.einsum(
        "trh,trk->thk", second_input[0:2], logit_low_two, preferred_element_type=jnp.float32
    )
    input_grads_two, weights_two = expert_backward(
        second_input, jnp.stack(expert_grads_two), saved_two
    )
    gate_input_grad = jnp.einsum(
        "trk,thk->trh", logit_low_two, gate_table_two, preferred_element_type=jnp.float32
    )
    mixed_grad = input_grads_two + jnp.concatenate(
        [gate_input_grad, jnp.zeros((1, row_count, H), jnp.float32)], axis=0
    )
    second_whole = pack_flat(
        weights_two
        + [grad_gate_two, grad_tower_in, grad_tower_in_bias, grad_tower_out, grad_tower_out_bias],
        second_params.shape[0] * devices_all,
    )
    second_grad = lax.psum_scatter(
        second_whole, ("wide", "narrow"), scatter_dimension=0, tiled=True
    )
    expert_grads_one = [None] * 6
    logit_grads_one = []
    for group_index in range(3):
        members = groups_one[group_index]
        gate_grad = jnp.stack(
            [jnp.sum(mixed_grad[group_index] * outputs_one[member], axis=-1) for member in members],
            axis=-1,
        )
        logit_grads_one.append(softmax_back(probs_one[group_index], gate_grad))
        for position, member in enumerate(members):
            add_into(
                expert_grads_one,
                member,
                probs_one[group_index][:, position : position + 1] * mixed_grad[group_index],
            )
    logit_low_one = jnp.concatenate(logit_grads_one, axis=1).astype(jnp.bfloat16)
    grad_gate_one = jnp.einsum(
        "rd,rk->dk", level_input, logit_low_one, preferred_element_type=jnp.float32
    )
    input_grads_one, weights_one = expert_backward(
        level_input[None], jnp.stack(expert_grads_one), saved_one
    )
    level_grad = input_grads_one[0] + jnp.einsum(
        "rk,dk->rd", logit_low_one, gate_table, preferred_element_type=jnp.float32
    )
    grad_in_gain = jnp.sum(level_grad * normed, axis=0)
    grad_in_bias = jnp.sum(level_grad, axis=0)
    scaled = level_grad * in_gain.astype(jnp.float32)
    plain_total, cross_total = lax.psum(
        (jnp.sum(scaled, axis=0), jnp.sum(scaled * normed, axis=0)), ("wide", "narrow")
    )
    input_grad = (
        mask_full
        * inv_scale
        * (scaled - plain_total / total_rows - normed * cross_total / total_rows)
    )
    first_whole = pack_flat(
        [grad_in_gain, grad_in_bias] + weights_one + [grad_gate_one],
        first_params.shape[0] * devices_all,
    )
    first_grad = lax.psum_scatter(first_whole, ("wide", "narrow"), scatter_dimension=0, tiled=True)
    return (towers, input_grad, first_grad, second_grad)


def solution(mesh):
    placed = (
        P(("wide", "narrow"), None),
        P(("wide", "narrow"), None),
        P(("wide", "narrow")),
        P(("wide", "narrow")),
        P(("wide", "narrow"), None),
    )
    return jax.shard_map(
        per_device,
        mesh=mesh,
        in_specs=placed,
        out_specs=(
            P(("wide", "narrow"), None),
            P(("wide", "narrow"), None),
            P(("wide", "narrow")),
            P(("wide", "narrow")),
        ),
        check_vma=False,
    )
```

profile of v0, /device:TPU:0, one launch (start us, length us, event | category | flops | bytes accessed | tf_op | source)
XLA Modules:
  0.0 635.3 jit_solution(4795590439869061348)
XLA Ops:
  15.3 42.2 %psum.28 = f32[512]{0:T(512)S(1)} all-reduce(f32[512]{0:T(512)S(1)} %fusion.93), channel_id=1, replica_groups=mesh['wide'=8,'narrow'=4] {'wide','narrow'}, use_global_device_ids=true, to_apply=%region_1.0 | all-reduce | flops 512 | bytes 4096 | tf_op jit(solution)/shard_map/psum | solution.py:112
  58.0 40.2 %psum.29 = f32[512]{0:T(512)S(1)} all-reduce(f32[512]{0:T(512)S(1)} %multiply_reduce_fusion.10), channel_id=1, replica_groups=mesh['wide'=8,'narrow'=4] {'wide','narrow'}, use_global_device_ids=true, to_apply=%region_3.0 | all-reduce | flops 512 | bytes 4096 | tf_op jit(solution)/shard_map/psum | solution.py:114
  102.1 38.9 %reduce.25 = bf16[32,27520]{1,0:T(8,128)(2,1)} reduce(bf16[32,1,27520]{2,1,0:T(2,128)(2,1)} %all-gather.7.cloned.1.call-done, bf16[]{:T(256)} %constant.53), dimensions={1}, to_apply=%all-gather.1.reduce_sub_computation | reduce | bytes 3522562 | tf_op jit(solution)/shard_map/all_gather | solution.py:118
  141.0 4.8 reshape.1447
  161.0 38.1 %reduce.24 = bf16[32,37376]{1,0:T(8,128)(2,1)} reduce(bf16[32,1,37376]{2,1,0:T(2,128)(2,1)} %all-gather.5.cloned.1.call-done, bf16[]{:T(256)} %constant.53), dimensions={1}, to_apply=%all-gather.reduce_sub_computation | reduce | bytes 4784130 | tf_op jit(solution)/shard_map/all_gather | solution.py:117
  199.1 6.0 reshape.1445
  229.7 4.2 fusion.6
  257.7 3.6 add_convert_fusion.2
  272.9 6.8 %copy.94 = f32[6,1024,256]{1,2,0:T(8,128)} copy(f32[6,1024,256]{2,1,0:T(8,128)} %copy-done.5) | data formatting | bytes 12582912 | tf_op jit(solution)/shard_map/stack | solution.py:263
  279.6 6.6 %multiply_reduce_fusion = (f32[3,2,256]{2,1,0:T(2,128)}, f32[3,2,1024]{2,1,0:T(2,128)S(1)}) fusion(f32[3,2,1024,256]{2,3,1,0:T(8,128)} %bitcast.374, f32[3,2,1024]{2,1,0:T(2,128)S(1)} %add_rsqrt_fusion.1, f32[3,2,1024]{2,1,0:T(2,128)S(1)} %broadcast_multiply_fusion.5, f32[3,2,1024,256]{2,3,1,0:T(8,128)} %copy-done, f32[3,2,256]{2,1,0:T(2,128)S(1)} %reshape.1440, ...), kind=kLoop, calls=%fused_computation.16 | loop fusion | flops 12575232 | bytes 12675072 | tf_op jit(solution)/shard_map/reduce_sum | solution.py:82
  291.3 6.8 %convert_reduce_fusion = (f32[3,2,256]{2,1,0:T(2,128)}, bf16[3,2,1024,256]{2,3,1,0:T(8,128)(2,1)S(1)}) fusion(f32[3,2,1024]{2,1,0:T(2,128)} %broadcast_multiply_fusion.4, f32[3,2,1024]{2,1,0:T(2,128)S(1)} %broadcast_multiply_fusion.5, f32[3,2,1024,256]{2,3,1,0:T(8,128)} %copy-done, f32[3,2,256]{2,1,0:T(2,128)S(1)} %reshape.1440, f32[3,2,1024]{2,1,0:T(2,128)S(1)} %div.106, ...), kind=kLoop, calls=%fused_computation.17 | loop fusion | flops 17299968 | bytes 15845376 | tf_op jit(solution)/shard_map/reduce_sum | solution.py:92
  298.1 5.9 convert_reduce_fusion.1
  312.2 3.4 multiply_reduce_fusion.1
  316.2 4.0 convert_reduce_fusion.2
  320.2 3.8 convert_reduce_fusion.3
  324.1 3.2 fusion.13
  327.3 3.5 fusion.19
  330.8 3.3 fusion.15
  346.9 4.5 multiply_reduce_fusion.8
  351.4 3.8 copy.99
  355.2 5.2 copy.149
  361.7 3.4 copy.150
  369.1 3.1 copy.105
  376.3 3.4 copy.153
  386.7 3.8 constant_dynamic-update-slice_fusion.9
  391.8 14.6 %dynamic-update-slice.15 = f32[1193984]{0:T(1024)} dynamic-update-slice(f32[1193984]{0:T(1024)} %constant_dynamic-update-slice_fusion.8, f32[393216]{0:T(1024)} %bitcast.383, s32[]{} %constant.69) | dynamic-update-slice | bytes 3145732
  411.0 4.1 pad.9
  416.4 14.7 %dynamic-update-slice.2 = f32[876928]{0:T(1024)} dynamic-update-slice(f32[876928]{0:T(1024)} %constant_dynamic-update-slice_fusion.19, f32[393216]{0:T(1024)} %bitcast.384, s32[]{} %constant.57) | dynamic-update-slice | bytes 3145732
  440.4 4.0 pad.10
  449.5 42.0 %all-reduce.5 = (f32[512]{0:T(512)S(1)}, f32[512]{0:T(512)S(1)}) all-reduce(f32[512]{0:T(512)S(1)} %get-tuple-element.38, f32[512]{0:T(512)S(1)} %copy-done.109), channel_id=1, replica_groups=mesh['wide'=8,'narrow'=4] {'wide','narrow'}, use_global_device_ids=true, to_apply=%region_50.51 | all-reduce | flops 1024 | bytes 8192 | tf_op jit(solution)/shard_map/psum | solution.py:307
  491.5 3.7 subtract_multiply_fusion.2
  495.2 130.0 %all-reduce.9.cloned.1.call-done = (f32[1196032]{0:T(1024)}, f32[880640]{0:T(1024)}) async-done(((f32[1196032]{0:T(1024)}, f32[880640]{0:T(1024)}), (f32[1196032]{0:T(1024)}, f32[880640]{0:T(1024)})) %all-reduce.9.cloned.1.call-update) | async-done | bytes 8306704
  (426 shorter events, 154.0 us)
Async XLA Ops:
  7.2 94.9 %all-gather.7.cloned.1.call-start = ((), (), s32[]{:S(2)}) async-start(), calls=%async_computation.1 | async-start | bytes 3632640 | tf_op jit(solution)/shard_map/all_gather | solution.py:118
  8.8 152.2 %all-gather.5.cloned.1.call-start = ((), (), s32[]{:S(2)}) async-start(), calls=%async_computation | async-start | bytes 4933632 | tf_op jit(solution)/shard_map/all_gather | solution.py:117
  10.5 614.7 %all-reduce.9.cloned.1.call-start = ((), (), s32[]{:S(2)}) async-start(), calls=%async_computation.2 | async-start | bytes 16613376
  12.9 85.3 %copy-start.24 = (bf16[1024,128]{1,0:T(8,128)(2,1)S(1)}, bf16[1024,128]{1,0:T(8,128)(2,1)}, u32[]{:S(2)}) copy-start(bf16[1024,128]{1,0:T(8,128)(2,1)} %param.9) | copy-start | bytes 786436
  14.9 196.8 %copy-start.3 = (f32[1024,512]{1,0:T(8,128)}, f32[1024,512]{1,0:T(8,128)S(1)}, u32[]{:S(2)}) copy-start(f32[1024,512]{1,0:T(8,128)S(1)} %copy.75) | copy-start | bytes 6291460
  57.5 154.2 %copy-start.65 = (f32[512]{0:T(512)}, f32[512]{0:T(512)S(1)}, u32[]{:S(2)}) copy-start(f32[512]{0:T(512)S(1)} %broadcast_multiply_fusion.7) | copy-start | bytes 6148
  98.2 113.5 %copy-start.90 = (f32[512]{0:T(512)}, f32[512]{0:T(512)S(1)}, u32[]{:S(2)}) copy-start(f32[512]{0:T(512)S(1)} %add_rsqrt_fusion.2) | copy-start | bytes 6148
  101.3 39.7 %copy-start.36 = (bf16[1024,64]{0,1:T(8,128)(2,1)}, bf16[1024,64]{0,1:T(8,128)(2,1)S(1)}, u32[]{:S(2)}) copy-start(bf16[1024,64]{0,1:T(8,128)(2,1)S(1)} %copy.147) | copy-start | bytes 393220
  145.7 12.4 %slice-start.7 = ((bf16[880640]{0:T(1024)(128)(2,1)}), bf16[2048]{0:T(1024)(128)(2,1)S(1)}, s32[]{:S(2)}) async-start(bf16[880640]{0:T(1024)(128)(2,1)} %reshape.1447), calls=%async_computation.10 | async-start | bytes 8192 | tf_op jit(solution)/shard_map/slice | solution.py:21
  272.9 14.0 %slice-start.4 = ((s8[6291456]{0:T(1024)(128)(4,1)}), s8[2097152]{0:T(1024)(128)(4,1)S(1)}, s32[]{:S(2)}) async-start(s8[6291456]{0:T(1024)(128)(4,1)} %bitcast.376), calls=%async_computation.7 | async-start | bytes 4194304
  289.9 8.2 %copy-start.95 = (bf16[1,1024,4]{1,2,0:T(4,128)(2,1)}, bf16[1,1024,4]{1,2,0:T(4,128)(2,1)S(1)}, u32[]{:S(2)}) copy-start(bf16[1,1024,4]{1,2,0:T(4,128)(2,1)S(1)} %get-tuple-element.109) | copy-start | bytes 24580
  289.9 8.2 %copy-start.97 = (bf16[1,1024,4]{1,2,0:T(4,128)(2,1)}, bf16[1,1024,4]{1,2,0:T(4,128)(2,1)S(1)}, u32[]{:S(2)}) copy-start(bf16[1,1024,4]{1,2,0:T(4,128)(2,1)S(1)} %get-tuple-element.110) | copy-start | bytes 24580
  291.3 13.8 %slice-start.2 = ((s8[6291456]{0:T(1024)(128)(4,1)}), s8[4194304]{0:T(1024)(128)(4,1)S(1)}, s32[]{:S(2)}) async-start(s8[6291456]{0:T(1024)(128)(4,1)} %bitcast.372), calls=%async_computation.5 | async-start | bytes 8388608
  339.0 7.9 %copy-start.4 = (f32[1024,512]{1,0:T(8,128)S(1)}, f32[1024,512]{1,0:T(8,128)}, u32[]{:S(2)}) copy-start(f32[1024,512]{1,0:T(8,128)} %copy-done.3) | copy-start | bytes 6291460
  339.0 7.9 %copy-start.7 = (bf16[1024,512]{1,0:T(8,128)(2,1)S(1)}, bf16[1024,512]{1,0:T(8,128)(2,1)}, u32[]{:S(2)}) copy-start(bf16[1024,512]{1,0:T(8,128)(2,1)} %param.5) | copy-start | bytes 3145732
  355.2 12.5 %copy-start.94 = (f32[6,256]{1,0:T(8,128)S(1)}, f32[6,256]{1,0:T(8,128)}, u32[]{:S(2)}) copy-start(f32[6,256]{1,0:T(8,128)} %get-tuple-element.36) | copy-start | bytes 18436
  355.2 13.1 %copy-start.25 = (f32[512,14]{1,0:T(8,128)S(1)}, f32[512,14]{1,0:T(8,128)}, u32[]{:S(2)}) copy-start(f32[512,14]{1,0:T(8,128)} %fusion.73) | copy-start | bytes 86020
  372.1 8.1 %copy-start.107 = (f32[3,2,256]{2,1,0:T(2,128)S(1)}, f32[3,2,256]{2,1,0:T(2,128)}, u32[]{:S(2)}) copy-start(f32[3,2,256]{2,1,0:T(2,128)} %get-tuple-element.18) | copy-start | bytes 18436
  372.1 8.7 %copy-start.92 = (f32[6,256]{1,0:T(8,128)S(1)}, f32[6,256]{1,0:T(8,128)}, u32[]{:S(2)}) copy-start(f32[6,256]{1,0:T(8,128)} %get-tuple-element.34) | copy-start | bytes 18436
  372.1 10.4 %copy-start.38 = (bf16[1024,64]{0,1:T(8,128)(2,1)S(1)}, bf16[1024,64]{0,1:T(8,128)(2,1)}, u32[]{:S(2)}) copy-start(bf16[1024,64]{0,1:T(8,128)(2,1)} %copy-done.36) | copy-start | bytes 393220
  384.0 22.4 %copy-start.104 = (f32[1536]{0:T(1024)S(1)}, f32[1536]{0:T(1024)}, u32[]{:S(2)}) copy-start(f32[1536]{0:T(1024)} %reshape.1420) | copy-start | bytes 18436
  384.1 23.7 %copy-start.102 = (f32[1536]{0:T(1024)S(1)}, f32[1536]{0:T(1024)}, u32[]{:S(2)}) copy-start(f32[1536]{0:T(1024)} %reshape.1421) | copy-start | bytes 18436
  384.1 25.0 %copy-start.103 = (f32[1536]{0:T(1024)S(1)}, f32[1536]{0:T(1024)}, u32[]{:S(2)}) copy-start(f32[1536]{0:T(1024)} %reshape.1422) | copy-start | bytes 18436
  384.1 26.3 %copy-start.47 = (f32[7168]{0:T(1024)S(1)}, f32[7168]{0:T(1024)}, u32[]{:S(2)}) copy-start(f32[7168]{0:T(1024)} %reshape.1423) | copy-start | bytes 86020
  411.0 20.1 %copy-start.99 = (f32[1536]{0:T(1024)S(1)}, f32[1536]{0:T(1024)}, u32[]{:S(2)}) copy-start(f32[1536]{0:T(1024)} %reshape.1427) | copy-start | bytes 18436
  411.0 21.4 %copy-start.100 = (f32[1536]{0:T(1024)S(1)}, f32[1536]{0:T(1024)}, u32[]{:S(2)}) copy-start(f32[1536]{0:T(1024)} %reshape.1428) | copy-start | bytes 18436
  411.0 22.7 %copy-start.105 = (f32[1536]{0:T(1024)S(1)}, f32[1536]{0:T(1024)}, u32[]{:S(2)}) copy-start(f32[1536]{0:T(1024)} %reshape.1429) | copy-start | bytes 18436
  411.0 24.6 %copy-start.46 = (f32[2,256,128]{2,1,0:T(8,128)S(1)}, f32[2,256,128]{2,1,0:T(8,128)}, u32[]{:S(2)}) copy-start(f32[2,256,128]{2,1,0:T(8,128)} %fusion.57) | copy-start | bytes 786436
  411.0 25.3 %copy-start.115 = (f32[2,128]{1,0:T(2,128)S(1)}, f32[2,128]{1,0:T(2,128)}, u32[]{:S(2)}) copy-start(f32[2,128]{1,0:T(2,128)} %get-tuple-element.150) | copy-start | bytes 3076
  411.0 28.1 %copy-start.117 = (f32[128]{0:T(128)S(1)}, f32[128]{0:T(128)}, u32[]{:S(2)}) copy-start(f32[128]{0:T(128)} %reshape.1434) | copy-start | bytes 1540
  444.4 47.1 %copy-start.89 = (f32[512]{0:T(512)S(1)}, f32[512]{0:T(512)}, u32[]{:S(2)}) copy-start(f32[512]{0:T(512)} %copy-done.88) | copy-start | bytes 6148
  444.4 47.1 %copy-start.91 = (f32[512]{0:T(512)S(1)}, f32[512]{0:T(512)}, u32[]{:S(2)}) copy-start(f32[512]{0:T(512)} %copy-done.90) | copy-start | bytes 6148
  (99 other events, 304.4 us)
Sparse Core Ops, SparseCore 0:
  11.4 63.0 all-gather.6
  78.0 62.9 all-gather.4
  444.5 180.6 all-reduce.8
where the time goes:
time: 643 us; the launch traced here: 635 us
  local copies, waits for them, and re-layouts  174 us (27%)
  other arithmetic  135 us (21%)
  waiting for transfers between devices  130 us (20%)
  blocking collectives  124 us (19%)
  matrix products  55.7 us (9%)
  between operations  15.7 us (2%)
    unnamed x4, waiting for transfers between devices  130 us
    unnamed x290, local copies, waits for them, and re-layouts  109 us
    psum x1, blocking collectives, per_device(): lax.psum(jnp.sum(masked, axis=0), ('wide', 'narrow')) / total_rows  42.2 us
    psum x1, blocking collectives, per_device(): lax.psum((jnp.sum(scaled, axis=0), jnp.sum(scaled * normed, axis=0)), ('w...  42 us
    psum x1, blocking collectives, per_device(): lax.psum(jnp.sum(jnp.square(masked - column_mean), axis=0), ('wide', 'nar...  40.2 us
    all_gather x1, other arithmetic, per_device(): lax.all_gather(second_params, ('wide', 'narrow'), axis=0, tiled=True)  38.9 us
    all_gather x1, other arithmetic, per_device(): lax.all_gather(first_params, ('wide', 'narrow'), axis=0, tiled=True)  38.1 us
  transfers between devices with their start and end apart: 3, of which 1 were waited for; matrix products, arithmetic and copies ran while one was open for 12% of the time, Pallas kernels for 0%

commit v1 on v0

v1 whole, which is shorter than its diff:
```python
import functools
import math

import jax
import jax.numpy as jnp
from jax import lax
from jax.experimental import pallas as pl
from jax.experimental.pallas import tpu as pltpu
from jax.sharding import PartitionSpec as P

H = 256
TOWER1 = 128
TOWER2 = 64
LANES = 128
EPSILON = 1e-05
AXES = ("wide", "narrow")
F32 = jnp.float32
BF16 = jnp.bfloat16
GROUPS_ONE = ((0, 4), (4, 8), (8, 14))
MEMBERS_ONE = ((0, 1, 4, 5), (2, 3, 4, 5), (0, 1, 2, 3, 4, 5))
GROUPS_TWO = ((0, 4), (4, 8))
MEMBERS_TWO = ((0, 1, 4, 5), (2, 3, 4, 5))
VMEM_LIMIT = 56 * 1024 * 1024


def up(value, step):
    return -(-value // step) * step


def mm(left, right):
    return jnp.dot(left, right, preferred_element_type=F32)


def mm_nt(left, right):
    return lax.dot_general(left, right, (((1,), (1,)), ((), ())), preferred_element_type=F32)


def mm_tn(left, right):
    return lax.dot_general(left, right, (((0,), (0,)), ((), ())), preferred_element_type=F32)


def sigmoid(values):
    return 0.5 * jnp.tanh(0.5 * values) + 0.5


def group_softmax(logits, groups):
    lane = lax.broadcasted_iota(jnp.int32, logits.shape, 1)
    spread = jnp.zeros_like(logits)
    for low, high in groups:
        inside = (lane >= low) & (lane < high)
        peak = jnp.max(jnp.where(inside, logits, -jnp.inf), axis=1, keepdims=True)
        spread = jnp.where(inside, logits - peak, spread)
    raw = jnp.exp(spread)
    result = jnp.zeros_like(logits)
    for low, high in groups:
        inside = (lane >= low) & (lane < high)
        total = jnp.sum(jnp.where(inside, raw, 0.0), axis=1, keepdims=True)
        result = jnp.where(inside, raw / total, result)
    return result


def group_softmax_back(probs, grads, groups):
    lane = lax.broadcasted_iota(jnp.int32, probs.shape, 1)
    product = probs * grads
    result = jnp.zeros_like(probs)
    for low, high in groups:
        inside = (lane >= low) & (lane < high)
        total = jnp.sum(jnp.where(inside, product, 0.0), axis=1, keepdims=True)
        result = jnp.where(inside, product - probs * total, result)
    return result


def into_lane(columns):
    rows = columns[0].shape[0]
    lane = lax.broadcasted_iota(jnp.int32, (rows, LANES), 1)
    result = jnp.zeros((rows, LANES), F32)
    for position, column in enumerate(columns):
        result = jnp.where(lane == position, column, result)
    return result


def mix_parts(weights, low, members, outputs):
    running = None
    for position, member in enumerate(members):
        term = weights[:, low + position : low + position + 1] * outputs[member]
        running = term if running is None else running + term
    return running


def row_sum(values):
    return jnp.sum(values, axis=1, keepdims=True)


def column_sum(values):
    return jnp.sum(values, axis=0, keepdims=True)


def norm_forward(post):
    centred = post - row_sum(post) * (1.0 / H)
    scale = lax.rsqrt(row_sum(centred * centred) * (1.0 / H) + EPSILON)
    return centred * scale, scale


def norm_backward(scaled, normal, scale):
    mean_one = row_sum(scaled) * (1.0 / H)
    mean_two = row_sum(scaled * normal) * (1.0 / H)
    return scale * (scaled - mean_one - normal * mean_two)


def first_layout(width):
    names = (
        ("in_gain", width),
        ("in_bias", width),
        ("expert_in", 6 * width * H),
        ("expert_in_bias", 6 * H),
        ("expert_out", 6 * H * H),
        ("expert_out_bias", 6 * H),
        ("norm_gain", 6 * H),
        ("norm_bias", 6 * H),
        ("gate", 14 * width),
    )
    return place_names(names)


def second_layout():
    names = (
        ("expert_in", 6 * H * H),
        ("expert_in_bias", 6 * H),
        ("expert_out", 6 * H * H),
        ("expert_out_bias", 6 * H),
        ("norm_gain", 6 * H),
        ("norm_bias", 6 * H),
        ("gate", 2 * H * 4),
        ("tower_in", 2 * H * TOWER1),
        ("tower_in_bias", 2 * TOWER1),
        ("tower_out", 2 * TOWER1 * TOWER2),
        ("tower_out_bias", 2 * TOWER2),
    )
    return place_names(names)


def place_names(names):
    rows = {}
    offset = 0
    for name, amount in names:
        rows[name] = offset // LANES
        offset += amount
    return rows, offset // LANES


def spread_pieces(me, count, rows, piece_refs, flat_ref):
    slot = 0
    for ref in piece_refs:
        for index in range(ref.shape[0]):
            owner = lax.bitwise_xor(me, jnp.int32(slot)) if count > 1 else 0
            flat_ref[pl.ds(owner * rows, rows), :] = ref[index, :rows, :].astype(F32)
            slot += 1


def wide_rows(flat_ref, row, amount):
    return jnp.concatenate(
        [flat_ref[pl.ds(row, amount, stride=2), :], flat_ref[pl.ds(row + 1, amount, stride=2), :]],
        axis=1,
    )


def put_wide_rows(flat_ref, row, amount, value):
    flat_ref[pl.ds(row, amount, stride=2), :] = value[:, :LANES]
    flat_ref[pl.ds(row + 1, amount, stride=2), :] = value[:, LANES:]


def collect_pieces(me, count, rows, flat_ref, out_ref):
    for slot in range(count):
        owner = lax.bitwise_xor(me, jnp.int32(slot)) if count > 1 else 0
        out_ref[slot, :rows, :] = flat_ref[pl.ds(owner * rows, rows), :].astype(BF16)


def gate_masks(width, columns, rows):
    period = columns // math.gcd(columns, LANES)
    item = lax.broadcasted_iota(jnp.int32, (width, LANES), 0)
    lane = lax.broadcasted_iota(jnp.int32, (width, LANES), 1)
    lane_a = lax.broadcasted_iota(jnp.int32, (LANES, LANES), 0)
    lane_b = lax.broadcasted_iota(jnp.int32, (LANES, LANES), 1)
    classes = []
    for kind in range(period):
        first = (item * columns) // LANES
        last = (item * columns + columns - 1) // LANES
        row = jnp.where(first % period == kind, first, last)
        match = (row % period == kind) & (row < rows) & ((row * LANES + lane) // columns == item)
        pattern = ((kind * LANES + lane_a) % columns == lane_b).astype(F32).astype(BF16)
        classes.append((row, match, pattern))
    return classes


def table_from_rows(flat, width, columns):
    rows = flat.shape[0]
    result = jnp.zeros((width, LANES), F32)
    index = lax.broadcasted_iota(jnp.int32, (width, rows), 1)
    for row, match, pattern in gate_masks(width, columns, rows):
        pick = (index == row[:, :1]).astype(F32).astype(BF16)
        chosen = mm(pick, flat)
        result = result + mm(jnp.where(match, chosen, 0.0).astype(BF16), pattern)
    return result


def rows_from_table(table, rows, columns):
    width = table.shape[0]
    result = jnp.zeros((rows, LANES), F32)
    index = lax.broadcasted_iota(jnp.int32, (width, rows), 1)
    for row, match, pattern in gate_masks(width, columns, rows):
        pick = (index == row[:, :1]).astype(F32).astype(BF16)
        moved = jnp.where(match, mm_nt(table, pattern), 0.0).astype(BF16)
        result = result + mm_tn(pick, moved)
    return result


def full_spec():
    return pl.BlockSpec(memory_space=pltpu.VMEM)


def tile_spec(shape, tile, dim):
    block = tuple(tile if index == dim else size for index, size in enumerate(shape))
    return pl.BlockSpec(
        block, lambda step: tuple(step if index == dim else 0 for index in range(len(shape)))
    )


def scalar_spec():
    return pl.BlockSpec(memory_space=pltpu.SMEM)


def run_kernel(kernel, grid, in_specs, out_specs, out_shape, scratch, args, flops, nbytes):
    return pl.pallas_call(
        kernel,
        grid=(grid,),
        in_specs=in_specs,
        out_specs=out_specs,
        out_shape=out_shape,
        scratch_shapes=scratch,
        compiler_params=pltpu.CompilerParams(
            dimension_semantics=("arbitrary",), vmem_limit_bytes=VMEM_LIMIT
        ),
        cost_estimate=pl.CostEstimate(flops=flops, bytes_accessed=nbytes, transcendentals=0),
    )(*args)


def spread_presence(presence, width):
    fields = presence.shape[1]
    field = lax.broadcasted_iota(jnp.int32, (fields, width), 0)
    column = lax.broadcasted_iota(jnp.int32, (fields, width), 1)
    pick = (column // (width // fields) == field).astype(F32).astype(BF16)
    return mm(presence.astype(F32).astype(BF16), pick)


def stats_kernel(features_ref, presence_ref, masked_ref, stats_ref):
    rows, width = features_ref.shape
    mask = spread_presence(presence_ref[...], width)
    masked = features_ref[...].astype(F32) * mask
    masked_ref[...] = masked.astype(BF16)
    mean = column_sum(masked) * (1.0 / rows)
    spread = masked - mean
    moment = column_sum(spread * spread)
    for index in range(width // LANES):
        part = slice(index * LANES, (index + 1) * LANES)
        stats_ref[index : index + 1, :] = mean[:, part]
        stats_ref[width // LANES + index : width // LANES + index + 1, :] = moment[:, part]


def from_lanes(block):
    return jnp.concatenate([block[index : index + 1, :] for index in range(block.shape[0])], axis=1)


def level_one_forward(
    count,
    rows,
    total_rows,
    n_pieces,
    me_ref,
    masked_ref,
    stats_ref,
    *rest,
):
    piece_refs = rest[:n_pieces]
    (
        level_ref,
        active_ref,
        slope_ref,
        normal_ref,
        scale_ref,
        probs_ref,
        mixed_ref,
        w_in_ref,
        w_out_ref,
        small_ref,
        gate_ref,
        entry_ref,
        flat_ref,
    ) = rest[n_pieces:]
    width = masked_ref.shape[1]
    where_row, _ = first_layout(width)

    @pl.when(pl.program_id(0) == 0)
    def _():
        spread_pieces(me_ref[0], count, rows, piece_refs, flat_ref)
        for e in range(6):
            w_in_ref[e] = wide_rows(flat_ref, where_row["expert_in"] + e * 2 * width, width).astype(
                BF16
            )
            w_out_ref[e] = wide_rows(flat_ref, where_row["expert_out"] + e * 2 * H, H).astype(BF16)
        for index, name in enumerate(
            ("expert_in_bias", "expert_out_bias", "norm_gain", "norm_bias")
        ):
            small_ref[index, :6, :] = wide_rows(flat_ref, where_row[name], 6)
        gate_flat = flat_ref[pl.ds(where_row["gate"], 14 * width // LANES), :].astype(BF16)
        gate_ref[...] = table_from_rows(gate_flat, width, 14).astype(BF16)
        lanes = width // LANES
        entry_ref[0:1, :] = from_lanes(stats_ref[0:lanes, :])
        variance = from_lanes(stats_ref[lanes : 2 * lanes, :]) * (1.0 / total_rows)
        entry_ref[1:2, :] = lax.rsqrt(variance + EPSILON)
        entry_ref[2:3, :] = from_lanes(flat_ref[0:lanes, :])
        entry_ref[3:4, :] = from_lanes(flat_ref[lanes : 2 * lanes, :])

    normed = (masked_ref[...].astype(F32) - entry_ref[0:1, :]) * entry_ref[1:2, :]
    level = (normed * entry_ref[2:3, :] + entry_ref[3:4, :]).astype(BF16)
    level_ref[...] = level
    probs = group_softmax(mm(level, gate_ref[...]), GROUPS_ONE)
    probs_ref[...] = probs
    outputs = []
    scales = []
    for e in range(6):
        pre = mm(level, w_in_ref[e]) + small_ref[0, e : e + 1, :]
        gate = sigmoid(pre)
        silu = pre * gate
        active = silu.astype(BF16)
        active_ref[e] = active
        slope_ref[e] = (gate + silu * (1.0 - gate)).astype(BF16)
        post = mm(active, w_out_ref[e]) + small_ref[1, e : e + 1, :]
        normal, scale = norm_forward(post)
        normal_ref[e] = normal.astype(BF16)
        scales.append(scale)
        outputs.append(normal * small_ref[2, e : e + 1, :] + small_ref[3, e : e + 1, :])
    scale_ref[...] = into_lane(scales)
    for index, (low, _) in enumerate(GROUPS_ONE):
        mixed_ref[index] = mix_parts(probs, low, MEMBERS_ONE[index], outputs).astype(BF16)


def level_two(count, rows, n_pieces, me_ref, mixed_ref, cotangent_ref, *rest):
    piece_refs = rest[:n_pieces]
    (
        towers_ref,
        mixed_grad_ref,
        grads_ref,
        flat_ref,
        w_in_ref,
        w_out_ref,
        small_ref,
        gate_ref,
        tower_in_ref,
        tower_out_ref,
        tower_tmp_ref,
        tower_small_ref,
        g_in_ref,
        g_out_ref,
        g_small_ref,
        g_gate_ref,
        g_tower_in_ref,
        g_tower_out_ref,
        g_tower_small_ref,
    ) = rest[n_pieces:]
    where_row, used_rows = second_layout()
    lane_h = lax.broadcasted_iota(jnp.int32, (H, LANES), 1)

    @pl.when(pl.program_id(0) == 0)
    def _():
        spread_pieces(me_ref[0], count, rows, piece_refs, flat_ref)
        for e in range(6):
            w_in_ref[e] = wide_rows(flat_ref, where_row["expert_in"] + e * 2 * H, H).astype(BF16)
            w_out_ref[e] = wide_rows(flat_ref, where_row["expert_out"] + e * 2 * H, H).astype(BF16)
        for index, name in enumerate(
            ("expert_in_bias", "expert_out_bias", "norm_gain", "norm_bias")
        ):
            small_ref[index, :6, :] = wide_rows(flat_ref, where_row[name], 6)
        gate_rows = H * 4 // LANES
        shift_a = lax.broadcasted_iota(jnp.int32, (LANES, LANES), 0)
        shift_b = lax.broadcasted_iota(jnp.int32, (LANES, LANES), 1)
        shift = ((shift_a + 4 == shift_b) & (shift_a < 4)).astype(F32).astype(BF16)
        tables = []
        for task in range(2):
            piece = flat_ref[pl.ds(where_row["gate"] + task * gate_rows, gate_rows), :].astype(BF16)
            tables.append(table_from_rows(piece, H, 4).astype(BF16))
        gate_ref[...] = (tables[0].astype(F32) + mm(tables[1], shift)).astype(BF16)
        zero = jnp.zeros((TOWER1, TOWER2), F32)
        for task in range(2):
            tower_in_ref[task] = flat_ref[pl.ds(where_row["tower_in"] + task * H, H), :].astype(
                BF16
            )
            packed = flat_ref[
                pl.ds(where_row["tower_out"] + task * TOWER1 // 2, TOWER1 // 2), :
            ]
            spot = task * TOWER1
            for half in range(2):
                part = packed[:, half * TOWER2 : (half + 1) * TOWER2]
                pair = [part, zero[: TOWER1 // 2]]
                if task == 1:
                    pair.reverse()
                tower_tmp_ref[pl.ds(spot + half, TOWER1 // 2, stride=2), :] = jnp.concatenate(
                    pair, axis=1
                )
        tower_out_ref[...] = tower_tmp_ref[...].astype(BF16)
        tower_small_ref[0:1, :] = from_lanes(flat_ref[pl.ds(where_row["tower_in_bias"], 2), :])
        tower_small_ref[1:2, :LANES] = flat_ref[pl.ds(where_row["tower_out_bias"], 1), :]
        for ref in (
            g_in_ref,
            g_out_ref,
            g_small_ref,
            g_gate_ref,
            g_tower_in_ref,
            g_tower_out_ref,
            g_tower_small_ref,
        ):
            ref[...] = jnp.zeros(ref.shape, F32)

    inputs = [mixed_ref[index] for index in range(3)]
    tile = inputs[0].shape[0]
    lane = lax.broadcasted_iota(jnp.int32, (tile, LANES), 1)
    actives, slopes, normals, scales, outputs = [], [], [], [], []
    for e in range(6):
        pre = mm(inputs[e // 2], w_in_ref[e]) + small_ref[0, e : e + 1, :]
        gate = sigmoid(pre)
        silu = pre * gate
        active = silu.astype(BF16)
        post = mm(active, w_out_ref[e]) + small_ref[1, e : e + 1, :]
        normal, scale = norm_forward(post)
        actives.append(active)
        slopes.append((gate + silu * (1.0 - gate)).astype(BF16))
        normals.append(normal)
        scales.append(scale)
        outputs.append(normal * small_ref[2, e : e + 1, :] + small_ref[3, e : e + 1, :])
    logits = jnp.where(lane < 4, mm(inputs[0], gate_ref[...]), mm(inputs[1], gate_ref[...]))
    probs = group_softmax(logits, GROUPS_TWO)
    combined = [
        mix_parts(probs, 4 * task, MEMBERS_TWO[task], outputs).astype(BF16) for task in range(2)
    ]
    tower_pre = (
        jnp.concatenate([mm(combined[task], tower_in_ref[task]) for task in range(2)], axis=1)
        + tower_small_ref[0:1, :]
    )
    tower_gate = sigmoid(tower_pre)
    tower_silu = tower_pre * tower_gate
    tower_active = tower_silu.astype(BF16)
    towers_ref[...] = mm(tower_active, tower_out_ref[...]) + tower_small_ref[1:2, :LANES]

    cotangent = cotangent_ref[...]
    g_tower_out_ref[...] += mm_tn(tower_active, cotangent)
    g_tower_small_ref[1:2, :LANES] += column_sum(cotangent.astype(F32))
    tower_slope = tower_gate + tower_silu * (1.0 - tower_gate)
    tower_grad = (mm_nt(cotangent, tower_out_ref[...]) * tower_slope).astype(BF16)
    g_tower_small_ref[0:1, :] += column_sum(tower_grad.astype(F32))
    combined_grads = []
    for task in range(2):
        part = tower_grad[:, task * TOWER1 : (task + 1) * TOWER1]
        g_tower_in_ref[task] += mm_tn(combined[task], part)
        combined_grads.append(mm_nt(part, tower_in_ref[task]))
    prob_grads = into_lane(
        [
            row_sum(combined_grads[task] * outputs[member])
            for task in range(2)
            for member in MEMBERS_TWO[task]
        ]
    )
    logit_grad = group_softmax_back(probs, prob_grads, GROUPS_TWO)
    logit_parts = [
        jnp.where(lane < 4, logit_grad, 0.0).astype(BF16),
        jnp.where((lane >= 4) & (lane < 8), logit_grad, 0.0).astype(BF16),
    ]
    g_gate_ref[...] += mm_tn(inputs[0], logit_parts[0]) + mm_tn(inputs[1], logit_parts[1])
    input_grads = [mm_nt(logit_parts[task], gate_ref[...]) for task in range(2)] + [None]
    for e in range(6):
        out_grad = None
        for task in range(2):
            if e in MEMBERS_TWO[task]:
                column = 4 * task + MEMBERS_TWO[task].index(e)
                term = probs[:, column : column + 1] * combined_grads[task]
                out_grad = term if out_grad is None else out_grad + term
        g_small_ref[2, e : e + 1, :] += column_sum(out_grad * normals[e])
        g_small_ref[3, e : e + 1, :] += column_sum(out_grad)
        post_grad = norm_backward(out_grad * small_ref[2, e : e + 1, :], normals[e], scales[e])
        post_grad = post_grad.astype(BF16)
        g_out_ref[e] += mm_tn(actives[e], post_grad)
        g_small_ref[1, e : e + 1, :] += column_sum(post_grad.astype(F32))
        pre_grad = (mm_nt(post_grad, w_out_ref[e]) * slopes[e].astype(F32)).astype(BF16)
        g_in_ref[e] += mm_tn(inputs[e // 2], pre_grad)
        g_small_ref[0, e : e + 1, :] += column_sum(pre_grad.astype(F32))
        term = mm_nt(pre_grad, w_in_ref[e])
        input_grads[e // 2] = term if input_grads[e // 2] is None else input_grads[e // 2] + term
    for index in range(3):
        mixed_grad_ref[index] = input_grads[index]

    @pl.when(pl.program_id(0) == pl.num_programs(0) - 1)
    def _():
        for e in range(6):
            put_wide_rows(flat_ref, where_row["expert_in"] + e * 2 * H, H, g_in_ref[e])
            put_wide_rows(flat_ref, where_row["expert_out"] + e * 2 * H, H, g_out_ref[e])
        for index, name in enumerate(
            ("expert_in_bias", "expert_out_bias", "norm_gain", "norm_bias")
        ):
            put_wide_rows(flat_ref, where_row[name], 6, g_small_ref[index, :6, :])
        gate_rows = H * 4 // LANES
        shift_a = lax.broadcasted_iota(jnp.int32, (LANES, LANES), 0)
        shift_b = lax.broadcasted_iota(jnp.int32, (LANES, LANES), 1)
        shift = ((shift_a == shift_b + 4) & (shift_b < 4)).astype(F32).astype(BF16)
        table = jnp.where(lane_h < 8, g_gate_ref[...], 0.0).astype(BF16)
        tables = [
            jnp.where(lane_h < 4, table.astype(F32), 0.0).astype(BF16),
            mm(table, shift).astype(BF16),
        ]
        for task in range(2):
            flat_ref[pl.ds(where_row["gate"] + task * gate_rows, gate_rows), :] = rows_from_table(
                tables[task], gate_rows, 4
            )
            flat_ref[pl.ds(where_row["tower_in"] + task * H, H), :] = g_tower_in_ref[task]
            spot = task * TOWER1
            flat_ref[pl.ds(where_row["tower_out"] + task * TOWER1 // 2, TOWER1 // 2), :] = (
                jnp.concatenate(
                    [
                        g_tower_out_ref[pl.ds(spot + half, TOWER1 // 2, stride=2), :][
                            :, task * TOWER2 : (task + 1) * TOWER2
                        ]
                        for half in range(2)
                    ],
                    axis=1,
                )
            )
            flat_ref[pl.ds(where_row["tower_in_bias"] + task, 1), :] = g_tower_small_ref[
                0:1, task * TOWER1 : (task + 1) * TOWER1
            ]
        flat_ref[pl.ds(where_row["tower_out_bias"], 1), :] = g_tower_small_ref[1:2, :LANES]
        if used_rows < count * rows:
            flat_ref[pl.ds(used_rows, count * rows - used_rows), :] = jnp.zeros(
                (count * rows - used_rows, LANES), F32
            )
        collect_pieces(me_ref[0], count, rows, flat_ref, grads_ref)


def level_one_backward(
    count,
    rows,
    me_ref,
    mixed_grad_ref,
    masked_ref,
    level_ref,
    active_ref,
    slope_ref,
    normal_ref,
    scale_ref,
    probs_ref,
    w_in_ref,
    w_out_ref,
    small_ref,
    gate_ref,
    entry_ref,
    level_grad_ref,
    sums_ref,
    grads_ref,
    flat_ref,
    g_in_ref,
    g_out_ref,
    g_small_ref,
    g_gate_ref,
    g_sum_ref,
):
    width = masked_ref.shape[1]
    lanes = width // LANES
    where_row, used_rows = first_layout(width)

    @pl.when(pl.program_id(0) == 0)
    def _():
        for ref in (g_in_ref, g_out_ref, g_small_ref, g_gate_ref, g_sum_ref):
            ref[...] = jnp.zeros(ref.shape, F32)

    level = level_ref[...]
    probs = probs_ref[...]
    mixed_grads = [mixed_grad_ref[index] for index in range(3)]
    columns = [None] * 14
    for e in range(6):
        output = normal_ref[e].astype(F32) * small_ref[2, e : e + 1, :] + small_ref[3, e : e + 1, :]
        for index, (low, _) in enumerate(GROUPS_ONE):
            if e in MEMBERS_ONE[index]:
                columns[low + MEMBERS_ONE[index].index(e)] = row_sum(mixed_grads[index] * output)
    logit_grad = group_softmax_back(probs, into_lane(columns), GROUPS_ONE).astype(BF16)
    g_gate_ref[...] += mm_tn(level, logit_grad)
    level_grad = mm_nt(logit_grad, gate_ref[...])
    for e in range(6):
        normal = normal_ref[e].astype(F32)
        out_grad = None
        for index, (low, _) in enumerate(GROUPS_ONE):
            if e in MEMBERS_ONE[index]:
                column = low + MEMBERS_ONE[index].index(e)
                term = probs[:, column : column + 1] * mixed_grads[index]
                out_grad = term if out_grad is None else out_grad + term
        g_small_ref[2, e : e + 1, :] += column_sum(out_grad * normal)
        g_small_ref[3, e : e + 1, :] += column_sum(out_grad)
        post_grad = norm_backward(
            out_grad * small_ref[2, e : e + 1, :], normal, scale_ref[:, e : e + 1]
        ).astype(BF16)
        g_out_ref[e] += mm_tn(active_ref[e], post_grad)
        g_small_ref[1, e : e + 1, :] += column_sum(post_grad.astype(F32))
        pre_grad = (mm_nt(post_grad, w_out_ref[e]) * slope_ref[e].astype(F32)).astype(BF16)
        g_in_ref[e] += mm_tn(level, pre_grad)
        g_small_ref[0, e : e + 1, :] += column_sum(pre_grad.astype(F32))
        level_grad = level_grad + mm_nt(pre_grad, w_in_ref[e])
    level_grad_ref[...] = level_grad
    normed = (masked_ref[...].astype(F32) - entry_ref[0:1, :]) * entry_ref[1:2, :]
    g_sum_ref[0:1, :] += column_sum(level_grad * normed)
    g_sum_ref[1:2, :] += column_sum(level_grad)

    @pl.when(pl.program_id(0) == pl.num_programs(0) - 1)
    def _():
        for e in range(6):
            put_wide_rows(flat_ref, where_row["expert_in"] + e * 2 * width, width, g_in_ref[e])
            put_wide_rows(flat_ref, where_row["expert_out"] + e * 2 * H, H, g_out_ref[e])
        for index, name in enumerate(
            ("expert_in_bias", "expert_out_bias", "norm_gain", "norm_bias")
        ):
            put_wide_rows(flat_ref, where_row[name], 6, g_small_ref[index, :6, :])
        gate_rows = 14 * width // LANES
        flat_ref[pl.ds(where_row["gate"], gate_rows), :] = rows_from_table(
            g_gate_ref[...].astype(BF16), gate_rows, 14
        )
        for index in range(lanes):
            part = slice(index * LANES, (index + 1) * LANES)
            sums_ref[index : index + 1, :] = g_sum_ref[0:1, part]
            sums_ref[lanes + index : lanes + index + 1, :] = g_sum_ref[1:2, part]
        flat_ref[0 : 2 * lanes, :] = jnp.zeros((2 * lanes, LANES), F32)
        if used_rows < count * rows:
            flat_ref[pl.ds(used_rows, count * rows - used_rows), :] = jnp.zeros(
                (count * rows - used_rows, LANES), F32
            )
        collect_pieces(me_ref[0], count, rows, flat_ref, grads_ref)


def input_kernel(total_rows, level_grad_ref, masked_ref, presence_ref, entry_ref, sums_ref, out_ref):
    width = masked_ref.shape[1]
    lanes = width // LANES
    mask = spread_presence(presence_ref[...], width)
    inv_scale = entry_ref[1:2, :]
    gain = entry_ref[2:3, :]
    normed = (masked_ref[...].astype(F32) - entry_ref[0:1, :]) * inv_scale
    cross = from_lanes(sums_ref[0:lanes, :]) * (1.0 / total_rows)
    plain = from_lanes(sums_ref[lanes : 2 * lanes, :]) * (1.0 / total_rows)
    out_ref[...] = mask * ((inv_scale * gain) * (level_grad_ref[...] - plain - normed * cross))


def xor_permute(value, axis, bit):
    size = lax.axis_size(axis)
    return lax.ppermute(value, axis, [(index, index ^ bit) for index in range(size)])


def is_power(value):
    return value & (value - 1) == 0


def butterfly(value, merge):
    for axis in AXES:
        bit = 1
        while bit < lax.axis_size(axis):
            value = merge(value, xor_permute(value, axis, bit), axis, bit)
            bit *= 2
    return value


def hypercube_ok():
    wide, narrow = lax.axis_size("wide"), lax.axis_size("narrow")
    return wide == 8 and narrow == 4


def gather_pieces(local, rows):
    padded = up(rows, 16)
    block = jnp.pad(local.reshape(rows, LANES), ((0, padded - rows), (0, 0)))
    near = [block] + [xor_permute(block, "narrow", k) for k in (1, 2, 3)]
    first, second = jnp.stack(near[:2]), jnp.stack(near[2:])
    first_y, second_x = xor_permute(first, "wide", 4), xor_permute(second, "wide", 2)
    first_x, second_y = xor_permute(first, "wide", 2), xor_permute(second, "wide", 4)
    first_xy, second_xy = xor_permute(first_y, "wide", 2), xor_permute(second_x, "wide", 4)
    own = [first, second, first_x, second_x, first_y, second_y, first_xy, second_xy]
    other = [xor_permute(piece, "wide", 1) for piece in own]
    pieces = []
    for index in range(4):
        pieces += [own[2 * index], own[2 * index + 1], other[2 * index], other[2 * index + 1]]
    return pieces


def scatter_pieces(value):
    split = value.reshape(2, 2, 2, 4, value.shape[1], LANES)
    keep = split[:, :, 0].astype(F32) + xor_permute(split[:, :, 1], "wide", 1).astype(F32)
    low = keep.astype(BF16)
    first = keep[0, :, :2] + xor_permute(low[1, :, :2], "wide", 4).astype(F32)
    second = keep[:, 0, 2:] + xor_permute(low[:, 1, 2:], "wide", 2).astype(F32)
    first = first[0] + xor_permute(first[1].astype(BF16), "wide", 2).astype(F32)
    second = second[0] + xor_permute(second[1].astype(BF16), "wide", 4).astype(F32)
    total = first[0]
    total = total + xor_permute(first[1].astype(BF16), "narrow", 1).astype(F32)
    total = total + xor_permute(second[0].astype(BF16), "narrow", 2).astype(F32)
    total = total + xor_permute(second[1].astype(BF16), "narrow", 3).astype(F32)
    return total


def gather_flat(local):
    whole = lax.all_gather(local, AXES, axis=0, tiled=True)
    return whole.reshape(1, whole.shape[0] // LANES, LANES)


def per_device(features, presence, first_params, second_params, cotangent):
    rows, width = features.shape
    lanes = width // LANES
    devices_all = lax.axis_size(AXES)
    total_rows = rows * devices_all
    cube = hypercube_ok()
    tile = math.gcd(rows, 256)
    steps = rows // tile
    me = lax.axis_index(AXES).astype(jnp.int32).reshape(1)
    flat_rows = [first_params.shape[0] // LANES, second_params.shape[0] // LANES]
    if cube:
        count, chunks = devices_all, flat_rows
        pieces_one = gather_pieces(first_params, flat_rows[0])
        pieces_two = gather_pieces(second_params, flat_rows[1])
    else:
        count, chunks = 1, [flat_rows[0] * devices_all, flat_rows[1] * devices_all]
        pieces_one, pieces_two = [gather_flat(first_params)], [gather_flat(second_params)]

    masked, stats = pl.pallas_call(
        stats_kernel,
        out_shape=(
            jax.ShapeDtypeStruct((rows, width), BF16),
            jax.ShapeDtypeStruct((2 * lanes, LANES), F32),
        ),
        compiler_params=pltpu.CompilerParams(vmem_limit_bytes=VMEM_LIMIT),
    )(features, presence)

    members = [rows]

    def merge(mine, theirs, axis, bit):
        delta = mine[:lanes] - theirs[:lanes]
        mean = 0.5 * (mine[:lanes] + theirs[:lanes])
        moment = mine[lanes:] + theirs[lanes:] + delta * delta * (0.5 * members[0])
        members[0] *= 2
        return jnp.concatenate([mean, moment])

    stats = butterfly(stats, merge)

    shape = jax.ShapeDtypeStruct
    saved = run_kernel(
        functools.partial(
            level_one_forward, count, chunks[0], float(total_rows), len(pieces_one)
        ),
        steps,
        [scalar_spec(), tile_spec((rows, width), tile, 0), full_spec()]
        + [full_spec()] * len(pieces_one),
        [
            tile_spec((rows, width), tile, 0),
            tile_spec((6, rows, H), tile, 1),
            tile_spec((6, rows, H), tile, 1),
            tile_spec((6, rows, H), tile, 1),
            tile_spec((rows, LANES), tile, 0),
            tile_spec((rows, LANES), tile, 0),
            tile_spec((3, rows, H), tile, 1),
            full_spec(),
            full_spec(),
            full_spec(),
            full_spec(),
            full_spec(),
        ],
        [
            shape((rows, width), BF16),
            shape((6, rows, H), BF16),
            shape((6, rows, H), BF16),
            shape((6, rows, H), BF16),
            shape((rows, LANES), F32),
            shape((rows, LANES), F32),
            shape((3, rows, H), BF16),
            shape((6, width, H), BF16),
            shape((6, H, H), BF16),
            shape((4, 8, H), F32),
            shape((width, LANES), BF16),
            shape((8, width), F32),
        ],
        [pltpu.VMEM((count * chunks[0], LANES), F32)],
        [me, masked, stats] + pieces_one,
        rows * 6 * (width + H) * H * 2,
        16 * 2**20,
    )
    level, active, slope, normal, scale, probs, mixed, w_in, w_out, small, gate, entry = saved

    towers, mixed_grad, grads_two = run_kernel(
        functools.partial(level_two, count, chunks[1], len(pieces_two)),
        steps,
        [scalar_spec(), tile_spec((3, rows, H), tile, 1), tile_spec((rows, LANES), tile, 0)]
        + [full_spec()] * len(pieces_two),
        [
            tile_spec((rows, LANES), tile, 0),
            tile_spec((3, rows, H), tile, 1),
            full_spec(),
        ],
        [
            shape((rows, LANES), F32),
            shape((3, rows, H), F32),
            shape((count, up(chunks[1], 16), LANES), BF16),
        ],
        [
            pltpu.VMEM((count * chunks[1], LANES), F32),
            pltpu.VMEM((6, H, H), BF16),
            pltpu.VMEM((6, H, H), BF16),
            pltpu.VMEM((4, 8, H), F32),
            pltpu.VMEM((H, LANES), BF16),
            pltpu.VMEM((2, H, TOWER1), BF16),
            pltpu.VMEM((2 * TOWER1, LANES), BF16),
            pltpu.VMEM((2 * TOWER1, LANES), F32),
            pltpu.VMEM((8, 2 * TOWER1), F32),
            pltpu.VMEM((6, H, H), F32),
            pltpu.VMEM((6, H, H), F32),
            pltpu.VMEM((4, 8, H), F32),
            pltpu.VMEM((H, LANES), F32),
            pltpu.VMEM((2, H, TOWER1), F32),
            pltpu.VMEM((2 * TOWER1, LANES), F32),
            pltpu.VMEM((8, 2 * TOWER1), F32),
        ],
        [me, mixed, cotangent] + pieces_two,
        rows * 6 * 2 * H * H * 2 * 3,
        8 * 2**20,
    )
    if cube:
        second_grad = scatter_pieces(grads_two)[: flat_rows[1]].reshape(-1)
    else:
        second_grad = lax.psum_scatter(
            grads_two.reshape(-1)[: flat_rows[1] * devices_all * LANES].astype(F32),
            AXES,
            scatter_dimension=0,
            tiled=True,
        )

    level_grad, sums, grads_one = run_kernel(
        functools.partial(level_one_backward, count, chunks[0]),
        steps,
        [
            scalar_spec(),
            tile_spec((3, rows, H), tile, 1),
            tile_spec((rows, width), tile, 0),
            tile_spec((rows, width), tile, 0),
            tile_spec((6, rows, H), tile, 1),
            tile_spec((6, rows, H), tile, 1),
            tile_spec((6, rows, H), tile, 1),
            tile_spec((rows, LANES), tile, 0),
            tile_spec((rows, LANES), tile, 0),
        ]
        + [full_spec()] * 5,
        [tile_spec((rows, width), tile, 0), full_spec(), full_spec()],
        [
            shape((rows, width), F32),
            shape((2 * lanes, LANES), F32),
            shape((count, up(chunks[0], 16), LANES), BF16),
        ],
        [
            pltpu.VMEM((count * chunks[0], LANES), F32),
            pltpu.VMEM((6, width, H), F32),
            pltpu.VMEM((6, H, H), F32),
            pltpu.VMEM((4, 8, H), F32),
            pltpu.VMEM((width, LANES), F32),
            pltpu.VMEM((8, width), F32),
        ],
        [
            me,
            mixed_grad,
            masked,
            level,
            active,
            slope,
            normal,
            scale,
            probs,
            w_in,
            w_out,
            small,
            gate,
            entry,
        ],
        rows * 6 * (width + H) * H * 2 * 2,
        20 * 2**20,
    )
    sums = butterfly(sums, lambda mine, theirs, axis, bit: mine + theirs)
    if cube:
        first_grad = scatter_pieces(grads_one)[: flat_rows[0]].reshape(-1)
    else:
        first_grad = lax.psum_scatter(
            grads_one.reshape(-1)[: flat_rows[0] * devices_all * LANES].astype(F32),
            AXES,
            scatter_dimension=0,
            tiled=True,
        )
    start = me[0] * first_params.shape[0]
    position = start + jnp.arange(2 * width)
    head = jnp.where(position < 2 * width, sums.reshape(-1), first_grad[: 2 * width])
    first_grad = jnp.concatenate([head, first_grad[2 * width :]])

    input_grad = run_kernel(
        functools.partial(input_kernel, float(total_rows)),
        steps,
        [
            tile_spec((rows, width), tile, 0),
            tile_spec((rows, width), tile, 0),
            tile_spec((rows, presence.shape[1]), tile, 0),
            full_spec(),
            full_spec(),
        ],
        tile_spec((rows, width), tile, 0),
        shape((rows, width), F32),
        [],
        [level_grad, masked, presence, entry, sums],
        rows * width * 10,
        6 * 2**20,
    )
    return (towers, input_grad, first_grad, second_grad)


def solution(mesh):
    placed = (
        P(AXES, None),
        P(AXES, None),
        P(AXES),
        P(AXES),
        P(AXES, None),
    )
    return jax.shard_map(
        per_device,
        mesh=mesh,
        in_specs=placed,
        out_specs=(P(AXES, None), P(AXES, None), P(AXES), P(AXES)),
        check_vma=False,
    )
```

time: 643 us -> 196 us (0.30); the launches traced: 635 us -> 196 us
  local copies, waits for them, and re-layouts: 174 us -> 8.48 us
  other arithmetic: 135 us -> 4.45 us
  blocking collectives: 124 us -> 0 us
  waiting for transfers between devices: 130 us -> 46.1 us
  Pallas kernels: 0 us -> 81.9 us
  matrix products: 55.7 us -> 0 us
  starting transfers between devices: 0.12 us -> 53.7 us
  between operations: 15.7 us -> 1.31 us
    unnamed x4 -> x0, waiting for transfers between devices: 130 us -> none
    psum x3 -> x0, blocking collectives: 124 us -> none  [the longest x1 42.2 us: per_device(): lax.psum(jnp.sum(masked, axis=0), ('wide', 'narrow')) / total_rows]
    unnamed x290 -> x75, local copies, waits for them, and re-layouts: 109 us -> 3.05 us
    pallas_call x0 -> x5, Pallas kernels: none -> 81.9 us  [the longest x4 79 us: run_kernel(): pl.pallas_call(kernel, grid=(grid,), in_specs=in_specs, out_specs=out_spe...]
    all_gather x2 -> x0, other arithmetic: 77 us -> none  [the longest x1 38.9 us: per_device(): lax.all_gather(second_params, ('wide', 'narrow'), axis=0, tiled=True)]
    ppermute x0 -> x60, starting transfers between devices: none -> 53.7 us  [xor_permute(): lax.ppermute(value, axis, [(index, index ^ bit) for index in range(size)])]
    dot_general x23 -> x0, matrix products: 53 us -> none  [the longest x2 9.78 us: expert_backward(): jnp.einsum('gerk,gehk->gerh', post_low, weight_out, preferred_element_typ...]
    ppermute x0 -> x60, waiting for transfers between devices: none -> 46.1 us  [xor_permute(): lax.ppermute(value, axis, [(index, index ^ bit) for index in range(size)])]
  transfers between devices with their start and end apart: 3 -> 60, of which waited for: 1 -> 26; matrix products, arithmetic and copies ran while one was open for 12% -> 3% of each run, Pallas kernels for 0% -> 25%
where the time goes in v1:
time: 196 us
  Pallas kernels  81.9 us (42%)
  starting transfers between devices  53.7 us (27%)
  waiting for transfers between devices  46.1 us (24%)
  local copies, waits for them, and re-layouts  8.48 us (4%)
  other arithmetic  4.45 us (2%)
    pallas_call x4, Pallas kernels, run_kernel(): pl.pallas_call(kernel, grid=(grid,), in_specs=in_specs, out_specs=out_spe...  79 us
    ppermute x60, starting transfers between devices, xor_permute(): lax.ppermute(value, axis, [(index, index ^ bit) for index in range(size)])  53.7 us
    ppermute x60, waiting for transfers between devices, xor_permute(): lax.ppermute(value, axis, [(index, index ^ bit) for index in range(size)])  46.1 us
  transfers between devices with their start and end apart: 60, of which 26 were waited for; matrix products, arithmetic and copies ran while one was open for 3% of the time, Pallas kernels for 25%

profile of v1, /device:TPU:0, one launch (start us, length us, event | category | flops | bytes accessed | tf_op | source)
XLA Modules:
  0.0 195.9 jit_solution(14924792088596441028)
XLA Ops:
  0.7 1.8 copy.9.presence_ref
  2.4 2.8 %shard_map.84 = (bf16[1024,512]{1,0:T(8,128)(2,1)}, f32[8,128]{1,0:T(8,128)}) custom-call(bf16[1024,512]{1,0:T(8,128)(2,1)} %features_ref.1, s32[1024,8]{1,0:T(8,128)} %copy.9.presence_ref), custom_call_target="tpu_custom_call" | custom-call | tf_op jit(solution)/shard_map/pallas_call | solution.py:731
  7.5 2.9 %collective-permute-start.1 = (f32[8,128]{1,0:T(8,128)S(1)}, f32[8,128]{1,0:T(8,128)S(1)}, u32[]{:S(2)}, u32[]{:S(2)}) collective-permute-start(f32[8,128]{1,0:T(8,128)S(1)} %pad_maximum_fusion.5), channel_id=1, source_target_pairs={{0,8},{4,12},{8,0},{12,4},{16,24},{20,28},{24,16},{28,20},{1,9},{5... | collective-permute-start | bytes 12296 | tf_op jit(solution)/shard_map/ppermute | solution.py:656
  10.4 1.6 collective-permute-done.1
  12.0 2.1 %collective-permute-start.2 = (f32[8,128]{1,0:T(8,128)S(1)}, f32[8,128]{1,0:T(8,128)S(1)}, u32[]{:S(2)}, u32[]{:S(2)}) collective-permute-start(f32[8,128]{1,0:T(8,128)S(1)} %pad_maximum_fusion.6), channel_id=1, source_target_pairs={{0,16},{4,20},{8,24},{12,28},{16,0},{20,4},{24,8},{28,12},{1,17},{... | collective-permute-start | bytes 12296 | tf_op jit(solution)/shard_map/ppermute | solution.py:656
  14.2 2.7 %collective-permute-start.6 = (bf16[304,128]{1,0:T(8,128)(2,1)S(1)}, bf16[304,128]{1,0:T(8,128)(2,1)S(1)}, u32[]{:S(2)}, u32[]{:S(2)}) collective-permute-start(bf16[304,128]{1,0:T(8,128)(2,1)S(1)} %get-tuple-element.59), channel_id=1, source_target_pairs={{0,2},{1,3},{2,0},{3,1},{4,6},{5,7},{6,4},{7,5},{8,10},{9,11},{10,... | collective-permute-start | bytes 233480 | tf_op jit(solution)/shard_map/ppermute | solution.py:656
  18.4 1.9 collective-permute-start.3
  20.3 2.5 %collective-permute-start.24 = (bf16[224,128]{1,0:T(8,128)(2,1)S(1)}, bf16[224,128]{1,0:T(8,128)(2,1)S(1)}, u32[]{:S(2)}, u32[]{:S(2)}) collective-permute-start(bf16[224,128]{1,0:T(8,128)(2,1)S(1)} %get-tuple-element.61), channel_id=1, source_target_pairs={{0,3},{1,2},{2,1},{3,0},{4,7},{5,6},{6,5},{7,4},{8,11},{9,10},{10,... | collective-permute-start | bytes 172040 | tf_op jit(solution)/shard_map/ppermute | solution.py:656
  26.3 1.6 collective-permute-start.22
  29.3 1.6 collective-permute-start.4
  30.9 1.5 collective-permute-start.28
  35.8 2.8 %collective-permute-done.31.rest_8_ = bf16[2,224,128]{2,1,0:T(8,128)(2,1)S(1)} collective-permute-done((bf16[2,224,128]{2,1,0:T(8,128)(2,1)S(1)}, bf16[2,224,128]{2,1,0:T(8,128)(2,1)S(1)}, u32[]{:S(2)}, u32[]{:S(2)}) %collective-permute-start.31) | collective-permute-done | bytes 114720 | tf_op jit(solution)/shard_map/ppermute | solution.py:656
  41.3 1.5 collective-permute-start.10
  49.2 1.8 collective-permute-done.36.rest_13_
  51.8 4.5 %collective-permute-done.35.rest_12_ = bf16[2,224,128]{2,1,0:T(8,128)(2,1)S(1)} collective-permute-done((bf16[2,224,128]{2,1,0:T(8,128)(2,1)S(1)}, bf16[2,224,128]{2,1,0:T(8,128)(2,1)S(1)}, u32[]{:S(2)}, u32[]{:S(2)}) %collective-permute-start.35) | collective-permute-done | bytes 114720 | tf_op jit(solution)/shard_map/ppermute | solution.py:656
  59.7 23.2 %shard_map.85 = (bf16[1024,512]{1,0:T(8,128)(2,1)}, bf16[6,1024,256]{2,1,0:T(8,128)(2,1)}, bf16[6,1024,256]{2,1,0:T(8,128)(2,1)}, bf16[6,1024,256]{2,1,0:T(8,128...) custom-call(s32[1]{0:T(128)} %bitcast.me_ref, ...), custom_call_target="tpu_custom_call" | custom-call | flops 2415919104 | bytes 16777216 | tf_op jit(solution)/shard_map/pallas_call | solution.py:233
  83.8 25.4 %shard_map.86 = (f32[1024,128]{1,0:T(8,128)}, f32[3,1024,256]{2,1,0:T(8,128)}, bf16[32,224,128]{2,1,0:T(8,128)(2,1)}) custom-call(s32[1]{0:T(128)} %bitcast.me_ref, bf16[3,1024,256]{2,1,0:T(8,128)(2,1)} %get-tuple-element.26.mixed_ref, bf16[1024,128]{1,0:T(8,128)(2,1)} %cotangent_ref.1, bf16[2,224,128]{2,1,0:T(8,128)(2,1)} %copy-done.5, ...), custom_call_target="tpu_custom_call" | custom-call | flops 4831838208 | bytes 8388608 | tf_op jit(solution)/shard_map/pallas_call | solution.py:233
  110.6 26.1 %shard_map.87 = (f32[1024,512]{1,0:T(8,128)}, f32[8,128]{1,0:T(8,128)}, bf16[32,304,128]{2,1,0:T(8,128)(2,1)}) custom-call(s32[1]{0:T(128)} %bitcast.me_ref, f32[3,1024,256]{2,1,0:T(8,128)} %get-tuple-element.28.mixed_grad_ref, bf16[1024,512]{1,0:T(8,128)(2,1)} %get-tuple-element.24.masked_ref, bf16[1024,512]{1,0:T(8,128)(2,1)} %get-tuple-element.29.level_ref, ...), custom_call_target="tpu_custom_call" | custom-call | flops 4831838208 | bytes 20971520 | tf_op jit(solution)/shard_map/pallas_call | solution.py:233
  136.7 2.6 %slice_bitcast_fusion = bf16[2,2,4,304,128]{4,3,2,1,0:T(8,128)(2,1)} fusion(bf16[2,2,2,4,304,128]{5,4,3,2,1,0:T(8,128)(2,1)} %bitcast.121), kind=kLoop, calls=%fused_computation.2 | loop fusion | bytes 2490368 | tf_op jit(solution)/shard_map/squeeze | solution.py:695
  141.3 1.6 collective-permute-start.53
  146.1 4.4 %collective-permute-done.40 = f32[8,128]{1,0:T(8,128)S(1)} collective-permute-done((f32[8,128]{1,0:T(8,128)S(1)}, f32[8,128]{1,0:T(8,128)S(1)}, u32[]{:S(2)}, u32[]{:S(2)}) %collective-permute-start.40) | collective-permute-done | bytes 4128 | tf_op jit(solution)/shard_map/ppermute | solution.py:656
  151.0 3.1 %collective-permute-done.41 = f32[8,128]{1,0:T(8,128)S(1)} collective-permute-done((f32[8,128]{1,0:T(8,128)S(1)}, f32[8,128]{1,0:T(8,128)S(1)}, u32[]{:S(2)}, u32[]{:S(2)}) %collective-permute-start.41) | collective-permute-done | bytes 4128 | tf_op jit(solution)/shard_map/ppermute | solution.py:656
  154.1 1.7 collective-permute-start.42
  155.8 1.9 collective-permute-done.42
  157.7 2.6 %collective-permute-start.43 = (f32[8,128]{1,0:T(8,128)S(1)}, f32[8,128]{1,0:T(8,128)S(1)}, u32[]{:S(2)}, u32[]{:S(2)}) collective-permute-start(f32[8,128]{1,0:T(8,128)S(1)} %add.140), channel_id=1, source_target_pairs={{0,2},{1,3},{2,0},{3,1},{4,6},{5,7},{6,4},{7,5},{8,10},{9,11},{10,... | collective-permute-start | bytes 12296 | tf_op jit(solution)/shard_map/ppermute | solution.py:656
  166.6 1.8 collective-permute-start.59
  168.5 1.8 collective-permute-done.45
  172.1 4.2 %collective-permute-done.49 = bf16[2,304,128]{2,1,0:T(8,128)(2,1)S(1)} collective-permute-done((bf16[2,304,128]{2,1,0:T(8,128)(2,1)S(1)}, bf16[2,304,128]{2,1,0:T(8,128)(2,1)S(1)}, u32[]{:S(2)}, u32[]{:S(2)}) %collective-permute-start.49) | collective-permute-done | bytes 155680 | tf_op jit(solution)/shard_map/ppermute | solution.py:656
  177.6 4.0 %collective-permute-done.46 = bf16[2,304,128]{2,1,0:T(8,128)(2,1)S(1)} collective-permute-done((bf16[2,304,128]{2,1,0:T(8,128)(2,1)S(1)}, bf16[2,304,128]{2,1,0:T(8,128)(2,1)S(1)}, u32[]{:S(2)}, u32[]{:S(2)}) %collective-permute-start.46) | collective-permute-done | bytes 155680 | tf_op jit(solution)/shard_map/ppermute | solution.py:656
  183.0 2.4 %collective-permute-start.51 = (bf16[304,128]{1,0:T(8,128)(2,1)S(1)}, bf16[304,128]{1,0:T(8,128)(2,1)S(1)}, u32[]{:S(2)}, u32[]{:S(2)}) collective-permute-start(bf16[304,128]{1,0:T(8,128)(2,1)S(1)} %get-tuple-element.55), channel_id=1, source_target_pairs={{0,3},{1,2},{2,1},{3,0},{4,7},{5,6},{6,5},{7,4},{8,11},{9,10},{10,... | collective-permute-start | bytes 233480 | tf_op jit(solution)/shard_map/ppermute | solution.py:656
  186.8 2.5 %collective-permute-done.51 = bf16[304,128]{1,0:T(8,128)(2,1)S(1)} collective-permute-done((bf16[304,128]{1,0:T(8,128)(2,1)S(1)}, bf16[304,128]{1,0:T(8,128)(2,1)S(1)}, u32[]{:S(2)}, u32[]{:S(2)}) %collective-permute-start.51) | collective-permute-done | bytes 77856 | tf_op jit(solution)/shard_map/ppermute | solution.py:656
  191.5 4.4 %shard_map.88 = f32[1024,512]{1,0:T(8,128)} custom-call(f32[1024,512]{1,0:T(8,128)} %get-tuple-element.40.level_grad_ref, bf16[1024,512]{1,0:T(8,128)(2,1)} %get-tuple-element.24.masked_ref, s32[1024,8]{1,0:T(8,128)} %copy.9.presence_ref, f32[8,512]{1,0:T(8,128)} %get-tuple-element.39.entry_ref, f32[8,128]{1,0:T(8,128)} %get-tuple-element.45.sums_ref), custom_call_target="tpu_custom_call" | custom-call | flops 5242880 | bytes 6291456 | tf_op jit(solution)/shard_map/pallas_call | solution.py:233
  (216 shorter events, 47.3 us)
Async XLA Ops:
  12.0 6.4 %collective-permute-start.2 = (f32[8,128]{1,0:T(8,128)S(1)}, f32[8,128]{1,0:T(8,128)S(1)}, u32[]{:S(2)}, u32[]{:S(2)}) collective-permute-start(f32[8,128]{1,0:T(8,128)S(1)} %pad_maximum_fusion.6), channel_id=1, source_target_pairs={{0,16},{4,20},{8,24},{12,28},{16,0},{20,4},{24,8},{28,12},{1,17},{... | collective-permute-start | bytes 12296 | tf_op jit(solution)/shard_map/ppermute | solution.py:656
  14.2 18.3 %collective-permute-start.6 = (bf16[304,128]{1,0:T(8,128)(2,1)S(1)}, bf16[304,128]{1,0:T(8,128)(2,1)S(1)}, u32[]{:S(2)}, u32[]{:S(2)}) collective-permute-start(bf16[304,128]{1,0:T(8,128)(2,1)S(1)} %get-tuple-element.59), channel_id=1, source_target_pairs={{0,2},{1,3},{2,0},{3,1},{4,6},{5,7},{6,4},{7,5},{8,10},{9,11},{10,... | collective-permute-start | bytes 233480 | tf_op jit(solution)/shard_map/ppermute | solution.py:656
  16.8 16.3 %collective-permute-start.7 = (bf16[304,128]{1,0:T(8,128)(2,1)S(1)}, bf16[304,128]{1,0:T(8,128)(2,1)S(1)}, u32[]{:S(2)}, u32[]{:S(2)}) collective-permute-start(bf16[304,128]{1,0:T(8,128)(2,1)S(1)} %get-tuple-element.59), channel_id=1, source_target_pairs={{0,3},{1,2},{2,1},{3,0},{4,7},{5,6},{6,5},{7,4},{8,11},{9,10},{10,... | collective-permute-start | bytes 233480 | tf_op jit(solution)/shard_map/ppermute | solution.py:656
  18.2 16.5 %collective-permute-start.5 = (bf16[304,128]{1,0:T(8,128)(2,1)S(1)}, bf16[304,128]{1,0:T(8,128)(2,1)S(1)}, u32[]{:S(2)}, u32[]{:S(2)}) collective-permute-start(bf16[304,128]{1,0:T(8,128)(2,1)S(1)} %get-tuple-element.59), channel_id=1, source_target_pairs={{0,1},{1,0},{2,3},{3,2},{4,5},{5,4},{6,7},{7,6},{8,9},{9,8},{10,11... | collective-permute-start | bytes 233480 | tf_op jit(solution)/shard_map/ppermute | solution.py:656
  20.3 6.0 %collective-permute-start.24 = (bf16[224,128]{1,0:T(8,128)(2,1)S(1)}, bf16[224,128]{1,0:T(8,128)(2,1)S(1)}, u32[]{:S(2)}, u32[]{:S(2)}) collective-permute-start(bf16[224,128]{1,0:T(8,128)(2,1)S(1)} %get-tuple-element.61), channel_id=1, source_target_pairs={{0,3},{1,2},{2,1},{3,0},{4,7},{5,6},{6,5},{7,4},{8,11},{9,10},{10,... | collective-permute-start | bytes 172040 | tf_op jit(solution)/shard_map/ppermute | solution.py:656
  32.5 6.7 %collective-permute-start.32 = (bf16[2,224,128]{2,1,0:T(8,128)(2,1)S(1)}, bf16[2,224,128]{2,1,0:T(8,128)(2,1)S(1)}, u32[]{:S(2)}, u32[]{:S(2)}) collective-permute-start(bf16[2,224,128]{2,1,0:T(8,128)(2,1)S(1)} %pad_maximum_fusion.4.rest_1_), channel_id=1, source_target_pairs={{0,16},{4,20},{8,24},{12,28},{16,0},{20,4},{24,8},{28,12},{1,17},{... | collective-permute-start | bytes 344072 | tf_op jit(solution)/shard_map/ppermute | solution.py:656
  34.7 6.6 %collective-permute-start.27 = (bf16[2,224,128]{2,1,0:T(8,128)(2,1)S(1)}, bf16[2,224,128]{2,1,0:T(8,128)(2,1)S(1)}, u32[]{:S(2)}, u32[]{:S(2)}) collective-permute-start(bf16[2,224,128]{2,1,0:T(8,128)(2,1)S(1)} %pad_maximum_fusion.3.rest_0_), channel_id=1, source_target_pairs={{0,8},{4,12},{8,0},{12,4},{16,24},{20,28},{24,16},{28,20},{1,9},{5... | collective-permute-start | bytes 344072 | tf_op jit(solution)/shard_map/ppermute | solution.py:656
  39.2 6.0 %collective-permute-start.14 = (bf16[2,304,128]{2,1,0:T(8,128)(2,1)S(1)}, bf16[2,304,128]{2,1,0:T(8,128)(2,1)S(1)}, u32[]{:S(2)}, u32[]{:S(2)}) collective-permute-start(bf16[2,304,128]{2,1,0:T(8,128)(2,1)S(1)} %pad_maximum_fusion.rest_0_), channel_id=1, source_target_pairs={{0,16},{4,20},{8,24},{12,28},{16,0},{20,4},{24,8},{28,12},{1,17},{... | collective-permute-start | bytes 466952 | tf_op jit(solution)/shard_map/ppermute | solution.py:656
  40.1 6.8 %collective-permute-start.15 = (bf16[2,304,128]{2,1,0:T(8,128)(2,1)S(1)}, bf16[2,304,128]{2,1,0:T(8,128)(2,1)S(1)}, u32[]{:S(2)}, u32[]{:S(2)}) collective-permute-start(bf16[2,304,128]{2,1,0:T(8,128)(2,1)S(1)} %pad_maximum_fusion.1.rest_1_), channel_id=1, source_target_pairs={{0,16},{4,20},{8,24},{12,28},{16,0},{20,4},{24,8},{28,12},{1,17},{... | collective-permute-start | bytes 466952 | tf_op jit(solution)/shard_map/ppermute | solution.py:656
  41.3 6.1 %collective-permute-start.9 = (bf16[2,304,128]{2,1,0:T(8,128)(2,1)S(1)}, bf16[2,304,128]{2,1,0:T(8,128)(2,1)S(1)}, u32[]{:S(2)}, u32[]{:S(2)}) collective-permute-start(bf16[2,304,128]{2,1,0:T(8,128)(2,1)S(1)} %pad_maximum_fusion.1.rest_1_), channel_id=1, source_target_pairs={{0,4},{4,0},{8,12},{12,8},{16,20},{20,16},{24,28},{28,24},{1,5},{5... | collective-permute-start | bytes 466952 | tf_op jit(solution)/shard_map/ppermute | solution.py:656
  41.3 6.4 %collective-permute-start.10 = (bf16[2,304,128]{2,1,0:T(8,128)(2,1)S(1)}, bf16[2,304,128]{2,1,0:T(8,128)(2,1)S(1)}, u32[]{:S(2)}, u32[]{:S(2)}) collective-permute-start(bf16[2,304,128]{2,1,0:T(8,128)(2,1)S(1)} %pad_maximum_fusion.rest_0_), channel_id=1, source_target_pairs={{0,8},{4,12},{8,0},{12,4},{16,24},{20,28},{24,16},{28,20},{1,9},{5... | collective-permute-start | bytes 466952 | tf_op jit(solution)/shard_map/ppermute | solution.py:656
  45.2 5.8 %collective-permute-start.36 = (bf16[2,224,128]{2,1,0:T(8,128)(2,1)S(1)}, bf16[2,224,128]{2,1,0:T(8,128)(2,1)S(1)}, u32[]{:S(2)}, u32[]{:S(2)}) collective-permute-start(bf16[2,224,128]{2,1,0:T(8,128)(2,1)S(1)} %collective-permute-done.28.rest_5_), channel_id=1, source_target_pairs={{0,16},{4,20},{8,24},{12,28},{16,0},{20,4},{24,8},{28,12},{1,17},{... | collective-permute-start | bytes 344072 | tf_op jit(solution)/shard_map/ppermute | solution.py:656
  46.9 9.4 %collective-permute-start.19 = (bf16[2,304,128]{2,1,0:T(8,128)(2,1)S(1)}, bf16[2,304,128]{2,1,0:T(8,128)(2,1)S(1)}, u32[]{:S(2)}, u32[]{:S(2)}) collective-permute-start(bf16[2,304,128]{2,1,0:T(8,128)(2,1)S(1)} %collective-permute-done.11.rest_5_), channel_id=1, source_target_pairs={{0,16},{4,20},{8,24},{12,28},{16,0},{20,4},{24,8},{28,12},{1,17},{... | collective-permute-start | bytes 466952 | tf_op jit(solution)/shard_map/ppermute | solution.py:656
  47.4 9.4 %collective-permute-start.13 = (bf16[2,304,128]{2,1,0:T(8,128)(2,1)S(1)}, bf16[2,304,128]{2,1,0:T(8,128)(2,1)S(1)}, u32[]{:S(2)}, u32[]{:S(2)}) collective-permute-start(bf16[2,304,128]{2,1,0:T(8,128)(2,1)S(1)} %collective-permute-done.11.rest_5_), channel_id=1, source_target_pairs={{0,4},{4,0},{8,12},{12,8},{16,20},{20,16},{24,28},{28,24},{1,5},{5... | collective-permute-start | bytes 466952 | tf_op jit(solution)/shard_map/ppermute | solution.py:656
  47.8 9.2 %collective-permute-start.18 = (bf16[2,304,128]{2,1,0:T(8,128)(2,1)S(1)}, bf16[2,304,128]{2,1,0:T(8,128)(2,1)S(1)}, u32[]{:S(2)}, u32[]{:S(2)}) collective-permute-start(bf16[2,304,128]{2,1,0:T(8,128)(2,1)S(1)} %collective-permute-done.14.rest_8_), channel_id=1, source_target_pairs={{0,8},{4,12},{8,0},{12,4},{16,24},{20,28},{24,16},{28,20},{1,9},{5... | collective-permute-start | bytes 466952 | tf_op jit(solution)/shard_map/ppermute | solution.py:656
  51.8 6.3 %collective-permute-start.16 = (bf16[2,304,128]{2,1,0:T(8,128)(2,1)S(1)}, bf16[2,304,128]{2,1,0:T(8,128)(2,1)S(1)}, u32[]{:S(2)}, u32[]{:S(2)}) collective-permute-start(bf16[2,304,128]{2,1,0:T(8,128)(2,1)S(1)} %collective-permute-done.14.rest_8_), channel_id=1, source_target_pairs={{0,4},{4,0},{8,12},{12,8},{16,20},{20,16},{24,28},{28,24},{1,5},{5... | collective-permute-start | bytes 466952 | tf_op jit(solution)/shard_map/ppermute | solution.py:656
  57.9 25.0 %collective-permute-start.33 = (bf16[2,224,128]{2,1,0:T(8,128)(2,1)S(1)}, bf16[2,224,128]{2,1,0:T(8,128)(2,1)S(1)}, u32[]{:S(2)}, u32[]{:S(2)}) collective-permute-start(bf16[2,224,128]{2,1,0:T(8,128)(2,1)S(1)} %collective-permute-done.31.rest_8_), channel_id=1, source_target_pairs={{0,4},{4,0},{8,12},{12,8},{16,20},{20,16},{24,28},{28,24},{1,5},{5... | collective-permute-start | bytes 344072 | tf_op jit(solution)/shard_map/ppermute | solution.py:656
  58.0 24.9 %collective-permute-start.34 = (bf16[2,224,128]{2,1,0:T(8,128)(2,1)S(1)}, bf16[2,224,128]{2,1,0:T(8,128)(2,1)S(1)}, u32[]{:S(2)}, u32[]{:S(2)}) collective-permute-start(bf16[2,224,128]{2,1,0:T(8,128)(2,1)S(1)} %collective-permute-done.32.rest_9_), channel_id=1, source_target_pairs={{0,4},{4,0},{8,12},{12,8},{16,20},{20,16},{24,28},{28,24},{1,5},{5... | collective-permute-start | bytes 344072 | tf_op jit(solution)/shard_map/ppermute | solution.py:656
  58.5 24.5 %collective-permute-start.29 = (bf16[2,224,128]{2,1,0:T(8,128)(2,1)S(1)}, bf16[2,224,128]{2,1,0:T(8,128)(2,1)S(1)}, u32[]{:S(2)}, u32[]{:S(2)}) collective-permute-start(bf16[2,224,128]{2,1,0:T(8,128)(2,1)S(1)} %collective-permute-done.27.rest_4_), channel_id=1, source_target_pairs={{0,4},{4,0},{8,12},{12,8},{16,20},{20,16},{24,28},{28,24},{1,5},{5... | collective-permute-start | bytes 344072 | tf_op jit(solution)/shard_map/ppermute | solution.py:656
  58.6 24.4 %collective-permute-start.38 = (bf16[2,224,128]{2,1,0:T(8,128)(2,1)S(1)}, bf16[2,224,128]{2,1,0:T(8,128)(2,1)S(1)}, u32[]{:S(2)}, u32[]{:S(2)}) collective-permute-start(bf16[2,224,128]{2,1,0:T(8,128)(2,1)S(1)} %collective-permute-done.36.rest_13_), channel_id=1, source_target_pairs={{0,4},{4,0},{8,12},{12,8},{16,20},{20,16},{24,28},{28,24},{1,5},{5... | collective-permute-start | bytes 344072 | tf_op jit(solution)/shard_map/ppermute | solution.py:656
  59.0 24.0 %collective-permute-start.37 = (bf16[2,224,128]{2,1,0:T(8,128)(2,1)S(1)}, bf16[2,224,128]{2,1,0:T(8,128)(2,1)S(1)}, u32[]{:S(2)}, u32[]{:S(2)}) collective-permute-start(bf16[2,224,128]{2,1,0:T(8,128)(2,1)S(1)} %collective-permute-done.35.rest_12_), channel_id=1, source_target_pairs={{0,4},{4,0},{8,12},{12,8},{16,20},{20,16},{24,28},{28,24},{1,5},{5... | collective-permute-start | bytes 344072 | tf_op jit(solution)/shard_map/ppermute | solution.py:656
  110.4 29.2 %collective-permute-start.52 = (bf16[2,2,4,224,128]{4,3,2,1,0:T(8,128)(2,1)S(1)}, bf16[2,2,4,224,128]{4,3,2,1,0:T(8,128)(2,1)S(1)}, u32[]{:S(2)}, u32[]{:S(2)}) collective-permute-start(bf16[2,2,4,224,128]{4,3,2,1,0:T(8,128)(2,1)S(1)} %slice_bitcast_fusion.2), channel_id=1, source_target_pairs={{0,4},{4,0},{8,12},{12,8},{16,20},{20,16},{24,28},{28,24},{1,5},{5... | collective-permute-start | bytes 2752520 | tf_op jit(solution)/shard_map/ppermute | solution.py:656
  139.2 23.0 %collective-permute-start.44 = (bf16[2,2,4,304,128]{4,3,2,1,0:T(8,128)(2,1)}, bf16[2,2,4,304,128]{4,3,2,1,0:T(8,128)(2,1)S(1)}, u32[]{:S(2)}, u32[]{:S(2)}) collective-permute-start(bf16[2,2,4,304,128]{4,3,2,1,0:T(8,128)(2,1)} %slice_bitcast_fusion), channel_id=1, source_target_pairs={{0,4},{4,0},{8,12},{12,8},{16,20},{20,16},{24,28},{28,24},{1,5},{5... | collective-permute-start | bytes 3735560 | tf_op jit(solution)/shard_map/ppermute | solution.py:656
  141.3 19.0 %collective-permute-start.53 = (bf16[2,2,224,128]{3,2,1,0:T(8,128)(2,1)}, bf16[2,2,224,128]{3,2,1,0:T(8,128)(2,1)S(1)}, u32[]{:S(2)}, u32[]{:S(2)}) collective-permute-start(bf16[2,2,224,128]{3,2,1,0:T(8,128)(2,1)} %slice_bitcast_fusion.15), channel_id=1, source_target_pairs={{0,16},{4,20},{8,24},{12,28},{16,0},{20,4},{24,8},{28,12},{1,17},{... | collective-permute-start | bytes 688136 | tf_op jit(solution)/shard_map/ppermute | solution.py:656
  142.9 17.4 %collective-permute-start.56 = (bf16[2,2,224,128]{3,2,1,0:T(8,128)(2,1)}, bf16[2,2,224,128]{3,2,1,0:T(8,128)(2,1)S(1)}, u32[]{:S(2)}, u32[]{:S(2)}) collective-permute-start(bf16[2,2,224,128]{3,2,1,0:T(8,128)(2,1)} %slice_bitcast_fusion.13), channel_id=1, source_target_pairs={{0,8},{4,12},{8,0},{12,4},{16,24},{20,28},{24,16},{28,20},{1,9},{5... | collective-permute-start | bytes 688136 | tf_op jit(solution)/shard_map/ppermute | solution.py:656
  157.7 32.5 %collective-permute-start.43 = (f32[8,128]{1,0:T(8,128)S(1)}, f32[8,128]{1,0:T(8,128)S(1)}, u32[]{:S(2)}, u32[]{:S(2)}) collective-permute-start(f32[8,128]{1,0:T(8,128)S(1)} %add.140), channel_id=1, source_target_pairs={{0,2},{1,3},{2,0},{3,1},{4,6},{5,7},{6,4},{7,5},{8,10},{9,11},{10,... | collective-permute-start | bytes 12296 | tf_op jit(solution)/shard_map/ppermute | solution.py:656
  162.7 7.6 %collective-permute-start.45 = (bf16[2,2,304,128]{3,2,1,0:T(8,128)(2,1)S(1)}, bf16[2,2,304,128]{3,2,1,0:T(8,128)(2,1)S(1)}, u32[]{:S(2)}, u32[]{:S(2)}) collective-permute-start(bf16[2,2,304,128]{3,2,1,0:T(8,128)(2,1)S(1)} %slice_bitcast_fusion.11), channel_id=1, source_target_pairs={{0,16},{4,20},{8,24},{12,28},{16,0},{20,4},{24,8},{28,12},{1,17},{... | collective-permute-start | bytes 933896 | tf_op jit(solution)/shard_map/ppermute | solution.py:656
  164.0 6.9 %collective-permute-start.48 = (bf16[2,2,304,128]{3,2,1,0:T(8,128)(2,1)S(1)}, bf16[2,2,304,128]{3,2,1,0:T(8,128)(2,1)S(1)}, u32[]{:S(2)}, u32[]{:S(2)}) collective-permute-start(bf16[2,2,304,128]{3,2,1,0:T(8,128)(2,1)S(1)} %slice_bitcast_fusion.9), channel_id=1, source_target_pairs={{0,8},{4,12},{8,0},{12,4},{16,24},{20,28},{24,16},{28,20},{1,9},{5... | collective-permute-start | bytes 933896 | tf_op jit(solution)/shard_map/ppermute | solution.py:656
  165.7 17.3 %collective-permute-start.58 = (bf16[224,128]{1,0:T(8,128)(2,1)S(1)}, bf16[224,128]{1,0:T(8,128)(2,1)S(1)}, u32[]{:S(2)}, u32[]{:S(2)}) collective-permute-start(bf16[224,128]{1,0:T(8,128)(2,1)S(1)} %get-tuple-element.56), channel_id=1, source_target_pairs={{0,2},{1,3},{2,0},{3,1},{4,6},{5,7},{6,4},{7,5},{8,10},{9,11},{10,... | collective-permute-start | bytes 172040 | tf_op jit(solution)/shard_map/ppermute | solution.py:656
  166.6 18.8 %collective-permute-start.59 = (bf16[224,128]{1,0:T(8,128)(2,1)S(1)}, bf16[224,128]{1,0:T(8,128)(2,1)S(1)}, u32[]{:S(2)}, u32[]{:S(2)}) collective-permute-start(bf16[224,128]{1,0:T(8,128)(2,1)S(1)} %get-tuple-element.57), channel_id=1, source_target_pairs={{0,3},{1,2},{2,1},{3,0},{4,7},{5,6},{6,5},{7,4},{8,11},{9,10},{10,... | collective-permute-start | bytes 172040 | tf_op jit(solution)/shard_map/ppermute | solution.py:656
  170.3 15.2 %collective-permute-start.55 = (bf16[224,128]{1,0:T(8,128)(2,1)S(1)}, bf16[224,128]{1,0:T(8,128)(2,1)S(1)}, u32[]{:S(2)}, u32[]{:S(2)}) collective-permute-start(bf16[224,128]{1,0:T(8,128)(2,1)S(1)} %fusion.21), channel_id=1, source_target_pairs={{0,1},{1,0},{2,3},{3,2},{4,5},{5,4},{6,7},{7,6},{8,9},{9,8},{10,11... | collective-permute-start | bytes 172040 | tf_op jit(solution)/shard_map/ppermute | solution.py:656
  183.0 6.3 %collective-permute-start.51 = (bf16[304,128]{1,0:T(8,128)(2,1)S(1)}, bf16[304,128]{1,0:T(8,128)(2,1)S(1)}, u32[]{:S(2)}, u32[]{:S(2)}) collective-permute-start(bf16[304,128]{1,0:T(8,128)(2,1)S(1)} %get-tuple-element.55), channel_id=1, source_target_pairs={{0,3},{1,2},{2,1},{3,0},{4,7},{5,6},{6,5},{7,4},{8,11},{9,10},{10,... | collective-permute-start | bytes 233480 | tf_op jit(solution)/shard_map/ppermute | solution.py:656
  (65 other events, 755.1 us)

commit v2 on v1

v2 whole, which is shorter than its diff:
```python
import functools
import math

import jax
import jax.numpy as jnp
from jax import lax
from jax.experimental import pallas as pl
from jax.experimental.pallas import tpu as pltpu
from jax.sharding import PartitionSpec as P

H = 256
TOWER1 = 128
TOWER2 = 64
LANES = 128
EPSILON = 1e-05
AXES = ("wide", "narrow")
F32 = jnp.float32
BF16 = jnp.bfloat16
GROUPS_ONE = ((0, 4), (4, 8), (8, 14))
MEMBERS_ONE = ((0, 1, 4, 5), (2, 3, 4, 5), (0, 1, 2, 3, 4, 5))
GROUPS_TWO = ((0, 4), (4, 8))
MEMBERS_TWO = ((0, 1, 4, 5), (2, 3, 4, 5))


def up(value, step):
    return -(-value // step) * step


def mm(left, right):
    return jnp.dot(left, right, preferred_element_type=F32)


def mm_nt(left, right):
    return lax.dot_general(left, right, (((1,), (1,)), ((), ())), preferred_element_type=F32)


def mm_tn(left, right):
    return lax.dot_general(left, right, (((0,), (0,)), ((), ())), preferred_element_type=F32)


def sigmoid(values):
    return 0.5 * jnp.tanh(0.5 * values) + 0.5


def group_softmax(logits, groups):
    lane = lax.broadcasted_iota(jnp.int32, logits.shape, 1)
    spread = jnp.zeros_like(logits)
    for low, high in groups:
        inside = (lane >= low) & (lane < high)
        peak = jnp.max(jnp.where(inside, logits, -jnp.inf), axis=1, keepdims=True)
        spread = jnp.where(inside, logits - peak, spread)
    raw = jnp.exp(spread)
    result = jnp.zeros_like(logits)
    for low, high in groups:
        inside = (lane >= low) & (lane < high)
        total = jnp.sum(jnp.where(inside, raw, 0.0), axis=1, keepdims=True)
        result = jnp.where(inside, raw / total, result)
    return result


def group_softmax_back(probs, grads, groups):
    lane = lax.broadcasted_iota(jnp.int32, probs.shape, 1)
    product = probs * grads
    result = jnp.zeros_like(probs)
    for low, high in groups:
        inside = (lane >= low) & (lane < high)
        total = jnp.sum(jnp.where(inside, product, 0.0), axis=1, keepdims=True)
        result = jnp.where(inside, product - probs * total, result)
    return result


def into_lane(columns):
    rows = columns[0].shape[0]
    lane = lax.broadcasted_iota(jnp.int32, (rows, LANES), 1)
    result = jnp.zeros((rows, LANES), F32)
    for position, column in enumerate(columns):
        result = jnp.where(lane == position, column, result)
    return result


def mix_parts(weights, low, members, outputs):
    running = None
    for position, member in enumerate(members):
        term = column_block(weights, low + position) * outputs[member]
        running = term if running is None else running + term
    return running


def row_sum(values):
    return jnp.sum(values, axis=1, keepdims=True)


def column_sum(values):
    return jnp.sum(values, axis=0, keepdims=True)


def norm_forward(post):
    centred = post - row_sum(post) * (1.0 / H)
    scale = lax.rsqrt(row_sum(centred * centred) * (1.0 / H) + EPSILON)
    return centred * scale, scale


def twice(values):
    return jnp.concatenate([values, values], axis=1)


def norm_backward(scaled, normal, scale, means):
    both = jnp.concatenate([scaled.astype(BF16), (scaled * normal).astype(BF16)], axis=1)
    mean = mm(both, means)
    return twice(scale) * (
        scaled - twice(mean[:, :LANES]) - normal * twice(mean[:, LANES:])
    )


def make_means():
    row = lax.broadcasted_iota(jnp.int32, (2 * H, 2 * LANES), 0)
    lane = lax.broadcasted_iota(jnp.int32, (2 * H, 2 * LANES), 1)
    return jnp.where((row < H) == (lane < LANES), 1.0 / H, 0.0).astype(BF16)


def make_spread(columns):
    row = lax.broadcasted_iota(jnp.int32, (2 * LANES, columns * LANES), 0)
    lane = lax.broadcasted_iota(jnp.int32, (2 * LANES, columns * LANES), 1)
    return jnp.where((row & (LANES - 1)) == (lane >> 7), 1.0, 0.0).astype(BF16)


def spread_columns(values, spread):
    high = values.astype(BF16)
    low = (values - high.astype(F32)).astype(BF16)
    return mm(jnp.concatenate([high, low], axis=1), spread)


def column_block(spread, column):
    return twice(spread[:, column * LANES : (column + 1) * LANES])


def first_layout(width):
    names = (
        ("in_gain", width),
        ("in_bias", width),
        ("expert_in", 6 * width * H),
        ("expert_in_bias", 6 * H),
        ("expert_out", 6 * H * H),
        ("expert_out_bias", 6 * H),
        ("norm_gain", 6 * H),
        ("norm_bias", 6 * H),
        ("gate", 14 * width),
    )
    return place_names(names)


def second_layout():
    names = (
        ("expert_in", 6 * H * H),
        ("expert_in_bias", 6 * H),
        ("expert_out", 6 * H * H),
        ("expert_out_bias", 6 * H),
        ("norm_gain", 6 * H),
        ("norm_bias", 6 * H),
        ("gate", 2 * H * 4),
        ("tower_in", 2 * H * TOWER1),
        ("tower_in_bias", 2 * TOWER1),
        ("tower_out", 2 * TOWER1 * TOWER2),
        ("tower_out_bias", 2 * TOWER2),
    )
    return place_names(names)


def place_names(names):
    rows = {}
    offset = 0
    for name, amount in names:
        rows[name] = offset // LANES
        offset += amount
    return rows, offset // LANES


def spread_pieces(me, rows, piece_refs, flat_ref, extra_ref=None):
    slot = 0
    for ref in piece_refs:
        for index in range(ref.shape[0]):
            owner = lax.bitwise_xor(me, jnp.int32(slot))
            block = ref[index].astype(F32)
            flat_ref[pl.ds(owner * rows, rows), :] = block[:rows]
            if extra_ref is not None:
                extra_ref[slot] = block[rows : rows + extra_ref.shape[1]]
            slot += 1


def wide_rows(flat_ref, row, amount):
    return jnp.concatenate(
        [flat_ref[pl.ds(row, amount, stride=2), :], flat_ref[pl.ds(row + 1, amount, stride=2), :]],
        axis=1,
    )


def put_wide_rows(flat_ref, row, amount, value):
    flat_ref[pl.ds(row, amount, stride=2), :] = value[:, :LANES]
    flat_ref[pl.ds(row + 1, amount, stride=2), :] = value[:, LANES:]


def collect_pieces(me, count, rows, flat_ref, out_refs):
    for slot in range(count):
        owner = lax.bitwise_xor(me, jnp.int32(slot))
        value = flat_ref[pl.ds(owner * rows, rows), :].astype(BF16)
        if len(out_refs) == 1:
            out_refs[0][slot, :rows, :] = value
        else:
            part, place = slot // 4 % 2, slot // 8 * 4 + slot % 4
            out_refs[part][place, :rows, :] = value


def roll_rows(value, columns, sign):
    item = lax.broadcasted_iota(jnp.int32, value.shape, 0)
    bit = 1
    while columns * bit % LANES:
        moved = pltpu.roll(value, sign * columns * bit % LANES, 1)
        value = jnp.where((item & bit) != 0, moved, value)
        bit *= 2
    return value


def table_places(width, columns, rows):
    item = lax.broadcasted_iota(jnp.int32, (width, rows), 0)
    index = lax.broadcasted_iota(jnp.int32, (width, rows), 1)
    first = (index == ((item * columns) >> 7)).astype(F32).astype(BF16)
    last = (index == ((item * columns + columns - 1) >> 7)).astype(F32).astype(BF16)
    item = lax.broadcasted_iota(jnp.int32, (width, LANES), 0)
    lane = lax.broadcasted_iota(jnp.int32, (width, LANES), 1)
    return first, last, lane >= ((item * columns) & (LANES - 1)), lane < columns


def table_from_rows(flat, width, columns):
    first, last, late, used = table_places(width, columns, flat.shape[0])
    chosen = jnp.where(late, mm(first, flat), mm(last, flat))
    return jnp.where(used, roll_rows(chosen, columns, -1), 0.0)


def rows_from_table(table, rows, columns):
    first, last, late, _ = table_places(table.shape[0], columns, rows)
    moved = roll_rows(table, columns, 1)
    return mm_tn(first, jnp.where(late, moved, 0.0).astype(BF16)) + mm_tn(
        last, jnp.where(late, 0.0, moved).astype(BF16)
    )


def full_spec():
    return pl.BlockSpec(memory_space=pltpu.VMEM)


def scalar_spec():
    return pl.BlockSpec(memory_space=pltpu.SMEM)


def run_kernel(kernel, inputs, out_shape, scratch, limit, flops, scalar=True):
    specs = [full_spec()] * len(inputs)
    if scalar:
        specs[0] = scalar_spec()
    out_specs = jax.tree.map(lambda _: full_spec(), out_shape)
    return pl.pallas_call(
        kernel,
        in_specs=specs,
        out_specs=out_specs,
        out_shape=out_shape,
        scratch_shapes=scratch,
        compiler_params=pltpu.CompilerParams(vmem_limit_bytes=limit * 2**20),
        cost_estimate=pl.CostEstimate(flops=2**20, bytes_accessed=2**10, transcendentals=0),
    )(*inputs)


def spread_presence(presence, width):
    fields = presence.shape[0]
    field = lax.broadcasted_iota(jnp.int32, (fields, width), 0)
    column = lax.broadcasted_iota(jnp.int32, (fields, width), 1)
    pick = (column // (width // fields) == field).astype(F32).astype(BF16)
    return mm_tn(presence.astype(F32).astype(BF16), pick)


def split_three(values):
    parts = []
    for _ in range(3):
        part = values.astype(BF16).astype(F32)
        parts.append(part)
        values = values - part
    return parts


def stats_kernel(
    me_ref, features_ref, presence_ref, params_ref, second_ref, masked_ref, block_ref, block_two_ref
):
    del me_ref
    rows, width = features_ref.shape
    mask = spread_presence(presence_ref[...], width)
    masked = features_ref[...].astype(F32) * mask
    masked_ref[...] = masked.astype(BF16)
    mean = column_sum(masked) * (1.0 / rows)
    spread = masked - mean
    moment = column_sum(spread * spread)
    lines = [params_ref[...].astype(F32)]
    for value in (mean, moment):
        for part in split_three(value):
            for index in range(width // LANES):
                lines.append(part[:, index * LANES : (index + 1) * LANES])
    used = params_ref.shape[0] + 6 * (width // LANES)
    lines.append(jnp.zeros((block_ref.shape[0] - used, LANES), F32))
    block_ref[...] = jnp.concatenate(lines, axis=0).astype(BF16)
    second = second_ref[...].astype(F32)
    rest = jnp.zeros((block_two_ref.shape[0] - second.shape[0], LANES), F32)
    block_two_ref[...] = jnp.concatenate([second, rest], axis=0).astype(BF16)


def from_lanes(block):
    return jnp.concatenate([block[index : index + 1, :] for index in range(block.shape[0])], axis=1)


def tiles(tile):
    return lambda ref_rows, body: lax.fori_loop(
        0, ref_rows // tile, lambda step, carry: body(pl.multiple_of(step * tile, tile), carry), 0
    )


def spot(e):
    return slice(e * H, (e + 1) * H)


def level_one_forward(
    rows,
    tile,
    n_pieces,
    me_ref,
    masked_ref,
    *rest,
):
    piece_refs = rest[:n_pieces]
    (
        level_ref,
        active_ref,
        slope_ref,
        normal_ref,
        scale_ref,
        probs_ref,
        mixed_ref,
        w_in_ref,
        w_out_ref,
        small_ref,
        gate_ref,
        entry_ref,
        flat_ref,
        extra_ref,
        output_ref,
        wide_ref,
        spread_ref,
    ) = rest[n_pieces:]
    width = masked_ref.shape[1]
    where_row, _ = first_layout(width)

    spread_pieces(me_ref[0], rows, piece_refs, flat_ref, extra_ref)
    spread_ref[...] = make_spread(14)
    for e in range(6):
        w_in_ref[:, spot(e)] = wide_rows(
            flat_ref, where_row["expert_in"] + e * 2 * width, width
        ).astype(BF16)
        w_out_ref[e] = wide_rows(flat_ref, where_row["expert_out"] + e * 2 * H, H).astype(BF16)
    for index, name in enumerate(("expert_in_bias", "expert_out_bias", "norm_gain", "norm_bias")):
        small_ref[index, :6, :] = wide_rows(flat_ref, where_row[name], 6)
    gate_flat = flat_ref[pl.ds(where_row["gate"], 14 * width // LANES), :].astype(BF16)
    gate_ref[...] = table_from_rows(gate_flat, width, 14).astype(BF16)
    lanes = width // LANES
    events = masked_ref.shape[0]
    count = extra_ref.shape[0]
    means = extra_ref[:, 0:lanes, :]
    for part in (1, 2):
        means = means + extra_ref[:, part * lanes : (part + 1) * lanes, :]
    mean = jnp.sum(means, axis=0) * (1.0 / count)
    away = jnp.sum(jnp.square(means - mean[None]), axis=0) * events
    for part in (3, 4, 5):
        away = away + jnp.sum(extra_ref[:, part * lanes : (part + 1) * lanes, :], axis=0)
    entry_ref[0:1, :] = from_lanes(mean)
    entry_ref[1:2, :] = from_lanes(lax.rsqrt(away * (1.0 / (events * count)) + EPSILON))
    entry_ref[2:3, :] = from_lanes(flat_ref[0:lanes, :])
    entry_ref[3:4, :] = from_lanes(flat_ref[lanes : 2 * lanes, :])

    def body(start, carry):
        now = pl.ds(start, tile)
        normed = (masked_ref[now, :].astype(F32) - entry_ref[0:1, :]) * entry_ref[1:2, :]
        level_ref[now, :] = (normed * entry_ref[2:3, :] + entry_ref[3:4, :]).astype(BF16)
        probs_ref[now, :] = group_softmax(mm(level_ref[now, :], gate_ref[...]), GROUPS_ONE)
        for e in range(6):
            pre = mm(level_ref[now, :], w_in_ref[:, spot(e)]) + small_ref[0, e : e + 1, :]
            gate = sigmoid(pre)
            silu = pre * gate
            active_ref[e, now, :] = silu.astype(BF16)
            slope_ref[e, now, :] = (gate + silu * (1.0 - gate)).astype(BF16)
        for e in range(6):
            post = mm(active_ref[e, now, :], w_out_ref[e]) + small_ref[1, e : e + 1, :]
            normal, scale = norm_forward(post)
            normal_ref[e, now, :] = normal.astype(BF16)
            scale_ref[e, now, :] = jnp.broadcast_to(scale, (tile, LANES))
            output_ref[e] = normal * small_ref[2, e : e + 1, :] + small_ref[3, e : e + 1, :]
        wide_ref[...] = spread_columns(probs_ref[now, :], spread_ref[...])
        for index, (low, _) in enumerate(GROUPS_ONE):
            mixed_ref[index, now, :] = mix_parts(
                wide_ref, low, MEMBERS_ONE[index], output_ref
            ).astype(BF16)
        return carry

    tiles(tile)(masked_ref.shape[0], body)


def level_two(count, rows, tile, n_pieces, n_outs, me_ref, mixed_ref, cotangent_ref, *rest):
    piece_refs = rest[:n_pieces]
    grads_refs = rest[n_pieces + 2 : n_pieces + 2 + n_outs]
    towers_ref, mixed_grad_ref = rest[n_pieces : n_pieces + 2]
    (
        flat_ref,
        w_in_ref,
        w_out_ref,
        small_ref,
        gate_ref,
        tower_in_ref,
        tower_out_ref,
        tower_tmp_ref,
        tower_small_ref,
        g_small_ref,
        g_tower_out_ref,
        g_tower_small_ref,
        active_ref,
        slope_ref,
        normal_ref,
        scale_ref,
        output_ref,
        combined_ref,
        combined_grad_ref,
        tower_active_ref,
        tower_grad_ref,
        logit_ref,
        post_grad_ref,
        pre_grad_ref,
        wide_ref,
        spread_ref,
        means_ref,
    ) = rest[n_pieces + 2 + n_outs :]
    where_row, used_rows = second_layout()
    all_rows = mixed_ref.shape[1]

    spread_pieces(me_ref[0], rows, piece_refs, flat_ref)
    spread_ref[...] = make_spread(8)
    means_ref[...] = make_means()
    for e in range(6):
        w_in_ref[:, spot(e)] = wide_rows(flat_ref, where_row["expert_in"] + e * 2 * H, H).astype(
            BF16
        )
        w_out_ref[e] = wide_rows(flat_ref, where_row["expert_out"] + e * 2 * H, H).astype(BF16)
    for index, name in enumerate(("expert_in_bias", "expert_out_bias", "norm_gain", "norm_bias")):
        small_ref[index, :6, :] = wide_rows(flat_ref, where_row[name], 6)
    gate_rows = H * 4 // LANES
    shift_a = lax.broadcasted_iota(jnp.int32, (LANES, LANES), 0)
    shift_b = lax.broadcasted_iota(jnp.int32, (LANES, LANES), 1)
    shift = ((shift_a + 4 == shift_b) & (shift_a < 4)).astype(F32).astype(BF16)
    tables = []
    for task in range(2):
        piece = flat_ref[pl.ds(where_row["gate"] + task * gate_rows, gate_rows), :].astype(BF16)
        tables.append(table_from_rows(piece, H, 4).astype(BF16))
    gate_ref[...] = (tables[0].astype(F32) + mm(tables[1], shift)).astype(BF16)
    zero = jnp.zeros((TOWER1 // 2, TOWER2), F32)
    for task in range(2):
        tower_in_ref[task] = flat_ref[pl.ds(where_row["tower_in"] + task * H, H), :].astype(BF16)
        packed = flat_ref[pl.ds(where_row["tower_out"] + task * TOWER1 // 2, TOWER1 // 2), :]
        for half in range(2):
            pair = [packed[:, half * TOWER2 : (half + 1) * TOWER2], zero]
            if task == 1:
                pair.reverse()
            tower_tmp_ref[pl.ds(task * TOWER1 + half, TOWER1 // 2, stride=2), :] = jnp.concatenate(
                pair, axis=1
            )
    tower_out_ref[...] = tower_tmp_ref[...].astype(BF16)
    tower_small_ref[0:1, :] = from_lanes(flat_ref[pl.ds(where_row["tower_in_bias"], 2), :])
    tower_small_ref[1:2, :LANES] = flat_ref[pl.ds(where_row["tower_out_bias"], 1), :]
    g_small_ref[...] = jnp.zeros(g_small_ref.shape, F32)
    g_tower_small_ref[...] = jnp.zeros(g_tower_small_ref.shape, F32)

    def body(start, carry):
        now = pl.ds(start, tile)
        lane = lax.broadcasted_iota(jnp.int32, (tile, LANES), 1)
        for e in range(6):
            pre = mm(mixed_ref[e // 2, now, :], w_in_ref[:, spot(e)]) + small_ref[0, e : e + 1, :]
            gate = sigmoid(pre)
            silu = pre * gate
            active_ref[e, now, :] = silu.astype(BF16)
            slope_ref[:, spot(e)] = gate + silu * (1.0 - gate)
        for e in range(6):
            post = mm(active_ref[e, now, :], w_out_ref[e]) + small_ref[1, e : e + 1, :]
            normal, scale = norm_forward(post)
            normal_ref[e] = normal
            scale_ref[e] = jnp.broadcast_to(scale, (tile, LANES))
            output_ref[e] = normal * small_ref[2, e : e + 1, :] + small_ref[3, e : e + 1, :]
        logits = jnp.where(
            lane < 4, mm(mixed_ref[0, now, :], gate_ref[...]), mm(mixed_ref[1, now, :], gate_ref[...])
        )
        probs = group_softmax(logits, GROUPS_TWO)
        wide_ref[...] = spread_columns(probs, spread_ref[...])
        for task in range(2):
            combined_ref[task, now, :] = mix_parts(
                wide_ref, 4 * task, MEMBERS_TWO[task], output_ref
            ).astype(BF16)
        tower_pre = (
            jnp.concatenate(
                [mm(combined_ref[task, now, :], tower_in_ref[task]) for task in range(2)], axis=1
            )
            + tower_small_ref[0:1, :]
        )
        tower_gate = sigmoid(tower_pre)
        tower_silu = tower_pre * tower_gate
        tower_active_ref[now, :] = tower_silu.astype(BF16)
        towers_ref[now, :] = (
            mm(tower_active_ref[now, :], tower_out_ref[...]) + tower_small_ref[1:2, :LANES]
        )
        cotangent = cotangent_ref[now, :]
        g_tower_small_ref[1:2, :LANES] += column_sum(cotangent.astype(F32))
        tower_slope = tower_gate + tower_silu * (1.0 - tower_gate)
        tower_grad = (mm_nt(cotangent, tower_out_ref[...]) * tower_slope).astype(BF16)
        tower_grad_ref[now, :] = tower_grad
        g_tower_small_ref[0:1, :] += column_sum(tower_grad.astype(F32))
        for task in range(2):
            combined_grad_ref[task] = mm_nt(
                tower_grad_ref[now, task * TOWER1 : (task + 1) * TOWER1], tower_in_ref[task]
            )
        prob_grads = into_lane(
            [
                row_sum(combined_grad_ref[task] * output_ref[member])
                for task in range(2)
                for member in MEMBERS_TWO[task]
            ]
        )
        logit_grad = group_softmax_back(probs, prob_grads, GROUPS_TWO)
        logit_ref[0, now, :] = jnp.where(lane < 4, logit_grad, 0.0).astype(BF16)
        logit_ref[1, now, :] = jnp.where((lane >= 4) & (lane < 8), logit_grad, 0.0).astype(BF16)
        for e in range(6):
            out_grad = None
            for task in range(2):
                if e in MEMBERS_TWO[task]:
                    column = 4 * task + MEMBERS_TWO[task].index(e)
                    term = column_block(wide_ref, column) * combined_grad_ref[task]
                    out_grad = term if out_grad is None else out_grad + term
            normal = normal_ref[e]
            g_small_ref[2, e : e + 1, :] += column_sum(out_grad * normal)
            g_small_ref[3, e : e + 1, :] += column_sum(out_grad)
            post_grad = norm_backward(
                out_grad * small_ref[2, e : e + 1, :], normal, scale_ref[e], means_ref[...]
            )
            post_grad = post_grad.astype(BF16)
            post_grad_ref[e, now, :] = post_grad
            g_small_ref[1, e : e + 1, :] += column_sum(post_grad.astype(F32))
        for e in range(6):
            act_grad = mm_nt(post_grad_ref[e, now, :], w_out_ref[e])
            pre_grad = (act_grad * slope_ref[:, spot(e)]).astype(BF16)
            pre_grad_ref[now, spot(e)] = pre_grad
            g_small_ref[0, e : e + 1, :] += column_sum(pre_grad.astype(F32))
        for index in range(3):
            pair = slice(2 * index * H, 2 * (index + 1) * H)
            grad = mm_nt(pre_grad_ref[now, pair], w_in_ref[:, pair])
            if index < 2:
                grad = grad + mm_nt(logit_ref[index, now, :], gate_ref[...])
            mixed_grad_ref[index, now, :] = grad
        return carry

    tiles(tile)(all_rows, body)

    for e in range(6):
        put_wide_rows(
            flat_ref,
            where_row["expert_in"] + e * 2 * H,
            H,
            mm_tn(mixed_ref[e // 2], pre_grad_ref[:, spot(e)]),
        )
        put_wide_rows(
            flat_ref,
            where_row["expert_out"] + e * 2 * H,
            H,
            mm_tn(active_ref[e], post_grad_ref[e]),
        )
    for index, name in enumerate(("expert_in_bias", "expert_out_bias", "norm_gain", "norm_bias")):
        put_wide_rows(flat_ref, where_row[name], 6, g_small_ref[index, :6, :])
    back = ((shift_a == shift_b + 4) & (shift_b < 4)).astype(F32).astype(BF16)
    tables = [mm_tn(mixed_ref[task], logit_ref[task]) for task in range(2)]
    tables[1] = mm(tables[1].astype(BF16), back)
    g_tower_out_ref[...] = mm_tn(tower_active_ref[...], cotangent_ref[...])
    for task in range(2):
        flat_ref[pl.ds(where_row["gate"] + task * gate_rows, gate_rows), :] = rows_from_table(
            tables[task], gate_rows, 4
        )
        flat_ref[pl.ds(where_row["tower_in"] + task * H, H), :] = mm_tn(
            combined_ref[task], tower_grad_ref[:, task * TOWER1 : (task + 1) * TOWER1]
        )
        flat_ref[pl.ds(where_row["tower_out"] + task * TOWER1 // 2, TOWER1 // 2), :] = (
            jnp.concatenate(
                [
                    g_tower_out_ref[pl.ds(task * TOWER1 + half, TOWER1 // 2, stride=2), :][
                        :, task * TOWER2 : (task + 1) * TOWER2
                    ]
                    for half in range(2)
                ],
                axis=1,
            )
        )
        flat_ref[pl.ds(where_row["tower_in_bias"] + task, 1), :] = g_tower_small_ref[
            0:1, task * TOWER1 : (task + 1) * TOWER1
        ]
    flat_ref[pl.ds(where_row["tower_out_bias"], 1), :] = g_tower_small_ref[1:2, :LANES]
    if used_rows < count * rows:
        flat_ref[pl.ds(used_rows, count * rows - used_rows), :] = jnp.zeros(
            (count * rows - used_rows, LANES), F32
        )
    collect_pieces(me_ref[0], count, rows, flat_ref, grads_refs)


def level_one_backward(
    tile,
    begin,
    mixed_grad_ref,
    masked_ref,
    slope_ref,
    normal_ref,
    scale_ref,
    probs_ref,
    w_in_ref,
    w_out_ref,
    small_ref,
    gate_ref,
    entry_ref,
    *rest,
):
    if begin:
        before_sum_ref, before_small_ref, *rest = rest
    (
        level_grad_ref,
        g_sum_ref,
        g_small_ref,
        logit_ref,
        post_grad_ref,
        pre_grad_ref,
        wide_ref,
        spread_ref,
        means_ref,
    ) = rest
    spread_ref[...] = make_spread(14)
    means_ref[...] = make_means()
    if begin:
        g_small_ref[...] = before_small_ref[...]
        g_sum_ref[...] = before_sum_ref[...]
    else:
        g_small_ref[...] = jnp.zeros(g_small_ref.shape, F32)
        g_sum_ref[...] = jnp.zeros(g_sum_ref.shape, F32)

    def body(start, carry):
        here = pl.ds(start, tile)
        now = pl.ds(begin + start, tile)
        probs = probs_ref[now, :]
        wide_ref[...] = spread_columns(probs, spread_ref[...])
        columns = [None] * 14
        for e in range(6):
            output = (
                normal_ref[e, now, :].astype(F32) * small_ref[2, e : e + 1, :]
                + small_ref[3, e : e + 1, :]
            )
            for index, (low, _) in enumerate(GROUPS_ONE):
                if e in MEMBERS_ONE[index]:
                    columns[low + MEMBERS_ONE[index].index(e)] = row_sum(
                        mixed_grad_ref[index, now, :] * output
                    )
        logit_ref[here, :] = group_softmax_back(probs, into_lane(columns), GROUPS_ONE).astype(BF16)
        for e in range(6):
            normal = normal_ref[e, now, :].astype(F32)
            out_grad = None
            for index, (low, _) in enumerate(GROUPS_ONE):
                if e in MEMBERS_ONE[index]:
                    column = low + MEMBERS_ONE[index].index(e)
                    term = column_block(wide_ref, column) * mixed_grad_ref[index, now, :]
                    out_grad = term if out_grad is None else out_grad + term
            g_small_ref[2, e : e + 1, :] += column_sum(out_grad * normal)
            g_small_ref[3, e : e + 1, :] += column_sum(out_grad)
            post_grad = norm_backward(
                out_grad * small_ref[2, e : e + 1, :],
                normal,
                scale_ref[e, now, :],
                means_ref[...],
            ).astype(BF16)
            post_grad_ref[e, here, :] = post_grad
            g_small_ref[1, e : e + 1, :] += column_sum(post_grad.astype(F32))
        for e in range(6):
            act_grad = mm_nt(post_grad_ref[e, here, :], w_out_ref[e])
            pre_grad = (act_grad * slope_ref[e, now, :].astype(F32)).astype(BF16)
            pre_grad_ref[here, spot(e)] = pre_grad
            g_small_ref[0, e : e + 1, :] += column_sum(pre_grad.astype(F32))
        level_grad = mm_nt(pre_grad_ref[here, :], w_in_ref[...]) + mm_nt(
            logit_ref[here, :], gate_ref[...]
        )
        level_grad_ref[here, :] = level_grad
        normed = (masked_ref[now, :].astype(F32) - entry_ref[0:1, :]) * entry_ref[1:2, :]
        g_sum_ref[0:1, :] += column_sum(level_grad * normed)
        g_sum_ref[1:2, :] += column_sum(level_grad)
        return carry

    tiles(tile)(logit_ref.shape[0], body)


def level_one_weights(
    count,
    rows,
    me_ref,
    level_ref,
    active_ref,
    small_ref,
    logit_a_ref,
    logit_b_ref,
    post_a_ref,
    post_b_ref,
    pre_a_ref,
    pre_b_ref,
    *rest,
):
    *grads_refs, flat_ref = rest
    width = level_ref.shape[1]
    lanes = width // LANES
    where_row, used_rows = first_layout(width)
    half = logit_a_ref.shape[0]
    one, two = slice(0, half), slice(half, level_ref.shape[0])
    for e in range(6):
        put_wide_rows(
            flat_ref,
            where_row["expert_in"] + e * 2 * width,
            width,
            mm_tn(level_ref[one, :], pre_a_ref[:, spot(e)])
            + mm_tn(level_ref[two, :], pre_b_ref[:, spot(e)]),
        )
        put_wide_rows(
            flat_ref,
            where_row["expert_out"] + e * 2 * H,
            H,
            mm_tn(active_ref[e, one, :], post_a_ref[e])
            + mm_tn(active_ref[e, two, :], post_b_ref[e]),
        )
    for index, name in enumerate(("expert_in_bias", "expert_out_bias", "norm_gain", "norm_bias")):
        put_wide_rows(flat_ref, where_row[name], 6, small_ref[index, :6, :])
    gate_rows = 14 * width // LANES
    gate = mm_tn(level_ref[one, :], logit_a_ref[...]) + mm_tn(level_ref[two, :], logit_b_ref[...])
    flat_ref[pl.ds(where_row["gate"], gate_rows), :] = rows_from_table(gate, gate_rows, 14)
    flat_ref[0 : 2 * lanes, :] = jnp.zeros((2 * lanes, LANES), F32)
    if used_rows < count * rows:
        flat_ref[pl.ds(used_rows, count * rows - used_rows), :] = jnp.zeros(
            (count * rows - used_rows, LANES), F32
        )
    collect_pieces(me_ref[0], count, rows, flat_ref, grads_refs)


def input_kernel(
    total_rows, grad_a_ref, grad_b_ref, masked_ref, presence_ref, entry_ref, sums_ref, out_ref
):
    width = masked_ref.shape[1]
    mask = spread_presence(presence_ref[...], width)
    inv_scale = entry_ref[1:2, :]
    gain = entry_ref[2:3, :]
    cross = sums_ref[0:1, :] * (1.0 / total_rows)
    plain = sums_ref[1:2, :] * (1.0 / total_rows)
    half = grad_a_ref.shape[0]
    for part, ref in enumerate((grad_a_ref, grad_b_ref)):
        now = slice(part * half, (part + 1) * half)
        normed = (masked_ref[now, :].astype(F32) - entry_ref[0:1, :]) * inv_scale
        out_ref[now, :] = mask[now] * ((inv_scale * gain) * (ref[...] - plain - normed * cross))


def xor_permute(value, axis, bit):
    size = lax.axis_size(axis)
    return lax.ppermute(value, axis, [(index, index ^ bit) for index in range(size)])


def hypercube_ok():
    wide, narrow = lax.axis_size("wide"), lax.axis_size("narrow")
    return wide == 8 and narrow == 4


def after(value, *others):
    return lax.optimization_barrier((value, *others))[0]


def small_kernel(kernel, inputs, out_shape, scalar=False):
    return run_kernel(kernel, inputs, out_shape, [], 8, 2**20, scalar=scalar)


def stack_kernel(*refs):
    sources, targets = refs[:4], refs[4:]
    each = 4 // len(targets)
    for index, ref in enumerate(sources):
        targets[index // each][index % each] = ref[...]


def gather_near(block):
    return [block] + [xor_permute(block, "narrow", k) for k in (1, 2, 3)]


def stack_near(near, parts):
    rows = near[0].shape[0]
    shapes = [jax.ShapeDtypeStruct((4 // parts, rows, LANES), BF16)] * parts
    return small_kernel(stack_kernel, near, shapes)


def gather_halves(first, second):
    first_y, second_x = xor_permute(first, "wide", 4), xor_permute(second, "wide", 2)
    first_x, second_y = xor_permute(first, "wide", 2), xor_permute(second, "wide", 4)
    first_xy, second_xy = xor_permute(first_y, "wide", 2), xor_permute(second_x, "wide", 4)
    own = [first, second, first_x, second_x, first_y, second_y, first_xy, second_xy]
    other = [xor_permute(piece, "wide", 1) for piece in own]
    pieces = []
    for index in range(4):
        pieces += [own[2 * index], own[2 * index + 1], other[2 * index], other[2 * index + 1]]
    return pieces


def gather_plane(stack):
    return [stack] + [xor_permute(stack, "wide", bit) for bit in (2, 4, 6)]


def gather_core(own):
    pieces = []
    for piece in own:
        pieces += [piece, xor_permute(piece, "wide", 1)]
    return pieces


def core_direct_kernel(keep_ref, got_ref, own_ref, *send_refs):
    total = keep_ref[...].astype(F32) + got_ref[...].astype(F32)
    own_ref[...] = total[0:4]
    for part, ref in enumerate(send_refs):
        ref[...] = total[4 * (part + 1) : 4 * (part + 2)].astype(BF16)


def plane_direct_kernel(own_ref, one_ref, two_ref, three_ref, keep_ref, *send_refs):
    total = own_ref[...]
    for ref in (one_ref, two_ref, three_ref):
        total = total + ref[...].astype(F32)
    keep_ref[...] = total[0]
    for part, ref in enumerate(send_refs):
        ref[...] = total[part + 1].astype(BF16)


def last_kernel(own_ref, one_ref, two_ref, three_ref, out_ref):
    total = own_ref[...]
    for ref in (one_ref, two_ref, three_ref):
        total = total + ref[...].astype(F32)
    out_ref[...] = total[: out_ref.shape[0]]


def last_head_kernel(me_ref, sums_ref, own_ref, one_ref, two_ref, three_ref, out_ref):
    last_kernel(own_ref, one_ref, two_ref, three_ref, out_ref)
    put_head(me_ref, sums_ref, out_ref)


def put_head(me_ref, sums_ref, out_ref):
    @pl.when(me_ref[0] == 0)
    def _():
        lanes = sums_ref.shape[1] // LANES
        for index in range(2 * lanes):
            part = slice(index % lanes * LANES, (index % lanes + 1) * LANES)
            row = index // lanes
            out_ref[index : index + 1, :] = sums_ref[row : row + 1, part]


def head_kernel(me_ref, sums_ref, block_ref, out_ref):
    out_ref[...] = block_ref[...]
    put_head(me_ref, sums_ref, out_ref)


def add_kernel(one_ref, two_ref, out_ref):
    out_ref[...] = one_ref[...] + two_ref[...]


def core_halves_kernel(
    keep_ref, got_ref, sums_ref, sums_got_ref, one_ref, two_ref, out_ref, send_one_ref, send_two_ref
):
    total = keep_ref[...].astype(F32) + got_ref[...].astype(F32)
    for x in range(2):
        for z in range(2):
            one_ref[2 * x + z] = total[4 * x + z]
            send_one_ref[2 * x + z] = total[8 + 4 * x + z].astype(BF16)
    for y in range(2):
        for z in range(2):
            two_ref[2 * y + z] = total[8 * y + 2 + z]
            send_two_ref[2 * y + z] = total[8 * y + 4 + 2 + z].astype(BF16)
    out_ref[...] = sums_ref[...] + sums_got_ref[...]


def plane_halves_kernel(
    one_ref,
    two_ref,
    got_one_ref,
    got_two_ref,
    sums_ref,
    sums_got_ref,
    keep_one_ref,
    keep_two_ref,
    out_ref,
    send_one_ref,
    send_two_ref,
):
    for ref, got, keep, send in (
        (one_ref, got_one_ref, keep_one_ref, send_one_ref),
        (two_ref, got_two_ref, keep_two_ref, send_two_ref),
    ):
        total = ref[...] + got[...].astype(F32)
        keep[...] = total[0:2]
        send[...] = total[2:4].astype(BF16)
    out_ref[...] = sums_ref[...] + sums_got_ref[...]


def near_halves_kernel(
    one_ref, two_ref, got_one_ref, got_two_ref, keep_ref, send_one_ref, send_two_ref, send_three_ref
):
    one = one_ref[...] + got_one_ref[...].astype(F32)
    two = two_ref[...] + got_two_ref[...].astype(F32)
    keep_ref[...] = one[0]
    send_one_ref[...] = one[1].astype(BF16)
    send_two_ref[...] = two[0].astype(BF16)
    send_three_ref[...] = two[1].astype(BF16)


def add_four_kernel(one_ref, two_ref, three_ref, four_ref, out_ref):
    out_ref[...] = (one_ref[...] + two_ref[...]) + (three_ref[...] + four_ref[...])


def scatter_plain(value):
    return lax.psum_scatter(value.astype(F32), AXES, scatter_dimension=0, tiled=True)[0]


def per_device(features, presence, first_params, second_params, cotangent):
    rows, width = features.shape
    lanes = width // LANES
    devices_all = count = lax.axis_size(AXES)
    total_rows = rows * devices_all
    cube = hypercube_ok()
    tile = math.gcd(rows, 256)
    half = rows // 2
    me = lax.axis_index(AXES).astype(jnp.int32).reshape(1)
    chunks = [first_params.shape[0] // LANES, second_params.shape[0] // LANES]
    extra = 6 * lanes
    shape = jax.ShapeDtypeStruct
    fields = presence.T
    blocks = [up(chunks[0], 16), up(chunks[1], 16)]

    masked, block_one, block_two = run_kernel(
        stats_kernel,
        [
            me,
            features,
            fields,
            first_params.reshape(chunks[0], LANES),
            second_params.reshape(chunks[1], LANES),
        ],
        (
            shape((rows, width), BF16),
            shape((up(chunks[0] + extra, 16), LANES), BF16),
            shape((blocks[1], LANES), BF16),
        ),
        [],
        8,
        rows * width * 10,
    )
    if cube:
        origin = me
        near_one = gather_near(block_one)
        first, second = stack_near(near_one, 2)
        near_two = gather_near(after(block_two, first))
        pieces_one = gather_halves(first, second)
        (stack_two,) = stack_near(near_two, 1)
        plane_two = gather_plane(after(stack_two, pieces_one[12], pieces_one[13]))
        masked = after(masked, stack_two)
    else:
        origin = jnp.zeros((1,), jnp.int32)
        pieces_one = [lax.all_gather(block_one, AXES)]
        plane_two = [lax.all_gather(block_two, AXES)]

    saved = run_kernel(
        functools.partial(level_one_forward, chunks[0], tile, len(pieces_one)),
        [origin, masked] + pieces_one,
        [
            shape((rows, width), BF16),
            shape((6, rows, H), BF16),
            shape((6, rows, H), BF16),
            shape((6, rows, H), BF16),
            shape((6, rows, LANES), F32),
            shape((rows, LANES), F32),
            shape((3, rows, H), BF16),
            shape((width, 6 * H), BF16),
            shape((6, H, H), BF16),
            shape((4, 8, H), F32),
            shape((width, LANES), BF16),
            shape((8, width), F32),
        ],
        [
            pltpu.VMEM((count * chunks[0], LANES), F32),
            pltpu.VMEM((count, extra, LANES), F32),
            pltpu.VMEM((6, tile, H), F32),
            pltpu.VMEM((tile, 14 * LANES), F32),
            pltpu.VMEM((2 * LANES, 14 * LANES), BF16),
        ],
        20,
        rows * 6 * (width + H) * H * 2,
    )
    level, active, slope, normal, scale, probs, mixed, w_in, w_out, small, gate, entry = saved
    pieces_two = gather_core([after(piece, entry) for piece in plane_two]) if cube else plane_two

    outs = 2 if cube else 1
    towers, mixed_grad, *grads_two = run_kernel(
        functools.partial(level_two, count, chunks[1], tile, len(pieces_two), outs),
        [origin, mixed, cotangent] + pieces_two,
        [
            shape((rows, LANES), F32),
            shape((3, rows, H), F32),
        ]
        + [shape((count // outs, blocks[1], LANES), BF16)] * outs,
        [
            pltpu.VMEM((count * chunks[1], LANES), F32),
            pltpu.VMEM((H, 6 * H), BF16),
            pltpu.VMEM((6, H, H), BF16),
            pltpu.VMEM((4, 8, H), F32),
            pltpu.VMEM((H, LANES), BF16),
            pltpu.VMEM((2, H, TOWER1), BF16),
            pltpu.VMEM((2 * TOWER1, LANES), BF16),
            pltpu.VMEM((2 * TOWER1, LANES), F32),
            pltpu.VMEM((8, 2 * TOWER1), F32),
            pltpu.VMEM((4, 8, H), F32),
            pltpu.VMEM((2 * TOWER1, LANES), F32),
            pltpu.VMEM((8, 2 * TOWER1), F32),
            pltpu.VMEM((6, rows, H), BF16),
            pltpu.VMEM((tile, 6 * H), F32),
            pltpu.VMEM((6, tile, H), F32),
            pltpu.VMEM((6, tile, LANES), F32),
            pltpu.VMEM((6, tile, H), F32),
            pltpu.VMEM((2, rows, H), BF16),
            pltpu.VMEM((2, tile, H), F32),
            pltpu.VMEM((rows, 2 * TOWER1), BF16),
            pltpu.VMEM((rows, 2 * TOWER1), BF16),
            pltpu.VMEM((2, rows, LANES), BF16),
            pltpu.VMEM((6, rows, H), BF16),
            pltpu.VMEM((rows, 6 * H), BF16),
            pltpu.VMEM((tile, 8 * LANES), F32),
            pltpu.VMEM((2 * LANES, 8 * LANES), BF16),
            pltpu.VMEM((2 * H, 2 * LANES), BF16),
        ],
        32,
        rows * 6 * 2 * H * H * 2 * 3,
    )
    if cube:
        keep_two, send_two = grads_two
        own_two, *sends_two = small_kernel(
            core_direct_kernel,
            [keep_two, xor_permute(send_two, "wide", 1)],
            [shape((4, blocks[1], LANES), F32)] + [shape((4, blocks[1], LANES), BF16)] * 3,
        )

    def backward(part, *before):
        return run_kernel(
            functools.partial(level_one_backward, min(tile, half), part * half),
            [
                mixed_grad,
                masked,
                slope,
                normal,
                scale,
                probs,
                w_in,
                w_out,
                small,
                gate,
                entry if part == 0 or not cube else after(entry, own_two),
                *before,
            ],
            [
                shape((half, width), F32),
                shape((8, width), F32),
                shape((4, 8, H), F32),
                shape((half, LANES), BF16),
                shape((6, half, H), BF16),
                shape((half, 6 * H), BF16),
            ],
            [
                pltpu.VMEM((min(tile, half), 14 * LANES), F32),
                pltpu.VMEM((2 * LANES, 14 * LANES), BF16),
                pltpu.VMEM((2 * H, 2 * LANES), BF16),
            ],
            12,
            rows * 6 * (width + H) * H * 2,
            scalar=False,
        )

    grad_a, sums, g_small, logit_a, post_a, pre_a = backward(0)
    grad_b, sums, g_small, logit_b, post_b, pre_b = backward(1, sums, g_small)
    grads_one = run_kernel(
        functools.partial(level_one_weights, count, chunks[0]),
        [
            origin,
            level,
            active,
            g_small,
            logit_a,
            logit_b,
            post_a,
            post_b,
            pre_a,
            pre_b,
        ],
        [shape((count // outs, blocks[0], LANES), BF16)] * outs,
        [pltpu.VMEM((count * chunks[0], LANES), F32)],
        12,
        rows * 6 * (width + H) * H * 2,
    )
    if cube:
        low, high = shape((4, blocks[0], LANES), BF16), shape((4, blocks[0], LANES), F32)
        summed = shape((8, width), F32)
        keep, send = grads_one
        sums = small_kernel(
            add_kernel, [sums, after(xor_permute(sums, "wide", 1), send)], summed
        )
        keep_two, *sends_two = small_kernel(
            plane_direct_kernel,
            [own_two]
            + [xor_permute(part, "wide", bit) for part, bit in zip(sends_two, (2, 4, 6))],
            [shape((blocks[1], LANES), F32)] + [shape((blocks[1], LANES), BF16)] * 3,
        )
        one, two, sums, send_one, send_two = small_kernel(
            core_halves_kernel,
            [after(keep, keep_two), xor_permute(send, "wide", 1), sums, xor_permute(sums, "wide", 4)],
            [high, high, summed, low, low],
        )
        low, high = shape((2, blocks[0], LANES), BF16), shape((2, blocks[0], LANES), F32)
        one, two, sums, send_one, send_two = small_kernel(
            plane_halves_kernel,
            [
                one,
                two,
                xor_permute(send_one, "wide", 4),
                xor_permute(send_two, "wide", 2),
                sums,
                xor_permute(sums, "wide", 2),
            ],
            [high, high, summed, low, low],
        )
        low, high = shape((blocks[0], LANES), BF16), shape((blocks[0], LANES), F32)
        keep, *sends = small_kernel(
            near_halves_kernel,
            [one, two, xor_permute(send_one, "wide", 2), xor_permute(send_two, "wide", 4)],
            [high, low, low, low],
        )
        sums = small_kernel(
            add_four_kernel,
            [sums] + [xor_permute(sums, "narrow", k) for k in (1, 2, 3)],
            summed,
        )
        second_grad = small_kernel(
            last_kernel,
            [keep_two]
            + [xor_permute(part, "narrow", k) for part, k in zip(sends_two, (1, 2, 3))],
            shape((chunks[1], LANES), F32),
        )
        first_grad = small_kernel(
            last_head_kernel,
            [me, sums, keep]
            + [xor_permute(part, "narrow", k) for part, k in zip(sends, (1, 2, 3))],
            shape((chunks[0], LANES), F32),
            scalar=True,
        )
    else:
        sums = lax.psum(sums, AXES)
        second_grad = scatter_plain(grads_two[0])[: chunks[1]]
        first_grad = small_kernel(
            head_kernel,
            [me, sums, scatter_plain(grads_one[0])[: chunks[0]]],
            shape((chunks[0], LANES), F32),
            scalar=True,
        )

    input_grad = run_kernel(
        functools.partial(input_kernel, float(total_rows)),
        [grad_a, grad_b, masked, fields, entry, sums],
        shape((rows, width), F32),
        [],
        8,
        rows * width * 10,
        scalar=False,
    )
    return (towers, input_grad, first_grad.reshape(-1), second_grad.reshape(-1))


def solution(mesh):
    placed = (
        P(AXES, None),
        P(AXES, None),
        P(AXES),
        P(AXES),
        P(AXES, None),
    )
    return jax.shard_map(
        per_device,
        mesh=mesh,
        in_specs=placed,
        out_specs=(P(AXES, None), P(AXES, None), P(AXES), P(AXES)),
        check_vma=False,
    )
```

time: 196 us -> 140 us (0.71)
  Pallas kernels: 81.9 us -> 49.5 us
  starting transfers between devices: 53.7 us -> 46 us
  waiting for transfers between devices: 46.1 us -> 39.6 us
  local copies, waits for them, and re-layouts: 8.48 us -> 3.68 us
  other arithmetic: 4.45 us -> 0 us
    pallas_call x5 -> x18, Pallas kernels: 81.9 us -> 49.5 us  [run_kernel(): pl.pallas_call(kernel, in_specs=specs, out_specs=out_specs, out_shape=out...]
    ppermute x60 -> x48, starting transfers between devices: 53.7 us -> 46 us  [xor_permute(): lax.ppermute(value, axis, [(index, index ^ bit) for index in range(size)])]
    ppermute x60 -> x48, waiting for transfers between devices: 46.1 us -> 39.6 us  [xor_permute(): lax.ppermute(value, axis, [(index, index ^ bit) for index in range(size)])]
    squeeze x7 -> x0, local copies, waits for them, and re-layouts: 5.27 us -> none  [the longest x2 3.81 us: scatter_pieces(): split[:, :, 1]]
  transfers between devices with their start and end apart: 60 -> 48, of which waited for: 26 -> 23; matrix products, arithmetic and copies ran while one was open for 3% -> 0% of each run, Pallas kernels for 25% -> 13%
where the time goes in v2:
time: 140 us
  Pallas kernels  49.5 us (35%)
  starting transfers between devices  46 us (33%)
  waiting for transfers between devices  39.6 us (28%)
  local copies, waits for them, and re-layouts  3.68 us (3%)
    pallas_call x18, Pallas kernels, run_kernel(): pl.pallas_call(kernel, in_specs=specs, out_specs=out_specs, out_shape=out...  49.5 us
    ppermute x48, starting transfers between devices, xor_permute(): lax.ppermute(value, axis, [(index, index ^ bit) for index in range(size)])  46 us
    ppermute x48, waiting for transfers between devices, xor_permute(): lax.ppermute(value, axis, [(index, index ^ bit) for index in range(size)])  39.6 us
    unnamed x12, local copies, waits for them, and re-layouts  3.68 us
  transfers between devices with their start and end apart: 48, of which 23 were waited for; matrix products, arithmetic and copies ran while one was open for 0% of the time, Pallas kernels for 13%

profile of v2, /device:TPU:0, one launch (start us, length us, event | category | flops | bytes accessed | tf_op | source)
XLA Modules:
  0.0 139.6 jit_solution(5399304044102772339)
XLA Ops:
  5.1 5.1 %collective-permute-start.2 = (bf16[320,128]{1,0:T(8,128)(2,1)S(1)}, bf16[320,128]{1,0:T(8,128)(2,1)S(1)}, u32[]{:S(2)}, u32[]{:S(2)}) collective-permute-start(bf16[320,128]{1,0:T(8,128)(2,1)S(1)} %get-tuple-element.73.refs_0_), channel_id=1, source_target_pairs={{0,3},{1,2},{2,1},{3,0},{4,7},{5,6},{6,5},{7,4},{8,11},{9,10},{10,... | collective-permute-start | bytes 245768 | tf_op jit(solution)/shard_map/ppermute | solution.py:774
  10.9 2.4 %collective-permute-done.2.refs_3_ = bf16[320,128]{1,0:T(8,128)(2,1)S(1)} collective-permute-done((bf16[320,128]{1,0:T(8,128)(2,1)S(1)}, bf16[320,128]{1,0:T(8,128)(2,1)S(1)}, u32[]{:S(2)}, u32[]{:S(2)}) %collective-permute-start.2) | collective-permute-done | bytes 81952 | tf_op jit(solution)/shard_map/ppermute | solution.py:774
  13.3 3.8 %collective-permute-done.1.refs_2_ = bf16[320,128]{1,0:T(8,128)(2,1)S(1)} collective-permute-done((bf16[320,128]{1,0:T(8,128)(2,1)S(1)}, bf16[320,128]{1,0:T(8,128)(2,1)S(1)}, u32[]{:S(2)}, u32[]{:S(2)}) %collective-permute-start.1) | collective-permute-done | bytes 81952 | tf_op jit(solution)/shard_map/ppermute | solution.py:774
  17.1 1.6 %collective-permute-start.9 = (bf16[2,320,128]{2,1,0:T(8,128)(2,1)S(1)}, bf16[2,320,128]{2,1,0:T(8,128)(2,1)S(1)}, u32[]{:S(2)}, u32[]{:S(2)}) collective-permute-start(bf16[2,320,128]{2,1,0:T(8,128)(2,1)S(1)} %get-tuple-element.77.rest_1_), channel_id=1, source_target_pairs={{0,8},{4,12},{8,0},{12,4},{16,24},{20,28},{24,16},{28,20},{1,9},{5... | collective-permute-start | bytes 491528 | tf_op jit(solution)/shard_map/ppermute | solution.py:774
  18.7 1.5 %collective-permute-start.12 = (bf16[2,320,128]{2,1,0:T(8,128)(2,1)S(1)}, bf16[2,320,128]{2,1,0:T(8,128)(2,1)S(1)}, u32[]{:S(2)}, u32[]{:S(2)}) collective-permute-start(bf16[2,320,128]{2,1,0:T(8,128)(2,1)S(1)} %get-tuple-element.74.rest_0_), channel_id=1, source_target_pairs={{0,16},{4,20},{8,24},{12,28},{16,0},{20,4},{24,8},{28,12},{1,17},{... | collective-permute-start | bytes 491528 | tf_op jit(solution)/shard_map/ppermute | solution.py:774
  20.2 2.7 %collective-permute-start.5 = (bf16[224,128]{1,0:T(8,128)(2,1)S(1)}, bf16[224,128]{1,0:T(8,128)(2,1)S(1)}, u32[]{:S(2)}, u32[]{:S(2)}) collective-permute-start(bf16[224,128]{1,0:T(8,128)(2,1)S(1)} %get-tuple-element.75.refs_0_), channel_id=1, source_target_pairs={{0,3},{1,2},{2,1},{3,0},{4,7},{5,6},{6,5},{7,4},{8,11},{9,10},{10,... | collective-permute-start | bytes 172040 | tf_op jit(solution)/shard_map/ppermute | solution.py:774
  22.9 1.7 %collective-permute-start.3 = (bf16[224,128]{1,0:T(8,128)(2,1)S(1)}, bf16[224,128]{1,0:T(8,128)(2,1)S(1)}, u32[]{:S(2)}, u32[]{:S(2)}) collective-permute-start(bf16[224,128]{1,0:T(8,128)(2,1)S(1)} %get-tuple-element.75.refs_0_), channel_id=1, source_target_pairs={{0,1},{1,0},{2,3},{3,2},{4,5},{5,4},{6,7},{7,6},{8,9},{9,8},{10,11... | collective-permute-start | bytes 172040 | tf_op jit(solution)/shard_map/ppermute | solution.py:774
  24.6 2.0 %collective-permute-done.5.refs_3_ = bf16[224,128]{1,0:T(8,128)(2,1)S(1)} collective-permute-done((bf16[224,128]{1,0:T(8,128)(2,1)S(1)}, bf16[224,128]{1,0:T(8,128)(2,1)S(1)}, u32[]{:S(2)}, u32[]{:S(2)}) %collective-permute-start.5) | collective-permute-done | bytes 57376 | tf_op jit(solution)/shard_map/ppermute | solution.py:774
  29.2 1.5 %collective-permute-start.16 = (bf16[2,320,128]{2,1,0:T(8,128)(2,1)S(1)}, bf16[2,320,128]{2,1,0:T(8,128)(2,1)S(1)}, u32[]{:S(2)}, u32[]{:S(2)}) collective-permute-start(bf16[2,320,128]{2,1,0:T(8,128)(2,1)S(1)} %collective-permute-done.12.rest_8_), channel_id=1, source_target_pairs={{0,8},{4,12},{8,0},{12,4},{16,24},{20,28},{24,16},{28,20},{1,9},{5... | collective-permute-start | bytes 491528 | tf_op jit(solution)/shard_map/ppermute | solution.py:774
  30.7 1.7 %collective-permute-done.13.rest_9_ = bf16[2,320,128]{2,1,0:T(8,128)(2,1)S(1)} collective-permute-done((bf16[2,320,128]{2,1,0:T(8,128)(2,1)S(1)}, bf16[2,320,128]{2,1,0:T(8,128)(2,1)S(1)}, u32[]{:S(2)}, u32[]{:S(2)}) %collective-permute-start.13) | collective-permute-done | bytes 163872 | tf_op jit(solution)/shard_map/ppermute | solution.py:774
  33.0 2.0 %collective-permute-done.8.rest_4_ = bf16[2,320,128]{2,1,0:T(8,128)(2,1)S(1)} collective-permute-done((bf16[2,320,128]{2,1,0:T(8,128)(2,1)S(1)}, bf16[2,320,128]{2,1,0:T(8,128)(2,1)S(1)}, u32[]{:S(2)}, u32[]{:S(2)}) %collective-permute-start.8) | collective-permute-done | bytes 163872 | tf_op jit(solution)/shard_map/ppermute | solution.py:774
  35.5 2.6 %collective-permute-done.16.rest_12_ = bf16[2,320,128]{2,1,0:T(8,128)(2,1)S(1)} collective-permute-done((bf16[2,320,128]{2,1,0:T(8,128)(2,1)S(1)}, bf16[2,320,128]{2,1,0:T(8,128)(2,1)S(1)}, u32[]{:S(2)}, u32[]{:S(2)}) %collective-permute-start.16) | collective-permute-done | bytes 163872 | tf_op jit(solution)/shard_map/ppermute | solution.py:774
  38.8 1.4 collective-permute-start.23
  40.2 1.5 %collective-permute-start.21 = (bf16[4,224,128]{2,1,0:T(8,128)(2,1)S(1)}, bf16[4,224,128]{2,1,0:T(8,128)(2,1)S(1)}, u32[]{:S(2)}, u32[]{:S(2)}) collective-permute-start(bf16[4,224,128]{2,1,0:T(8,128)(2,1)S(1)} %shard_map.86.rest_0_), channel_id=1, source_target_pairs={{0,8},{4,12},{8,0},{12,4},{16,24},{20,28},{24,16},{28,20},{1,9},{5... | collective-permute-start | bytes 688136 | tf_op jit(solution)/shard_map/ppermute | solution.py:774
  43.3 9.2 %shard_map.87 = (bf16[1024,512]{1,0:T(8,128)(2,1)S(1)}, bf16[6,1024,256]{2,1,0:T(8,128)(2,1)S(1)}, bf16[6,1024,256]{2,1,0:T(8,128)(2,1)S(1)}, bf16[6,1024,256]{2...) custom-call(s32[1]{0:T(128)} %bitcast.me_ref, ...), custom_call_target="tpu_custom_call" | custom-call | flops 1048576 | bytes 1024 | tf_op jit(solution)/shard_map/pallas_call | solution.py:260
  55.1 20.3 %shard_map.88 = (f32[1024,128]{1,0:T(8,128)}, f32[3,1024,256]{2,1,0:T(8,128)S(1)}, bf16[16,224,128]{2,1,0:T(8,128)(2,1)S(1)}, bf16[16,224,128]{2,1,0:T(8,128)(2,1)S(1)}) custom-call(s32[1]{0:T(128)} %bitcast.me_ref, bf16[3,1024,256]{2,1,0:T(8,128)(2,1)S(1)} %get-tuple-element.78.mixed_ref, bf16[1024,128]{1,0:T(8,128)(2,1)S(1)} %copy-done.1, ...), custom_call_target="tpu_custom_call" | custom-call | flops 1048576 | bytes 1024 | tf_op jit(solution)/shard_map/pallas_call | solution.py:260
  75.6 5.6 %shard_map.89 = (f32[512,512]{1,0:T(8,128)S(1)}, f32[8,512]{1,0:T(8,128)S(1)}, f32[4,8,256]{2,1,0:T(8,128)S(1)}, bf16[512,128]{1,0:T(8,128)(2,1)S(1)}, bf16[6,51...) custom-call(f32[3,1024,256]{2,1,0:T(8,128)S(1)} %get-tuple-element.86.mixed_grad_ref, ...), custom_call_target="tpu_custom_call" | custom-call | flops 1048576 | bytes 1024 | tf_op jit(solution)/shard_map/pallas_call | solution.py:260
  81.5 5.4 %shard_map.91 = (f32[512,512]{1,0:T(8,128)S(1)}, f32[8,512]{1,0:T(8,128)S(1)}, f32[4,8,256]{2,1,0:T(8,128)S(1)}, bf16[512,128]{1,0:T(8,128)(2,1)S(1)}, bf16[6,51...) custom-call(f32[3,1024,256]{2,1,0:T(8,128)S(1)} %get-tuple-element.86.mixed_grad_ref, ...), custom_call_target="tpu_custom_call" | custom-call | flops 1048576 | bytes 1024 | tf_op jit(solution)/shard_map/pallas_call | solution.py:260
  86.9 4.0 %shard_map.92 = (bf16[16,304,128]{2,1,0:T(8,128)(2,1)S(1)}, bf16[16,304,128]{2,1,0:T(8,128)(2,1)S(1)}) custom-call(s32[1]{0:T(128)} %bitcast.me_ref, bf16[1024,512]{1,0:T(8,128)(2,1)S(1)} %get-tuple-element.103.level_ref, bf16[6,1024,256]{2,1,0:T(8,128)(2,1)S(1)} %get-tuple-element.104.active_ref, f32[4,8,256]{2,1,0:T(8,128)S(1)} %get-tuple-element.105.small_ref, ...), custom_call_target="tpu_custom_call" | custom-call | flops 1048576 | bytes 1024 | tf_op jit(solution)/shard_map/pallas_call | solution.py:260
  92.4 2.3 %collective-permute-start.30 = (bf16[4,224,128]{2,1,0:T(8,128)(2,1)S(1)}, bf16[4,224,128]{2,1,0:T(8,128)(2,1)S(1)}, u32[]{:S(2)}, u32[]{:S(2)}) collective-permute-start(bf16[4,224,128]{2,1,0:T(8,128)(2,1)S(1)} %get-tuple-element.115), channel_id=1, source_target_pairs={{0,24},{4,28},{8,16},{12,20},{16,8},{20,12},{24,0},{28,4},{1,25},{... | collective-permute-start | bytes 688136 | tf_op jit(solution)/shard_map/ppermute | solution.py:774
  96.5 3.1 %collective-permute-done.28.one_ref = bf16[4,224,128]{2,1,0:T(8,128)(2,1)S(1)} collective-permute-done((bf16[4,224,128]{2,1,0:T(8,128)(2,1)S(1)}, bf16[4,224,128]{2,1,0:T(8,128)(2,1)S(1)}, u32[]{:S(2)}, u32[]{:S(2)}) %collective-permute-start.28) | collective-permute-done | bytes 229408 | tf_op jit(solution)/shard_map/ppermute | solution.py:774
  99.6 4.7 %collective-permute-done.29.two_ref = bf16[4,224,128]{2,1,0:T(8,128)(2,1)S(1)} collective-permute-done((bf16[4,224,128]{2,1,0:T(8,128)(2,1)S(1)}, bf16[4,224,128]{2,1,0:T(8,128)(2,1)S(1)}, u32[]{:S(2)}, u32[]{:S(2)}) %collective-permute-start.29) | collective-permute-done | bytes 229408 | tf_op jit(solution)/shard_map/ppermute | solution.py:774
  107.8 6.7 %collective-permute-done.36.sums_got_ref = f32[8,512]{1,0:T(8,128)S(1)} collective-permute-done((f32[8,512]{1,0:T(8,128)S(1)}, f32[8,512]{1,0:T(8,128)S(1)}, u32[]{:S(2)}, u32[]{:S(2)}) %collective-permute-start.36) | collective-permute-done | bytes 16416 | tf_op jit(solution)/shard_map/ppermute | solution.py:774
  115.4 1.6 %collective-permute-start.41 = (bf16[2,304,128]{2,1,0:T(8,128)(2,1)S(1)}, bf16[2,304,128]{2,1,0:T(8,128)(2,1)S(1)}, u32[]{:S(2)}, u32[]{:S(2)}) collective-permute-start(bf16[2,304,128]{2,1,0:T(8,128)(2,1)S(1)} %get-tuple-element.130), channel_id=1, source_target_pairs={{0,16},{4,20},{8,24},{12,28},{16,0},{20,4},{24,8},{28,12},{1,17},{... | collective-permute-start | bytes 466952 | tf_op jit(solution)/shard_map/ppermute | solution.py:774
  117.0 2.7 %collective-permute-start.46 = (bf16[224,128]{1,0:T(8,128)(2,1)S(1)}, bf16[224,128]{1,0:T(8,128)(2,1)S(1)}, u32[]{:S(2)}, u32[]{:S(2)}) collective-permute-start(bf16[224,128]{1,0:T(8,128)(2,1)S(1)} %get-tuple-element.136), channel_id=1, source_target_pairs={{0,2},{1,3},{2,0},{3,1},{4,6},{5,7},{6,4},{7,5},{8,10},{9,11},{10,... | collective-permute-start | bytes 172040 | tf_op jit(solution)/shard_map/ppermute | solution.py:774
  121.3 2.2 %collective-permute-start.43 = (bf16[304,128]{1,0:T(8,128)(2,1)S(1)}, bf16[304,128]{1,0:T(8,128)(2,1)S(1)}, u32[]{:S(2)}, u32[]{:S(2)}) collective-permute-start(bf16[304,128]{1,0:T(8,128)(2,1)S(1)} %get-tuple-element.133), channel_id=1, source_target_pairs={{0,2},{1,3},{2,0},{3,1},{4,6},{5,7},{6,4},{7,5},{8,10},{9,11},{10,... | collective-permute-start | bytes 233480 | tf_op jit(solution)/shard_map/ppermute | solution.py:774
  123.4 1.7 %collective-permute-start.44 = (bf16[304,128]{1,0:T(8,128)(2,1)S(1)}, bf16[304,128]{1,0:T(8,128)(2,1)S(1)}, u32[]{:S(2)}, u32[]{:S(2)}) collective-permute-start(bf16[304,128]{1,0:T(8,128)(2,1)S(1)} %get-tuple-element.134), channel_id=1, source_target_pairs={{0,3},{1,2},{2,1},{3,0},{4,7},{5,6},{6,5},{7,4},{8,11},{9,10},{10,... | collective-permute-start | bytes 233480 | tf_op jit(solution)/shard_map/ppermute | solution.py:774
  125.2 2.1 %collective-permute-start.47 = (bf16[224,128]{1,0:T(8,128)(2,1)S(1)}, bf16[224,128]{1,0:T(8,128)(2,1)S(1)}, u32[]{:S(2)}, u32[]{:S(2)}) collective-permute-start(bf16[224,128]{1,0:T(8,128)(2,1)S(1)} %get-tuple-element.137), channel_id=1, source_target_pairs={{0,3},{1,2},{2,1},{3,0},{4,7},{5,6},{6,5},{7,4},{8,11},{9,10},{10,... | collective-permute-start | bytes 172040 | tf_op jit(solution)/shard_map/ppermute | solution.py:774
  127.3 1.7 %collective-permute-start.39 = (f32[8,512]{1,0:T(8,128)S(1)}, f32[8,512]{1,0:T(8,128)S(1)}, u32[]{:S(2)}, u32[]{:S(2)}) collective-permute-start(f32[8,512]{1,0:T(8,128)S(1)} %get-tuple-element.126.one_ref), channel_id=1, source_target_pairs={{0,3},{1,2},{2,1},{3,0},{4,7},{5,6},{6,5},{7,4},{8,11},{9,10},{10,... | collective-permute-start | bytes 49160 | tf_op jit(solution)/shard_map/ppermute | solution.py:774
  129.0 2.3 %collective-permute-done.47.three_ref = bf16[224,128]{1,0:T(8,128)(2,1)S(1)} collective-permute-done((bf16[224,128]{1,0:T(8,128)(2,1)S(1)}, bf16[224,128]{1,0:T(8,128)(2,1)S(1)}, u32[]{:S(2)}, u32[]{:S(2)}) %collective-permute-start.47) | collective-permute-done | bytes 57376 | tf_op jit(solution)/shard_map/ppermute | solution.py:774
  131.2 1.9 %collective-permute-start.38 = (f32[8,512]{1,0:T(8,128)S(1)}, f32[8,512]{1,0:T(8,128)S(1)}, u32[]{:S(2)}, u32[]{:S(2)}) collective-permute-start(f32[8,512]{1,0:T(8,128)S(1)} %get-tuple-element.126.one_ref), channel_id=1, source_target_pairs={{0,2},{1,3},{2,0},{3,1},{4,6},{5,7},{6,4},{7,5},{8,10},{9,11},{10,... | collective-permute-start | bytes 49160 | tf_op jit(solution)/shard_map/ppermute | solution.py:774
  136.8 2.0 %shard_map.98 = f32[1024,512]{1,0:T(8,128)} custom-call(f32[512,512]{1,0:T(8,128)S(1)} %get-tuple-element.95.grad_a_ref, f32[512,512]{1,0:T(8,128)S(1)} %get-tuple-element.102.grad_b_ref, bf16[1024,512]{1,0:T(8,128)(2,1)S(1)} %get-tuple-element.76.masked_ref, s32[8,1024]{1,0:T(8,128)S(1)} %bitcast.7, f32[8,512]{1,0:T(8,128)S(1)} %get-tuple-element.99.entry_ref, ...), custom_call_target="tpu_custom_call" | custom-call | flops 1048576 | bytes 1024 | tf_op jit(solution)/shard_map/pallas_call | solution.py:260
  (94 shorter events, 27.8 us)
Async XLA Ops:
  5.1 8.1 %collective-permute-start.2 = (bf16[320,128]{1,0:T(8,128)(2,1)S(1)}, bf16[320,128]{1,0:T(8,128)(2,1)S(1)}, u32[]{:S(2)}, u32[]{:S(2)}) collective-permute-start(bf16[320,128]{1,0:T(8,128)(2,1)S(1)} %get-tuple-element.73.refs_0_), channel_id=1, source_target_pairs={{0,3},{1,2},{2,1},{3,0},{4,7},{5,6},{6,5},{7,4},{8,11},{9,10},{10,... | collective-permute-start | bytes 245768 | tf_op jit(solution)/shard_map/ppermute | solution.py:774
  10.2 6.9 %collective-permute-start.1 = (bf16[320,128]{1,0:T(8,128)(2,1)S(1)}, bf16[320,128]{1,0:T(8,128)(2,1)S(1)}, u32[]{:S(2)}, u32[]{:S(2)}) collective-permute-start(bf16[320,128]{1,0:T(8,128)(2,1)S(1)} %get-tuple-element.73.refs_0_), channel_id=1, source_target_pairs={{0,2},{1,3},{2,0},{3,1},{4,6},{5,7},{6,4},{7,5},{8,10},{9,11},{10,... | collective-permute-start | bytes 245768 | tf_op jit(solution)/shard_map/ppermute | solution.py:774
  10.2 6.9 %collective-permute-start = (bf16[320,128]{1,0:T(8,128)(2,1)S(1)}, bf16[320,128]{1,0:T(8,128)(2,1)S(1)}, u32[]{:S(2)}, u32[]{:S(2)}) collective-permute-start(bf16[320,128]{1,0:T(8,128)(2,1)S(1)} %get-tuple-element.73.refs_0_), channel_id=1, source_target_pairs={{0,1},{1,0},{2,3},{3,2},{4,5},{5,4},{6,7},{7,6},{8,9},{9,8},{10,11... | collective-permute-start | bytes 245768 | tf_op jit(solution)/shard_map/ppermute | solution.py:774
  17.1 11.4 %collective-permute-start.9 = (bf16[2,320,128]{2,1,0:T(8,128)(2,1)S(1)}, bf16[2,320,128]{2,1,0:T(8,128)(2,1)S(1)}, u32[]{:S(2)}, u32[]{:S(2)}) collective-permute-start(bf16[2,320,128]{2,1,0:T(8,128)(2,1)S(1)} %get-tuple-element.77.rest_1_), channel_id=1, source_target_pairs={{0,8},{4,12},{8,0},{12,4},{16,24},{20,28},{24,16},{28,20},{1,9},{5... | collective-permute-start | bytes 491528 | tf_op jit(solution)/shard_map/ppermute | solution.py:774
  18.7 10.6 %collective-permute-start.12 = (bf16[2,320,128]{2,1,0:T(8,128)(2,1)S(1)}, bf16[2,320,128]{2,1,0:T(8,128)(2,1)S(1)}, u32[]{:S(2)}, u32[]{:S(2)}) collective-permute-start(bf16[2,320,128]{2,1,0:T(8,128)(2,1)S(1)} %get-tuple-element.74.rest_0_), channel_id=1, source_target_pairs={{0,16},{4,20},{8,24},{12,28},{16,0},{20,4},{24,8},{28,12},{1,17},{... | collective-permute-start | bytes 491528 | tf_op jit(solution)/shard_map/ppermute | solution.py:774
  20.2 6.4 %collective-permute-start.5 = (bf16[224,128]{1,0:T(8,128)(2,1)S(1)}, bf16[224,128]{1,0:T(8,128)(2,1)S(1)}, u32[]{:S(2)}, u32[]{:S(2)}) collective-permute-start(bf16[224,128]{1,0:T(8,128)(2,1)S(1)} %get-tuple-element.75.refs_0_), channel_id=1, source_target_pairs={{0,3},{1,2},{2,1},{3,0},{4,7},{5,6},{6,5},{7,4},{8,11},{9,10},{10,... | collective-permute-start | bytes 172040 | tf_op jit(solution)/shard_map/ppermute | solution.py:774
  26.6 5.9 %collective-permute-start.13 = (bf16[2,320,128]{2,1,0:T(8,128)(2,1)S(1)}, bf16[2,320,128]{2,1,0:T(8,128)(2,1)S(1)}, u32[]{:S(2)}, u32[]{:S(2)}) collective-permute-start(bf16[2,320,128]{2,1,0:T(8,128)(2,1)S(1)} %get-tuple-element.77.rest_1_), channel_id=1, source_target_pairs={{0,16},{4,20},{8,24},{12,28},{16,0},{20,4},{24,8},{28,12},{1,17},{... | collective-permute-start | bytes 491528 | tf_op jit(solution)/shard_map/ppermute | solution.py:774
  28.0 7.0 %collective-permute-start.8 = (bf16[2,320,128]{2,1,0:T(8,128)(2,1)S(1)}, bf16[2,320,128]{2,1,0:T(8,128)(2,1)S(1)}, u32[]{:S(2)}, u32[]{:S(2)}) collective-permute-start(bf16[2,320,128]{2,1,0:T(8,128)(2,1)S(1)} %get-tuple-element.74.rest_0_), channel_id=1, source_target_pairs={{0,8},{4,12},{8,0},{12,4},{16,24},{20,28},{24,16},{28,20},{1,9},{5... | collective-permute-start | bytes 491528 | tf_op jit(solution)/shard_map/ppermute | solution.py:774
  28.5 6.9 %collective-permute-start.17 = (bf16[2,320,128]{2,1,0:T(8,128)(2,1)S(1)}, bf16[2,320,128]{2,1,0:T(8,128)(2,1)S(1)}, u32[]{:S(2)}, u32[]{:S(2)}) collective-permute-start(bf16[2,320,128]{2,1,0:T(8,128)(2,1)S(1)} %collective-permute-done.9.rest_5_), channel_id=1, source_target_pairs={{0,16},{4,20},{8,24},{12,28},{16,0},{20,4},{24,8},{28,12},{1,17},{... | collective-permute-start | bytes 491528 | tf_op jit(solution)/shard_map/ppermute | solution.py:774
  29.2 8.9 %collective-permute-start.16 = (bf16[2,320,128]{2,1,0:T(8,128)(2,1)S(1)}, bf16[2,320,128]{2,1,0:T(8,128)(2,1)S(1)}, u32[]{:S(2)}, u32[]{:S(2)}) collective-permute-start(bf16[2,320,128]{2,1,0:T(8,128)(2,1)S(1)} %collective-permute-done.12.rest_8_), channel_id=1, source_target_pairs={{0,8},{4,12},{8,0},{12,4},{16,24},{20,28},{24,16},{28,20},{1,9},{5... | collective-permute-start | bytes 491528 | tf_op jit(solution)/shard_map/ppermute | solution.py:774
  32.5 5.7 %collective-permute-start.6 = (bf16[2,320,128]{2,1,0:T(8,128)(2,1)S(1)}, bf16[2,320,128]{2,1,0:T(8,128)(2,1)S(1)}, u32[]{:S(2)}, u32[]{:S(2)}) collective-permute-start(bf16[2,320,128]{2,1,0:T(8,128)(2,1)S(1)} %get-tuple-element.74.rest_0_), channel_id=1, source_target_pairs={{0,4},{4,0},{8,12},{12,8},{16,20},{20,16},{24,28},{28,24},{1,5},{5... | collective-permute-start | bytes 491528 | tf_op jit(solution)/shard_map/ppermute | solution.py:774
  32.5 6.4 %collective-permute-start.15 = (bf16[2,320,128]{2,1,0:T(8,128)(2,1)S(1)}, bf16[2,320,128]{2,1,0:T(8,128)(2,1)S(1)}, u32[]{:S(2)}, u32[]{:S(2)}) collective-permute-start(bf16[2,320,128]{2,1,0:T(8,128)(2,1)S(1)} %collective-permute-done.13.rest_9_), channel_id=1, source_target_pairs={{0,4},{4,0},{8,12},{12,8},{16,20},{20,16},{24,28},{28,24},{1,5},{5... | collective-permute-start | bytes 491528 | tf_op jit(solution)/shard_map/ppermute | solution.py:774
  35.4 6.3 %collective-permute-start.14 = (bf16[2,320,128]{2,1,0:T(8,128)(2,1)S(1)}, bf16[2,320,128]{2,1,0:T(8,128)(2,1)S(1)}, u32[]{:S(2)}, u32[]{:S(2)}) collective-permute-start(bf16[2,320,128]{2,1,0:T(8,128)(2,1)S(1)} %collective-permute-done.12.rest_8_), channel_id=1, source_target_pairs={{0,4},{4,0},{8,12},{12,8},{16,20},{20,16},{24,28},{28,24},{1,5},{5... | collective-permute-start | bytes 491528 | tf_op jit(solution)/shard_map/ppermute | solution.py:774
  38.1 14.7 %collective-permute-start.25 = (bf16[4,224,128]{2,1,0:T(8,128)(2,1)S(1)}, bf16[4,224,128]{2,1,0:T(8,128)(2,1)S(1)}, u32[]{:S(2)}, u32[]{:S(2)}) collective-permute-start(bf16[4,224,128]{2,1,0:T(8,128)(2,1)S(1)} %shard_map.86.rest_0_), channel_id=1, source_target_pairs={{0,24},{4,28},{8,16},{12,20},{16,8},{20,12},{24,0},{28,4},{1,25},{... | collective-permute-start | bytes 688136 | tf_op jit(solution)/shard_map/ppermute | solution.py:774
  38.8 14.0 %collective-permute-start.23 = (bf16[4,224,128]{2,1,0:T(8,128)(2,1)S(1)}, bf16[4,224,128]{2,1,0:T(8,128)(2,1)S(1)}, u32[]{:S(2)}, u32[]{:S(2)}) collective-permute-start(bf16[4,224,128]{2,1,0:T(8,128)(2,1)S(1)} %shard_map.86.rest_0_), channel_id=1, source_target_pairs={{0,16},{4,20},{8,24},{12,28},{16,0},{20,4},{24,8},{28,12},{1,17},{... | collective-permute-start | bytes 688136 | tf_op jit(solution)/shard_map/ppermute | solution.py:774
  40.2 12.7 %collective-permute-start.21 = (bf16[4,224,128]{2,1,0:T(8,128)(2,1)S(1)}, bf16[4,224,128]{2,1,0:T(8,128)(2,1)S(1)}, u32[]{:S(2)}, u32[]{:S(2)}) collective-permute-start(bf16[4,224,128]{2,1,0:T(8,128)(2,1)S(1)} %shard_map.86.rest_0_), channel_id=1, source_target_pairs={{0,8},{4,12},{8,0},{12,4},{16,24},{20,28},{24,16},{28,20},{1,9},{5... | collective-permute-start | bytes 688136 | tf_op jit(solution)/shard_map/ppermute | solution.py:774
  75.4 5.9 %collective-permute-start.27 = (bf16[16,224,128]{2,1,0:T(8,128)(2,1)S(1)}, bf16[16,224,128]{2,1,0:T(8,128)(2,1)S(1)}, u32[]{:S(2)}, u32[]{:S(2)}) collective-permute-start(bf16[16,224,128]{2,1,0:T(8,128)(2,1)S(1)} %get-tuple-element.97), channel_id=1, source_target_pairs={{0,4},{4,0},{8,12},{12,8},{16,20},{20,16},{24,28},{28,24},{1,5},{5... | collective-permute-start | bytes 2752520 | tf_op jit(solution)/shard_map/ppermute | solution.py:774
  90.9 13.6 %collective-permute-start.31 = (bf16[16,304,128]{2,1,0:T(8,128)(2,1)S(1)}, bf16[16,304,128]{2,1,0:T(8,128)(2,1)S(1)}, u32[]{:S(2)}, u32[]{:S(2)}) collective-permute-start(bf16[16,304,128]{2,1,0:T(8,128)(2,1)S(1)} %get-tuple-element.118), channel_id=1, source_target_pairs={{0,4},{4,0},{8,12},{12,8},{16,20},{20,16},{24,28},{28,24},{1,5},{5... | collective-permute-start | bytes 3735560 | tf_op jit(solution)/shard_map/ppermute | solution.py:774
  91.2 8.4 %collective-permute-start.28 = (bf16[4,224,128]{2,1,0:T(8,128)(2,1)S(1)}, bf16[4,224,128]{2,1,0:T(8,128)(2,1)S(1)}, u32[]{:S(2)}, u32[]{:S(2)}) collective-permute-start(bf16[4,224,128]{2,1,0:T(8,128)(2,1)S(1)} %get-tuple-element.113), channel_id=1, source_target_pairs={{0,8},{4,12},{8,0},{12,4},{16,24},{20,28},{24,16},{28,20},{1,9},{5... | collective-permute-start | bytes 688136 | tf_op jit(solution)/shard_map/ppermute | solution.py:774
  91.7 12.6 %collective-permute-start.29 = (bf16[4,224,128]{2,1,0:T(8,128)(2,1)S(1)}, bf16[4,224,128]{2,1,0:T(8,128)(2,1)S(1)}, u32[]{:S(2)}, u32[]{:S(2)}) collective-permute-start(bf16[4,224,128]{2,1,0:T(8,128)(2,1)S(1)} %get-tuple-element.114), channel_id=1, source_target_pairs={{0,16},{4,20},{8,24},{12,28},{16,0},{20,4},{24,8},{28,12},{1,17},{... | collective-permute-start | bytes 688136 | tf_op jit(solution)/shard_map/ppermute | solution.py:774
  92.4 11.9 %collective-permute-start.30 = (bf16[4,224,128]{2,1,0:T(8,128)(2,1)S(1)}, bf16[4,224,128]{2,1,0:T(8,128)(2,1)S(1)}, u32[]{:S(2)}, u32[]{:S(2)}) collective-permute-start(bf16[4,224,128]{2,1,0:T(8,128)(2,1)S(1)} %get-tuple-element.115), channel_id=1, source_target_pairs={{0,24},{4,28},{8,16},{12,20},{16,8},{20,12},{24,0},{28,4},{1,25},{... | collective-permute-start | bytes 688136 | tf_op jit(solution)/shard_map/ppermute | solution.py:774
  95.9 8.6 %collective-permute-start.33 = (f32[8,512]{1,0:T(8,128)S(1)}, f32[8,512]{1,0:T(8,128)S(1)}, u32[]{:S(2)}, u32[]{:S(2)}) collective-permute-start(f32[8,512]{1,0:T(8,128)S(1)} %shard_map.94.sums_ref), channel_id=1, source_target_pairs={{0,16},{4,20},{8,24},{12,28},{16,0},{20,4},{24,8},{28,12},{1,17},{... | collective-permute-start | bytes 49160 | tf_op jit(solution)/shard_map/ppermute | solution.py:774
  104.7 9.8 %collective-permute-start.34 = (bf16[4,304,128]{2,1,0:T(8,128)(2,1)S(1)}, bf16[4,304,128]{2,1,0:T(8,128)(2,1)S(1)}, u32[]{:S(2)}, u32[]{:S(2)}) collective-permute-start(bf16[4,304,128]{2,1,0:T(8,128)(2,1)S(1)} %get-tuple-element.123), channel_id=1, source_target_pairs={{0,16},{4,20},{8,24},{12,28},{16,0},{20,4},{24,8},{28,12},{1,17},{... | collective-permute-start | bytes 933896 | tf_op jit(solution)/shard_map/ppermute | solution.py:774
  105.8 8.8 %collective-permute-start.35 = (bf16[4,304,128]{2,1,0:T(8,128)(2,1)S(1)}, bf16[4,304,128]{2,1,0:T(8,128)(2,1)S(1)}, u32[]{:S(2)}, u32[]{:S(2)}) collective-permute-start(bf16[4,304,128]{2,1,0:T(8,128)(2,1)S(1)} %get-tuple-element.124), channel_id=1, source_target_pairs={{0,8},{4,12},{8,0},{12,4},{16,24},{20,28},{24,16},{28,20},{1,9},{5... | collective-permute-start | bytes 933896 | tf_op jit(solution)/shard_map/ppermute | solution.py:774
  107.0 7.6 %collective-permute-start.36 = (f32[8,512]{1,0:T(8,128)S(1)}, f32[8,512]{1,0:T(8,128)S(1)}, u32[]{:S(2)}, u32[]{:S(2)}) collective-permute-start(f32[8,512]{1,0:T(8,128)S(1)} %get-tuple-element.125.sums_ref), channel_id=1, source_target_pairs={{0,8},{4,12},{8,0},{12,4},{16,24},{20,28},{24,16},{28,20},{1,9},{5... | collective-permute-start | bytes 49160 | tf_op jit(solution)/shard_map/ppermute | solution.py:774
  117.0 8.2 %collective-permute-start.45 = (bf16[224,128]{1,0:T(8,128)(2,1)S(1)}, bf16[224,128]{1,0:T(8,128)(2,1)S(1)}, u32[]{:S(2)}, u32[]{:S(2)}) collective-permute-start(bf16[224,128]{1,0:T(8,128)(2,1)S(1)} %get-tuple-element.135), channel_id=1, source_target_pairs={{0,1},{1,0},{2,3},{3,2},{4,5},{5,4},{6,7},{7,6},{8,9},{9,8},{10,11... | collective-permute-start | bytes 172040 | tf_op jit(solution)/shard_map/ppermute | solution.py:774
  117.0 10.3 %collective-permute-start.46 = (bf16[224,128]{1,0:T(8,128)(2,1)S(1)}, bf16[224,128]{1,0:T(8,128)(2,1)S(1)}, u32[]{:S(2)}, u32[]{:S(2)}) collective-permute-start(bf16[224,128]{1,0:T(8,128)(2,1)S(1)} %get-tuple-element.136), channel_id=1, source_target_pairs={{0,2},{1,3},{2,0},{3,1},{4,6},{5,7},{6,4},{7,5},{8,10},{9,11},{10,... | collective-permute-start | bytes 172040 | tf_op jit(solution)/shard_map/ppermute | solution.py:774
  120.7 18.2 %collective-permute-start.42 = (bf16[304,128]{1,0:T(8,128)(2,1)S(1)}, bf16[304,128]{1,0:T(8,128)(2,1)S(1)}, u32[]{:S(2)}, u32[]{:S(2)}) collective-permute-start(bf16[304,128]{1,0:T(8,128)(2,1)S(1)} %get-tuple-element.132), channel_id=1, source_target_pairs={{0,1},{1,0},{2,3},{3,2},{4,5},{5,4},{6,7},{7,6},{8,9},{9,8},{10,11... | collective-permute-start | bytes 233480 | tf_op jit(solution)/shard_map/ppermute | solution.py:774
  121.3 17.6 %collective-permute-start.43 = (bf16[304,128]{1,0:T(8,128)(2,1)S(1)}, bf16[304,128]{1,0:T(8,128)(2,1)S(1)}, u32[]{:S(2)}, u32[]{:S(2)}) collective-permute-start(bf16[304,128]{1,0:T(8,128)(2,1)S(1)} %get-tuple-element.133), channel_id=1, source_target_pairs={{0,2},{1,3},{2,0},{3,1},{4,6},{5,7},{6,4},{7,5},{8,10},{9,11},{10,... | collective-permute-start | bytes 233480 | tf_op jit(solution)/shard_map/ppermute | solution.py:774
  123.4 15.4 %collective-permute-start.44 = (bf16[304,128]{1,0:T(8,128)(2,1)S(1)}, bf16[304,128]{1,0:T(8,128)(2,1)S(1)}, u32[]{:S(2)}, u32[]{:S(2)}) collective-permute-start(bf16[304,128]{1,0:T(8,128)(2,1)S(1)} %get-tuple-element.134), channel_id=1, source_target_pairs={{0,3},{1,2},{2,1},{3,0},{4,7},{5,6},{6,5},{7,4},{8,11},{9,10},{10,... | collective-permute-start | bytes 233480 | tf_op jit(solution)/shard_map/ppermute | solution.py:774
  125.2 6.1 %collective-permute-start.47 = (bf16[224,128]{1,0:T(8,128)(2,1)S(1)}, bf16[224,128]{1,0:T(8,128)(2,1)S(1)}, u32[]{:S(2)}, u32[]{:S(2)}) collective-permute-start(bf16[224,128]{1,0:T(8,128)(2,1)S(1)} %get-tuple-element.137), channel_id=1, source_target_pairs={{0,3},{1,2},{2,1},{3,0},{4,7},{5,6},{6,5},{7,4},{8,11},{9,10},{10,... | collective-permute-start | bytes 172040 | tf_op jit(solution)/shard_map/ppermute | solution.py:774
  127.3 5.8 %collective-permute-start.39 = (f32[8,512]{1,0:T(8,128)S(1)}, f32[8,512]{1,0:T(8,128)S(1)}, u32[]{:S(2)}, u32[]{:S(2)}) collective-permute-start(f32[8,512]{1,0:T(8,128)S(1)} %get-tuple-element.126.one_ref), channel_id=1, source_target_pairs={{0,3},{1,2},{2,1},{3,0},{4,7},{5,6},{6,5},{7,4},{8,11},{9,10},{10,... | collective-permute-start | bytes 49160 | tf_op jit(solution)/shard_map/ppermute | solution.py:774
  (22 other events, 91.7 us)

commit v3 on v2

--- a/solution.py
+++ b/solution.py
@@ -252,11 +252,12 @@
     return pl.BlockSpec(memory_space=pltpu.SMEM)
 
 
-def run_kernel(kernel, inputs, out_shape, scratch, limit, flops, scalar=True):
-    specs = [full_spec()] * len(inputs)
+def run_kernel(kernel, inputs, out_shape, scratch, limit, flops, scalar=True, spec=None):
+    specs = [spec or full_spec()] * len(inputs)
     if scalar:
         specs[0] = scalar_spec()
-    out_specs = jax.tree.map(lambda _: full_spec(), out_shape)
+    several = isinstance(out_shape, (list, tuple))
+    out_specs = [full_spec()] * len(out_shape) if several else full_spec()
     return pl.pallas_call(
         kernel,
         in_specs=specs,
@@ -286,9 +287,36 @@
 
 
 def stats_kernel(
-    me_ref, features_ref, presence_ref, params_ref, second_ref, masked_ref, block_ref, block_two_ref
+    me_ref,
+    features_hbm,
+    presence_hbm,
+    params_hbm,
+    second_hbm,
+    masked_ref,
+    block_ref,
+    block_two_ref,
+    features_ref,
+    presence_ref,
+    params_ref,
+    second_ref,
+    sems,
 ):
     del me_ref
+    copies = [
+        pltpu.make_async_copy(source, target, sems.at[index])
+        for index, (source, target) in enumerate(
+            (
+                (presence_hbm, presence_ref),
+                (features_hbm, features_ref),
+                (params_hbm, params_ref),
+                (second_hbm, second_ref),
+            )
+        )
+    ]
+    for copy in copies:
+        copy.start()
+    for copy in copies:
+        copy.wait()
     rows, width = features_ref.shape
     mask = spread_presence(presence_ref[...], width)
     masked = features_ref[...].astype(F32) * mask
@@ -317,6 +345,14 @@
     return lambda ref_rows, body: lax.fori_loop(
         0, ref_rows // tile, lambda step, carry: body(pl.multiple_of(step * tile, tile), carry), 0
     )
+
+
+def in_turn(first, second):
+    for e in range(7):
+        if e < 6:
+            first(e)
+        if e > 0:
+            second(e - 1)
 
 
 def spot(e):
@@ -385,18 +421,21 @@
         normed = (masked_ref[now, :].astype(F32) - entry_ref[0:1, :]) * entry_ref[1:2, :]
         level_ref[now, :] = (normed * entry_ref[2:3, :] + entry_ref[3:4, :]).astype(BF16)
         probs_ref[now, :] = group_softmax(mm(level_ref[now, :], gate_ref[...]), GROUPS_ONE)
-        for e in range(6):
+        def first_half(e):
             pre = mm(level_ref[now, :], w_in_ref[:, spot(e)]) + small_ref[0, e : e + 1, :]
             gate = sigmoid(pre)
             silu = pre * gate
             active_ref[e, now, :] = silu.astype(BF16)
             slope_ref[e, now, :] = (gate + silu * (1.0 - gate)).astype(BF16)
-        for e in range(6):
+
+        def second_half(e):
             post = mm(active_ref[e, now, :], w_out_ref[e]) + small_ref[1, e : e + 1, :]
             normal, scale = norm_forward(post)
             normal_ref[e, now, :] = normal.astype(BF16)
             scale_ref[e, now, :] = jnp.broadcast_to(scale, (tile, LANES))
             output_ref[e] = normal * small_ref[2, e : e + 1, :] + small_ref[3, e : e + 1, :]
+
+        in_turn(first_half, second_half)
         wide_ref[...] = spread_columns(probs_ref[now, :], spread_ref[...])
         for index, (low, _) in enumerate(GROUPS_ONE):
             mixed_ref[index, now, :] = mix_parts(
@@ -482,18 +521,21 @@
     def body(start, carry):
         now = pl.ds(start, tile)
         lane = lax.broadcasted_iota(jnp.int32, (tile, LANES), 1)
-        for e in range(6):
+        def first_half(e):
             pre = mm(mixed_ref[e // 2, now, :], w_in_ref[:, spot(e)]) + small_ref[0, e : e + 1, :]
             gate = sigmoid(pre)
             silu = pre * gate
             active_ref[e, now, :] = silu.astype(BF16)
             slope_ref[:, spot(e)] = gate + silu * (1.0 - gate)
-        for e in range(6):
+
+        def second_half(e):
             post = mm(active_ref[e, now, :], w_out_ref[e]) + small_ref[1, e : e + 1, :]
             normal, scale = norm_forward(post)
             normal_ref[e] = normal
             scale_ref[e] = jnp.broadcast_to(scale, (tile, LANES))
             output_ref[e] = normal * small_ref[2, e : e + 1, :] + small_ref[3, e : e + 1, :]
+
+        in_turn(first_half, second_half)
         logits = jnp.where(
             lane < 4, mm(mixed_ref[0, now, :], gate_ref[...]), mm(mixed_ref[1, now, :], gate_ref[...])
         )
@@ -535,7 +577,7 @@
         logit_grad = group_softmax_back(probs, prob_grads, GROUPS_TWO)
         logit_ref[0, now, :] = jnp.where(lane < 4, logit_grad, 0.0).astype(BF16)
         logit_ref[1, now, :] = jnp.where((lane >= 4) & (lane < 8), logit_grad, 0.0).astype(BF16)
-        for e in range(6):
+        def norm_half(e):
             out_grad = None
             for task in range(2):
                 if e in MEMBERS_TWO[task]:
@@ -551,11 +593,14 @@
             post_grad = post_grad.astype(BF16)
             post_grad_ref[e, now, :] = post_grad
             g_small_ref[1, e : e + 1, :] += column_sum(post_grad.astype(F32))
-        for e in range(6):
+
+        def active_half(e):
             act_grad = mm_nt(post_grad_ref[e, now, :], w_out_ref[e])
             pre_grad = (act_grad * slope_ref[:, spot(e)]).astype(BF16)
             pre_grad_ref[now, spot(e)] = pre_grad
             g_small_ref[0, e : e + 1, :] += column_sum(pre_grad.astype(F32))
+
+        in_turn(norm_half, active_half)
         for index in range(3):
             pair = slice(2 * index * H, 2 * (index + 1) * H)
             grad = mm_nt(pre_grad_ref[now, pair], w_in_ref[:, pair])
@@ -669,7 +714,7 @@
                         mixed_grad_ref[index, now, :] * output
                     )
         logit_ref[here, :] = group_softmax_back(probs, into_lane(columns), GROUPS_ONE).astype(BF16)
-        for e in range(6):
+        def norm_half(e):
             normal = normal_ref[e, now, :].astype(F32)
             out_grad = None
             for index, (low, _) in enumerate(GROUPS_ONE):
@@ -687,11 +732,14 @@
             ).astype(BF16)
             post_grad_ref[e, here, :] = post_grad
             g_small_ref[1, e : e + 1, :] += column_sum(post_grad.astype(F32))
-        for e in range(6):
+
+        def active_half(e):
             act_grad = mm_nt(post_grad_ref[e, here, :], w_out_ref[e])
             pre_grad = (act_grad * slope_ref[e, now, :].astype(F32)).astype(BF16)
             pre_grad_ref[here, spot(e)] = pre_grad
             g_small_ref[0, e : e + 1, :] += column_sum(pre_grad.astype(F32))
+
+        in_turn(norm_half, active_half)
         level_grad = mm_nt(pre_grad_ref[here, :], w_in_ref[...]) + mm_nt(
             logit_ref[here, :], gate_ref[...]
         )
@@ -702,6 +750,27 @@
         return carry
 
     tiles(tile)(logit_ref.shape[0], body)
+
+
+def send_sums(sums, block_refs):
+    high = sums.astype(BF16).astype(F32)
+    lines = []
+    for value in (high, sums - high):
+        for row in range(2):
+            for index in range(value.shape[1] // LANES):
+                lines.append(value[row : row + 1, index * LANES : (index + 1) * LANES])
+    block = jnp.concatenate(lines, axis=0).astype(BF16)
+    for ref in block_refs:
+        ref[ref.shape[0] - 16 :, :] = block
+
+
+def got_sums(block_ref, shape):
+    rows = block_ref.shape[0]
+    block = block_ref[rows - 16 :, :].astype(F32)
+    block = block[:8] + block[8:]
+    lanes = shape[1] // LANES
+    lines = [from_lanes(block[row * lanes : (row + 1) * lanes]) for row in range(2)]
+    return jnp.concatenate(lines + [jnp.zeros((shape[0] - 2, shape[1]), F32)], axis=0)
 
 
 def level_one_weights(
@@ -710,6 +779,7 @@
     me_ref,
     level_ref,
     active_ref,
+    sums_ref,
     small_ref,
     logit_a_ref,
     logit_b_ref,
@@ -751,6 +821,8 @@
             (count * rows - used_rows, LANES), F32
         )
     collect_pieces(me_ref[0], count, rows, flat_ref, grads_refs)
+    if len(grads_refs) > 1:
+        send_sums(sums_ref[...], [grads_refs[1].at[0]])
 
 
 def input_kernel(
@@ -850,9 +922,15 @@
     out_ref[...] = total[: out_ref.shape[0]]
 
 
-def last_head_kernel(me_ref, sums_ref, own_ref, one_ref, two_ref, three_ref, out_ref):
+def last_head_kernel(
+    me_ref, sums_ref, own_ref, one_ref, two_ref, three_ref, out_ref, total_ref
+):
     last_kernel(own_ref, one_ref, two_ref, three_ref, out_ref)
-    put_head(me_ref, sums_ref, out_ref)
+    sums = sums_ref[...]
+    for ref in (one_ref, two_ref, three_ref):
+        sums = sums + got_sums(ref, sums.shape)
+    total_ref[...] = sums
+    put_head(me_ref, total_ref, out_ref)
 
 
 def put_head(me_ref, sums_ref, out_ref):
@@ -870,12 +948,8 @@
     put_head(me_ref, sums_ref, out_ref)
 
 
-def add_kernel(one_ref, two_ref, out_ref):
-    out_ref[...] = one_ref[...] + two_ref[...]
-
-
 def core_halves_kernel(
-    keep_ref, got_ref, sums_ref, sums_got_ref, one_ref, two_ref, out_ref, send_one_ref, send_two_ref
+    keep_ref, got_ref, sums_ref, one_ref, two_ref, out_ref, send_one_ref, send_two_ref
 ):
     total = keep_ref[...].astype(F32) + got_ref[...].astype(F32)
     for x in range(2):
@@ -886,7 +960,9 @@
         for z in range(2):
             two_ref[2 * y + z] = total[8 * y + 2 + z]
             send_two_ref[2 * y + z] = total[8 * y + 4 + 2 + z].astype(BF16)
-    out_ref[...] = sums_ref[...] + sums_got_ref[...]
+    sums = sums_ref[...] + got_sums(got_ref.at[0], sums_ref.shape)
+    out_ref[...] = sums
+    send_sums(sums, [send_one_ref.at[0]])
 
 
 def plane_halves_kernel(
@@ -895,7 +971,6 @@
     got_one_ref,
     got_two_ref,
     sums_ref,
-    sums_got_ref,
     keep_one_ref,
     keep_two_ref,
     out_ref,
@@ -909,11 +984,22 @@
         total = ref[...] + got[...].astype(F32)
         keep[...] = total[0:2]
         send[...] = total[2:4].astype(BF16)
-    out_ref[...] = sums_ref[...] + sums_got_ref[...]
+    sums = sums_ref[...] + got_sums(got_one_ref.at[0], sums_ref.shape)
+    out_ref[...] = sums
+    send_sums(sums, [send_one_ref.at[0]])
 
 
 def near_halves_kernel(
-    one_ref, two_ref, got_one_ref, got_two_ref, keep_ref, send_one_ref, send_two_ref, send_three_ref
+    one_ref,
+    two_ref,
+    got_one_ref,
+    got_two_ref,
+    sums_ref,
+    keep_ref,
+    out_ref,
+    send_one_ref,
+    send_two_ref,
+    send_three_ref,
 ):
     one = one_ref[...] + got_one_ref[...].astype(F32)
     two = two_ref[...] + got_two_ref[...].astype(F32)
@@ -921,10 +1007,9 @@
     send_one_ref[...] = one[1].astype(BF16)
     send_two_ref[...] = two[0].astype(BF16)
     send_three_ref[...] = two[1].astype(BF16)
-
-
-def add_four_kernel(one_ref, two_ref, three_ref, four_ref, out_ref):
-    out_ref[...] = (one_ref[...] + two_ref[...]) + (three_ref[...] + four_ref[...])
+    sums = sums_ref[...] + got_sums(got_one_ref.at[0], sums_ref.shape)
+    out_ref[...] = sums
+    send_sums(sums, [send_one_ref, send_two_ref, send_three_ref])
 
 
 def scatter_plain(value):
@@ -939,12 +1024,13 @@
     cube = hypercube_ok()
     tile = math.gcd(rows, 256)
     half = rows // 2
+    big = math.gcd(rows, 512)
     me = lax.axis_index(AXES).astype(jnp.int32).reshape(1)
     chunks = [first_params.shape[0] // LANES, second_params.shape[0] // LANES]
     extra = 6 * lanes
     shape = jax.ShapeDtypeStruct
     fields = presence.T
-    blocks = [up(chunks[0], 16), up(chunks[1], 16)]
+    blocks = [up(chunks[0], 16) + (16 if cube else 0), up(chunks[1], 16)]
 
     masked, block_one, block_two = run_kernel(
         stats_kernel,
@@ -956,13 +1042,20 @@
             second_params.reshape(chunks[1], LANES),
         ],
         (
-            shape((rows, width), BF16),
-            shape((up(chunks[0] + extra, 16), LANES), BF16),
-            shape((blocks[1], LANES), BF16),
+            pltpu.VMEM((rows, width), BF16),
+            pltpu.VMEM((up(chunks[0] + extra, 16), LANES), BF16),
+            pltpu.VMEM((blocks[1], LANES), BF16),
         ),
-        [],
-        8,
+        [
+            pltpu.VMEM((rows, width), BF16),
+            pltpu.VMEM(fields.shape, jnp.int32),
+            pltpu.VMEM((chunks[0], LANES), BF16),
+            pltpu.VMEM((chunks[1], LANES), BF16),
+            pltpu.SemaphoreType.DMA((4,)),
+        ],
+        60,
         rows * width * 10,
+        spec=pl.BlockSpec(memory_space=pltpu.HBM),
     )
     if cube:
         origin = me
@@ -970,6 +1063,7 @@
         first, second = stack_near(near_one, 2)
         near_two = gather_near(after(block_two, first))
         pieces_one = gather_halves(first, second)
+        near_two[3] = after(near_two[3], pieces_one[12], pieces_one[13])
         (stack_two,) = stack_near(near_two, 1)
         plane_two = gather_plane(after(stack_two, pieces_one[12], pieces_one[13]))
         masked = after(masked, stack_two)
@@ -979,7 +1073,7 @@
         plane_two = [lax.all_gather(block_two, AXES)]
 
     saved = run_kernel(
-        functools.partial(level_one_forward, chunks[0], tile, len(pieces_one)),
+        functools.partial(level_one_forward, chunks[0], big, len(pieces_one)),
         [origin, masked] + pieces_one,
         [
             shape((rows, width), BF16),
@@ -998,11 +1092,11 @@
         [
             pltpu.VMEM((count * chunks[0], LANES), F32),
             pltpu.VMEM((count, extra, LANES), F32),
-            pltpu.VMEM((6, tile, H), F32),
-            pltpu.VMEM((tile, 14 * LANES), F32),
+            pltpu.VMEM((6, big, H), F32),
+            pltpu.VMEM((big, 14 * LANES), F32),
             pltpu.VMEM((2 * LANES, 14 * LANES), BF16),
         ],
-        20,
+        28,
         rows * 6 * (width + H) * H * 2,
     )
     level, active, slope, normal, scale, probs, mixed, w_in, w_out, small, gate, entry = saved
@@ -1049,17 +1143,9 @@
         32,
         rows * 6 * 2 * H * H * 2 * 3,
     )
-    if cube:
-        keep_two, send_two = grads_two
-        own_two, *sends_two = small_kernel(
-            core_direct_kernel,
-            [keep_two, xor_permute(send_two, "wide", 1)],
-            [shape((4, blocks[1], LANES), F32)] + [shape((4, blocks[1], LANES), BF16)] * 3,
-        )
-
     def backward(part, *before):
         return run_kernel(
-            functools.partial(level_one_backward, min(tile, half), part * half),
+            functools.partial(level_one_backward, math.gcd(big, half), part * half),
             [
                 mixed_grad,
                 masked,
@@ -1071,7 +1157,7 @@
                 w_out,
                 small,
                 gate,
-                entry if part == 0 or not cube else after(entry, own_two),
+                entry,
                 *before,
             ],
             [
@@ -1083,16 +1169,24 @@
                 shape((half, 6 * H), BF16),
             ],
             [
-                pltpu.VMEM((min(tile, half), 14 * LANES), F32),
+                pltpu.VMEM((math.gcd(big, half), 14 * LANES), F32),
                 pltpu.VMEM((2 * LANES, 14 * LANES), BF16),
                 pltpu.VMEM((2 * H, 2 * LANES), BF16),
             ],
-            12,
+            16,
             rows * 6 * (width + H) * H * 2,
             scalar=False,
         )
 
     grad_a, sums, g_small, logit_a, post_a, pre_a = backward(0)
+    if cube:
+        keep_two, send_two = grads_two
+        own_two, *sends_two = small_kernel(
+            core_direct_kernel,
+            [after(keep_two, sums), xor_permute(send_two, "wide", 1)],
+            [shape((4, blocks[1], LANES), F32)] + [shape((4, blocks[1], LANES), BF16)] * 3,
+        )
+        sums = after(sums, own_two)
     grad_b, sums, g_small, logit_b, post_b, pre_b = backward(1, sums, g_small)
     grads_one = run_kernel(
         functools.partial(level_one_weights, count, chunks[0]),
@@ -1100,6 +1194,7 @@
             origin,
             level,
             active,
+            sums,
             g_small,
             logit_a,
             logit_b,
@@ -1114,46 +1209,19 @@
         rows * 6 * (width + H) * H * 2,
     )
     if cube:
-        low, high = shape((4, blocks[0], LANES), BF16), shape((4, blocks[0], LANES), F32)
-        summed = shape((8, width), F32)
-        keep, send = grads_one
-        sums = small_kernel(
-            add_kernel, [sums, after(xor_permute(sums, "wide", 1), send)], summed
-        )
         keep_two, *sends_two = small_kernel(
             plane_direct_kernel,
             [own_two]
             + [xor_permute(part, "wide", bit) for part, bit in zip(sends_two, (2, 4, 6))],
             [shape((blocks[1], LANES), F32)] + [shape((blocks[1], LANES), BF16)] * 3,
         )
+        summed = shape((8, width), F32)
+        low, high = shape((4, blocks[0], LANES), BF16), shape((4, blocks[0], LANES), F32)
+        keep, send = grads_one
         one, two, sums, send_one, send_two = small_kernel(
             core_halves_kernel,
-            [after(keep, keep_two), xor_permute(send, "wide", 1), sums, xor_permute(sums, "wide", 4)],
+            [keep, xor_permute(after(send, keep_two), "wide", 1), sums],
             [high, high, summed, low, low],
-        )
-        low, high = shape((2, blocks[0], LANES), BF16), shape((2, blocks[0], LANES), F32)
-        one, two, sums, send_one, send_two = small_kernel(
-            plane_halves_kernel,
-            [
-                one,
-                two,
-                xor_permute(send_one, "wide", 4),
-                xor_permute(send_two, "wide", 2),
-                sums,
-                xor_permute(sums, "wide", 2),
-            ],
-            [high, high, summed, low, low],
-        )
-        low, high = shape((blocks[0], LANES), BF16), shape((blocks[0], LANES), F32)
-        keep, *sends = small_kernel(
-            near_halves_kernel,
-            [one, two, xor_permute(send_one, "wide", 2), xor_permute(send_two, "wide", 4)],
-            [high, low, low, low],
-        )
-        sums = small_kernel(
-            add_four_kernel,
-            [sums] + [xor_permute(sums, "narrow", k) for k in (1, 2, 3)],
-            summed,
         )
         second_grad = small_kernel(
             last_kernel,
@@ -1161,11 +1229,35 @@
             + [xor_permute(part, "narrow", k) for part, k in zip(sends_two, (1, 2, 3))],
             shape((chunks[1], LANES), F32),
         )
-        first_grad = small_kernel(
+        low, high = shape((2, blocks[0], LANES), BF16), shape((2, blocks[0], LANES), F32)
+        one, two, sums, send_one, send_two = small_kernel(
+            plane_halves_kernel,
+            [
+                after(one, second_grad),
+                two,
+                xor_permute(send_one, "wide", 4),
+                xor_permute(send_two, "wide", 2),
+                sums,
+            ],
+            [high, high, summed, low, low],
+        )
+        low, high = shape((blocks[0], LANES), BF16), shape((blocks[0], LANES), F32)
+        keep, sums, *sends = small_kernel(
+            near_halves_kernel,
+            [
+                one,
+                two,
+                xor_permute(send_one, "wide", 2),
+                xor_permute(send_two, "wide", 4),
+                sums,
+            ],
+            [high, summed, low, low, low],
+        )
+        first_grad, sums = small_kernel(
             last_head_kernel,
             [me, sums, keep]
             + [xor_permute(part, "narrow", k) for part, k in zip(sends, (1, 2, 3))],
-            shape((chunks[0], LANES), F32),
+            [shape((chunks[0], LANES), F32), summed],
             scalar=True,
         )
     else:

time: 140 us -> 124 us (0.89)
  starting transfers between devices: 46 us -> 38.8 us
  waiting for transfers between devices: 39.6 us -> 32.7 us
  local copies, waits for them, and re-layouts: 3.68 us -> 1.64 us
    ppermute x48 -> x42, starting transfers between devices: 46 us -> 38.8 us  [xor_permute(): lax.ppermute(value, axis, [(index, index ^ bit) for index in range(size)])]
    ppermute x48 -> x42, waiting for transfers between devices: 39.6 us -> 32.7 us  [xor_permute(): lax.ppermute(value, axis, [(index, index ^ bit) for index in range(size)])]
    unnamed x12 -> x8, local copies, waits for them, and re-layouts: 3.68 us -> 1.64 us
    pallas_call x18 -> x16, Pallas kernels: 49.5 us -> 50.3 us  [run_kernel(): pl.pallas_call(kernel, in_specs=specs, out_specs=out_specs, out_shape=out...]
  transfers between devices with their start and end apart: 48 -> 42, of which waited for: 23 -> 23; matrix products, arithmetic and copies ran while one was open for 0% -> 0% of each run, Pallas kernels for 13% -> 20%
where the time goes in v3:
time: 124 us
  Pallas kernels  50.3 us (41%)
  starting transfers between devices  38.8 us (31%)
  waiting for transfers between devices  32.7 us (26%)
  local copies, waits for them, and re-layouts  1.64 us (1%)
    pallas_call x16, Pallas kernels, run_kernel(): pl.pallas_call(kernel, in_specs=specs, out_specs=out_specs, out_shape=out...  50.3 us
    ppermute x42, starting transfers between devices, xor_permute(): lax.ppermute(value, axis, [(index, index ^ bit) for index in range(size)])  38.8 us
    ppermute x42, waiting for transfers between devices, xor_permute(): lax.ppermute(value, axis, [(index, index ^ bit) for index in range(size)])  32.7 us
  transfers between devices with their start and end apart: 42, of which 23 were waited for; matrix products, arithmetic and copies ran while one was open for 0% of the time, Pallas kernels for 20%

profile of v3, /device:TPU:0, one launch (start us, length us, event | category | flops | bytes accessed | tf_op | source)
XLA Modules:
  0.0 124.3 jit_solution(8757515620838412898)
XLA Ops:
  0.6 2.1 %shard_map.84 = (bf16[1024,512]{1,0:T(8,128)(2,1)S(1)}, bf16[320,128]{1,0:T(8,128)(2,1)S(1)}, bf16[224,128]{1,0:T(8,128)(2,1)S(1)}) custom-call(s32[1]{0:T(128)} %bitcast.me_ref, bf16[1024,512]{1,0:T(8,128)(2,1)} %features_hbm.1, s32[8,1024]{1,0:T(8,128)} %bitcast.6, bf16[292,128]{1,0:T(8,128)(2,1)} %bitcast.9, bf16[215,128]{1,0:T(8,128)(2,1)} %bitcast.10), custom_call_target="tpu_custom_call" | custom-call | flops 1048576 | bytes 1024 | tf_op jit(solution)/shard_map/pallas_call | solution.py:261
  2.7 3.1 %collective-permute-start = (bf16[320,128]{1,0:T(8,128)(2,1)S(1)}, bf16[320,128]{1,0:T(8,128)(2,1)S(1)}, u32[]{:S(2)}, u32[]{:S(2)}) collective-permute-start(bf16[320,128]{1,0:T(8,128)(2,1)S(1)} %get-tuple-element.78.refs_0_), channel_id=1, source_target_pairs={{0,1},{1,0},{2,3},{3,2},{4,5},{5,4},{6,7},{7,6},{8,9},{9,8},{10,11... | collective-permute-start | bytes 245768 | tf_op jit(solution)/shard_map/ppermute | solution.py:846
  5.8 2.6 %collective-permute-start.1 = (bf16[320,128]{1,0:T(8,128)(2,1)S(1)}, bf16[320,128]{1,0:T(8,128)(2,1)S(1)}, u32[]{:S(2)}, u32[]{:S(2)}) collective-permute-start(bf16[320,128]{1,0:T(8,128)(2,1)S(1)} %get-tuple-element.78.refs_0_), channel_id=1, source_target_pairs={{0,2},{1,3},{2,0},{3,1},{4,6},{5,7},{6,4},{7,5},{8,10},{9,11},{10,... | collective-permute-start | bytes 245768 | tf_op jit(solution)/shard_map/ppermute | solution.py:846
  8.4 6.6 %collective-permute-done.1.refs_2_ = bf16[320,128]{1,0:T(8,128)(2,1)S(1)} collective-permute-done((bf16[320,128]{1,0:T(8,128)(2,1)S(1)}, bf16[320,128]{1,0:T(8,128)(2,1)S(1)}, u32[]{:S(2)}, u32[]{:S(2)}) %collective-permute-start.1) | collective-permute-done | bytes 81952 | tf_op jit(solution)/shard_map/ppermute | solution.py:846
  15.1 1.6 %collective-permute-start.6 = (bf16[2,320,128]{2,1,0:T(8,128)(2,1)S(1)}, bf16[2,320,128]{2,1,0:T(8,128)(2,1)S(1)}, u32[]{:S(2)}, u32[]{:S(2)}) collective-permute-start(bf16[2,320,128]{2,1,0:T(8,128)(2,1)S(1)} %get-tuple-element.79.rest_0_), channel_id=1, source_target_pairs={{0,16},{4,20},{8,24},{12,28},{16,0},{20,4},{24,8},{28,12},{1,17},{... | collective-permute-start | bytes 491528 | tf_op jit(solution)/shard_map/ppermute | solution.py:846
  16.6 1.5 %collective-permute-start.8 = (bf16[2,320,128]{2,1,0:T(8,128)(2,1)S(1)}, bf16[2,320,128]{2,1,0:T(8,128)(2,1)S(1)}, u32[]{:S(2)}, u32[]{:S(2)}) collective-permute-start(bf16[2,320,128]{2,1,0:T(8,128)(2,1)S(1)} %get-tuple-element.81.rest_1_), channel_id=1, source_target_pairs={{0,8},{4,12},{8,0},{12,4},{16,24},{20,28},{24,16},{28,20},{1,9},{5... | collective-permute-start | bytes 491528 | tf_op jit(solution)/shard_map/ppermute | solution.py:846
  18.1 2.5 %collective-permute-start.5 = (bf16[224,128]{1,0:T(8,128)(2,1)S(1)}, bf16[224,128]{1,0:T(8,128)(2,1)S(1)}, u32[]{:S(2)}, u32[]{:S(2)}) collective-permute-start(bf16[224,128]{1,0:T(8,128)(2,1)S(1)} %get-tuple-element.80.refs_0_), channel_id=1, source_target_pairs={{0,3},{1,2},{2,1},{3,0},{4,7},{5,6},{6,5},{7,4},{8,11},{9,10},{10,... | collective-permute-start | bytes 172040 | tf_op jit(solution)/shard_map/ppermute | solution.py:846
  21.1 1.4 %collective-permute-start.4 = (bf16[224,128]{1,0:T(8,128)(2,1)S(1)}, bf16[224,128]{1,0:T(8,128)(2,1)S(1)}, u32[]{:S(2)}, u32[]{:S(2)}) collective-permute-start(bf16[224,128]{1,0:T(8,128)(2,1)S(1)} %get-tuple-element.80.refs_0_), channel_id=1, source_target_pairs={{0,2},{1,3},{2,0},{3,1},{4,6},{5,7},{6,4},{7,5},{8,10},{9,11},{10,... | collective-permute-start | bytes 172040 | tf_op jit(solution)/shard_map/ppermute | solution.py:846
  22.5 1.7 %collective-permute-done.5.refs_3_ = bf16[224,128]{1,0:T(8,128)(2,1)S(1)} collective-permute-done((bf16[224,128]{1,0:T(8,128)(2,1)S(1)}, bf16[224,128]{1,0:T(8,128)(2,1)S(1)}, u32[]{:S(2)}, u32[]{:S(2)}) %collective-permute-start.5) | collective-permute-done | bytes 57376 | tf_op jit(solution)/shard_map/ppermute | solution.py:846
  26.8 1.5 %collective-permute-start.9 = (bf16[2,320,128]{2,1,0:T(8,128)(2,1)S(1)}, bf16[2,320,128]{2,1,0:T(8,128)(2,1)S(1)}, u32[]{:S(2)}, u32[]{:S(2)}) collective-permute-start(bf16[2,320,128]{2,1,0:T(8,128)(2,1)S(1)} %collective-permute-done.8.rest_5_), channel_id=1, source_target_pairs={{0,16},{4,20},{8,24},{12,28},{16,0},{20,4},{24,8},{28,12},{1,17},{... | collective-permute-start | bytes 491528 | tf_op jit(solution)/shard_map/ppermute | solution.py:846
  31.3 1.8 %collective-permute-done.7.rest_12_ = bf16[2,320,128]{2,1,0:T(8,128)(2,1)S(1)} collective-permute-done((bf16[2,320,128]{2,1,0:T(8,128)(2,1)S(1)}, bf16[2,320,128]{2,1,0:T(8,128)(2,1)S(1)}, u32[]{:S(2)}, u32[]{:S(2)}) %collective-permute-start.7) | collective-permute-done | bytes 163872 | tf_op jit(solution)/shard_map/ppermute | solution.py:846
  33.7 1.4 %collective-permute-start.25 = (bf16[4,224,128]{2,1,0:T(8,128)(2,1)S(1)}, bf16[4,224,128]{2,1,0:T(8,128)(2,1)S(1)}, u32[]{:S(2)}, u32[]{:S(2)}) collective-permute-start(bf16[4,224,128]{2,1,0:T(8,128)(2,1)S(1)} %shard_map.86.rest_0_), channel_id=1, source_target_pairs={{0,24},{4,28},{8,16},{12,20},{16,8},{20,12},{24,0},{28,4},{1,25},{... | collective-permute-start | bytes 688136 | tf_op jit(solution)/shard_map/ppermute | solution.py:846
  35.1 1.5 %collective-permute-start.23 = (bf16[4,224,128]{2,1,0:T(8,128)(2,1)S(1)}, bf16[4,224,128]{2,1,0:T(8,128)(2,1)S(1)}, u32[]{:S(2)}, u32[]{:S(2)}) collective-permute-start(bf16[4,224,128]{2,1,0:T(8,128)(2,1)S(1)} %shard_map.86.rest_0_), channel_id=1, source_target_pairs={{0,16},{4,20},{8,24},{12,28},{16,0},{20,4},{24,8},{28,12},{1,17},{... | collective-permute-start | bytes 688136 | tf_op jit(solution)/shard_map/ppermute | solution.py:846
  38.9 8.7 %shard_map.87 = (bf16[1024,512]{1,0:T(8,128)(2,1)S(1)}, bf16[6,1024,256]{2,1,0:T(8,128)(2,1)S(1)}, bf16[6,1024,256]{2,1,0:T(8,128)(2,1)S(1)}, bf16[6,1024,256]{2...) custom-call(s32[1]{0:T(128)} %bitcast.me_ref, ...), custom_call_target="tpu_custom_call" | custom-call | flops 1048576 | bytes 1024 | tf_op jit(solution)/shard_map/pallas_call | solution.py:261
  47.7 1.6 %copy-done = bf16[6,1024,256]{2,1,0:T(8,128)(2,1)} copy-done((bf16[6,1024,256]{2,1,0:T(8,128)(2,1)}, bf16[6,1024,256]{2,1,0:T(8,128)(2,1)S(1)}, u32[]{:S(2)}) %copy-start) | copy-done | bytes 3145752
  51.8 20.4 %shard_map.88 = (f32[1024,128]{1,0:T(8,128)}, f32[3,1024,256]{2,1,0:T(8,128)S(1)}, bf16[16,224,128]{2,1,0:T(8,128)(2,1)S(1)}, bf16[16,224,128]{2,1,0:T(8,128)(2,1)S(1)}) custom-call(s32[1]{0:T(128)} %bitcast.me_ref, bf16[3,1024,256]{2,1,0:T(8,128)(2,1)S(1)} %get-tuple-element.84.mixed_ref, bf16[1024,128]{1,0:T(8,128)(2,1)S(1)} %copy-done.2, ...), custom_call_target="tpu_custom_call" | custom-call | flops 1048576 | bytes 1024 | tf_op jit(solution)/shard_map/pallas_call | solution.py:261
  72.4 5.3 %shard_map.89 = (f32[512,512]{1,0:T(8,128)S(1)}, f32[8,512]{1,0:T(8,128)S(1)}, f32[4,8,256]{2,1,0:T(8,128)S(1)}, bf16[512,128]{1,0:T(8,128)(2,1)S(1)}, bf16[6,51...) custom-call(f32[3,1024,256]{2,1,0:T(8,128)S(1)} %get-tuple-element.92.mixed_grad_ref, ...), custom_call_target="tpu_custom_call" | custom-call | flops 1048576 | bytes 1024 | tf_op jit(solution)/shard_map/pallas_call | solution.py:261
  78.0 1.4 %collective-permute-start.28 = (bf16[4,224,128]{2,1,0:T(8,128)(2,1)S(1)}, bf16[4,224,128]{2,1,0:T(8,128)(2,1)S(1)}, u32[]{:S(2)}, u32[]{:S(2)}) collective-permute-start(bf16[4,224,128]{2,1,0:T(8,128)(2,1)S(1)} %get-tuple-element.122), channel_id=1, source_target_pairs={{0,8},{4,12},{8,0},{12,4},{16,24},{20,28},{24,16},{28,20},{1,9},{5... | collective-permute-start | bytes 688136 | tf_op jit(solution)/shard_map/ppermute | solution.py:846
  79.9 1.6 %collective-permute-start.30 = (bf16[4,224,128]{2,1,0:T(8,128)(2,1)S(1)}, bf16[4,224,128]{2,1,0:T(8,128)(2,1)S(1)}, u32[]{:S(2)}, u32[]{:S(2)}) collective-permute-start(bf16[4,224,128]{2,1,0:T(8,128)(2,1)S(1)} %get-tuple-element.124), channel_id=1, source_target_pairs={{0,24},{4,28},{8,16},{12,20},{16,8},{20,12},{24,0},{28,4},{1,25},{... | collective-permute-start | bytes 688136 | tf_op jit(solution)/shard_map/ppermute | solution.py:846
  81.5 5.6 %shard_map.91 = (f32[512,512]{1,0:T(8,128)S(1)}, f32[8,512]{1,0:T(8,128)S(1)}, f32[4,8,256]{2,1,0:T(8,128)S(1)}, bf16[512,128]{1,0:T(8,128)(2,1)S(1)}, bf16[6,51...) custom-call(f32[3,1024,256]{2,1,0:T(8,128)S(1)} %get-tuple-element.92.mixed_grad_ref, ...), custom_call_target="tpu_custom_call" | custom-call | flops 1048576 | bytes 1024 | tf_op jit(solution)/shard_map/pallas_call | solution.py:261
  87.1 4.0 %shard_map.92 = (bf16[16,320,128]{2,1,0:T(8,128)(2,1)S(1)}, bf16[16,320,128]{2,1,0:T(8,128)(2,1)S(1)}) custom-call(s32[1]{0:T(128)} %bitcast.me_ref, bf16[1024,512]{1,0:T(8,128)(2,1)S(1)} %get-tuple-element.110.level_ref, bf16[6,1024,256]{2,1,0:T(8,128)(2,1)S(1)} %copy-done.1, f32[8,512]{1,0:T(8,128)S(1)} %get-tuple-element.112.sums_ref, ...), custom_call_target="tpu_custom_call" | custom-call | flops 1048576 | bytes 1024 | tf_op jit(solution)/shard_map/pallas_call | solution.py:261
  92.0 3.0 %collective-permute-done.31.got_ref = bf16[16,320,128]{2,1,0:T(8,128)(2,1)S(1)} collective-permute-done((bf16[16,320,128]{2,1,0:T(8,128)(2,1)S(1)}, bf16[16,320,128]{2,1,0:T(8,128)(2,1)S(1)}, u32[]{:S(2)}, u32[]{:S(2)}) %collective-permute-start.31) | collective-permute-done | bytes 1310752 | tf_op jit(solution)/shard_map/ppermute | solution.py:846
  98.1 2.0 %collective-permute-start.33 = (bf16[224,128]{1,0:T(8,128)(2,1)S(1)}, bf16[224,128]{1,0:T(8,128)(2,1)S(1)}, u32[]{:S(2)}, u32[]{:S(2)}) collective-permute-start(bf16[224,128]{1,0:T(8,128)(2,1)S(1)} %get-tuple-element.129), channel_id=1, source_target_pairs={{0,2},{1,3},{2,0},{3,1},{4,6},{5,7},{6,4},{7,5},{8,10},{9,11},{10,... | collective-permute-start | bytes 172040 | tf_op jit(solution)/shard_map/ppermute | solution.py:846
  101.9 2.7 %collective-permute-done.33.two_ref = bf16[224,128]{1,0:T(8,128)(2,1)S(1)} collective-permute-done((bf16[224,128]{1,0:T(8,128)(2,1)S(1)}, bf16[224,128]{1,0:T(8,128)(2,1)S(1)}, u32[]{:S(2)}, u32[]{:S(2)}) %collective-permute-start.33) | collective-permute-done | bytes 57376 | tf_op jit(solution)/shard_map/ppermute | solution.py:846
  104.6 1.5 %collective-permute-done.34.three_ref = bf16[224,128]{1,0:T(8,128)(2,1)S(1)} collective-permute-done((bf16[224,128]{1,0:T(8,128)(2,1)S(1)}, bf16[224,128]{1,0:T(8,128)(2,1)S(1)}, u32[]{:S(2)}, u32[]{:S(2)}) %collective-permute-start.34) | collective-permute-done | bytes 57376 | tf_op jit(solution)/shard_map/ppermute | solution.py:846
  107.8 1.5 %collective-permute-start.38 = (bf16[2,320,128]{2,1,0:T(8,128)(2,1)S(1)}, bf16[2,320,128]{2,1,0:T(8,128)(2,1)S(1)}, u32[]{:S(2)}, u32[]{:S(2)}) collective-permute-start(bf16[2,320,128]{2,1,0:T(8,128)(2,1)S(1)} %get-tuple-element.139), channel_id=1, source_target_pairs={{0,16},{4,20},{8,24},{12,28},{16,0},{20,4},{24,8},{28,12},{1,17},{... | collective-permute-start | bytes 491528 | tf_op jit(solution)/shard_map/ppermute | solution.py:846
  109.3 3.0 %collective-permute-done.37.got_one_ref = bf16[2,320,128]{2,1,0:T(8,128)(2,1)S(1)} collective-permute-done((bf16[2,320,128]{2,1,0:T(8,128)(2,1)S(1)}, bf16[2,320,128]{2,1,0:T(8,128)(2,1)S(1)}, u32[]{:S(2)}, u32[]{:S(2)}) %collective-permute-start.37) | collective-permute-done | bytes 163872 | tf_op jit(solution)/shard_map/ppermute | solution.py:846
  113.2 2.0 %collective-permute-start.40 = (bf16[320,128]{1,0:T(8,128)(2,1)S(1)}, bf16[320,128]{1,0:T(8,128)(2,1)S(1)}, u32[]{:S(2)}, u32[]{:S(2)}) collective-permute-start(bf16[320,128]{1,0:T(8,128)(2,1)S(1)} %get-tuple-element.144), channel_id=1, source_target_pairs={{0,2},{1,3},{2,0},{3,1},{4,6},{5,7},{6,4},{7,5},{8,10},{9,11},{10,... | collective-permute-start | bytes 245768 | tf_op jit(solution)/shard_map/ppermute | solution.py:846
  115.2 2.4 %collective-permute-start.41 = (bf16[320,128]{1,0:T(8,128)(2,1)S(1)}, bf16[320,128]{1,0:T(8,128)(2,1)S(1)}, u32[]{:S(2)}, u32[]{:S(2)}) collective-permute-start(bf16[320,128]{1,0:T(8,128)(2,1)S(1)} %get-tuple-element.145), channel_id=1, source_target_pairs={{0,3},{1,2},{2,1},{3,0},{4,7},{5,6},{6,5},{7,4},{8,11},{9,10},{10,... | collective-permute-start | bytes 245768 | tf_op jit(solution)/shard_map/ppermute | solution.py:846
  117.6 1.8 %collective-permute-done.39.one_ref = bf16[320,128]{1,0:T(8,128)(2,1)S(1)} collective-permute-done((bf16[320,128]{1,0:T(8,128)(2,1)S(1)}, bf16[320,128]{1,0:T(8,128)(2,1)S(1)}, u32[]{:S(2)}, u32[]{:S(2)}) %collective-permute-start.39) | collective-permute-done | bytes 81952 | tf_op jit(solution)/shard_map/ppermute | solution.py:846
  119.4 2.2 %collective-permute-done.41.three_ref = bf16[320,128]{1,0:T(8,128)(2,1)S(1)} collective-permute-done((bf16[320,128]{1,0:T(8,128)(2,1)S(1)}, bf16[320,128]{1,0:T(8,128)(2,1)S(1)}, u32[]{:S(2)}, u32[]{:S(2)}) %collective-permute-start.41) | collective-permute-done | bytes 81952 | tf_op jit(solution)/shard_map/ppermute | solution.py:846
  122.3 2.0 %shard_map.99 = f32[1024,512]{1,0:T(8,128)} custom-call(f32[512,512]{1,0:T(8,128)S(1)} %get-tuple-element.101.grad_a_ref, f32[512,512]{1,0:T(8,128)S(1)} %get-tuple-element.109.grad_b_ref, bf16[1024,512]{1,0:T(8,128)(2,1)S(1)} %get-tuple-element.83.masked_ref, s32[8,1024]{1,0:T(8,128)S(1)} %bitcast.7, f32[8,512]{1,0:T(8,128)S(1)} %get-tuple-element.86.entry_ref, ...), custom_call_target="tpu_custom_call" | custom-call | flops 1048576 | bytes 1024 | tf_op jit(solution)/shard_map/pallas_call | solution.py:261
  (76 shorter events, 21.5 us)
Async XLA Ops:
  2.7 5.7 %collective-permute-start = (bf16[320,128]{1,0:T(8,128)(2,1)S(1)}, bf16[320,128]{1,0:T(8,128)(2,1)S(1)}, u32[]{:S(2)}, u32[]{:S(2)}) collective-permute-start(bf16[320,128]{1,0:T(8,128)(2,1)S(1)} %get-tuple-element.78.refs_0_), channel_id=1, source_target_pairs={{0,1},{1,0},{2,3},{3,2},{4,5},{5,4},{6,7},{7,6},{8,9},{9,8},{10,11... | collective-permute-start | bytes 245768 | tf_op jit(solution)/shard_map/ppermute | solution.py:846
  5.8 9.2 %collective-permute-start.1 = (bf16[320,128]{1,0:T(8,128)(2,1)S(1)}, bf16[320,128]{1,0:T(8,128)(2,1)S(1)}, u32[]{:S(2)}, u32[]{:S(2)}) collective-permute-start(bf16[320,128]{1,0:T(8,128)(2,1)S(1)} %get-tuple-element.78.refs_0_), channel_id=1, source_target_pairs={{0,2},{1,3},{2,0},{3,1},{4,6},{5,7},{6,4},{7,5},{8,10},{9,11},{10,... | collective-permute-start | bytes 245768 | tf_op jit(solution)/shard_map/ppermute | solution.py:846
  8.4 6.6 %collective-permute-start.2 = (bf16[320,128]{1,0:T(8,128)(2,1)S(1)}, bf16[320,128]{1,0:T(8,128)(2,1)S(1)}, u32[]{:S(2)}, u32[]{:S(2)}) collective-permute-start(bf16[320,128]{1,0:T(8,128)(2,1)S(1)} %get-tuple-element.78.refs_0_), channel_id=1, source_target_pairs={{0,3},{1,2},{2,1},{3,0},{4,7},{5,6},{6,5},{7,4},{8,11},{9,10},{10,... | collective-permute-start | bytes 245768 | tf_op jit(solution)/shard_map/ppermute | solution.py:846
  15.1 11.2 %collective-permute-start.6 = (bf16[2,320,128]{2,1,0:T(8,128)(2,1)S(1)}, bf16[2,320,128]{2,1,0:T(8,128)(2,1)S(1)}, u32[]{:S(2)}, u32[]{:S(2)}) collective-permute-start(bf16[2,320,128]{2,1,0:T(8,128)(2,1)S(1)} %get-tuple-element.79.rest_0_), channel_id=1, source_target_pairs={{0,16},{4,20},{8,24},{12,28},{16,0},{20,4},{24,8},{28,12},{1,17},{... | collective-permute-start | bytes 491528 | tf_op jit(solution)/shard_map/ppermute | solution.py:846
  16.6 10.2 %collective-permute-start.8 = (bf16[2,320,128]{2,1,0:T(8,128)(2,1)S(1)}, bf16[2,320,128]{2,1,0:T(8,128)(2,1)S(1)}, u32[]{:S(2)}, u32[]{:S(2)}) collective-permute-start(bf16[2,320,128]{2,1,0:T(8,128)(2,1)S(1)} %get-tuple-element.81.rest_1_), channel_id=1, source_target_pairs={{0,8},{4,12},{8,0},{12,4},{16,24},{20,28},{24,16},{28,20},{1,9},{5... | collective-permute-start | bytes 491528 | tf_op jit(solution)/shard_map/ppermute | solution.py:846
  18.1 6.1 %collective-permute-start.5 = (bf16[224,128]{1,0:T(8,128)(2,1)S(1)}, bf16[224,128]{1,0:T(8,128)(2,1)S(1)}, u32[]{:S(2)}, u32[]{:S(2)}) collective-permute-start(bf16[224,128]{1,0:T(8,128)(2,1)S(1)} %get-tuple-element.80.refs_0_), channel_id=1, source_target_pairs={{0,3},{1,2},{2,1},{3,0},{4,7},{5,6},{6,5},{7,4},{8,11},{9,10},{10,... | collective-permute-start | bytes 172040 | tf_op jit(solution)/shard_map/ppermute | solution.py:846
  20.6 4.3 %collective-permute-start.3 = (bf16[224,128]{1,0:T(8,128)(2,1)S(1)}, bf16[224,128]{1,0:T(8,128)(2,1)S(1)}, u32[]{:S(2)}, u32[]{:S(2)}) collective-permute-start(bf16[224,128]{1,0:T(8,128)(2,1)S(1)} %get-tuple-element.80.refs_0_), channel_id=1, source_target_pairs={{0,1},{1,0},{2,3},{3,2},{4,5},{5,4},{6,7},{7,6},{8,9},{9,8},{10,11... | collective-permute-start | bytes 172040 | tf_op jit(solution)/shard_map/ppermute | solution.py:846
  21.1 5.1 %collective-permute-start.4 = (bf16[224,128]{1,0:T(8,128)(2,1)S(1)}, bf16[224,128]{1,0:T(8,128)(2,1)S(1)}, u32[]{:S(2)}, u32[]{:S(2)}) collective-permute-start(bf16[224,128]{1,0:T(8,128)(2,1)S(1)} %get-tuple-element.80.refs_0_), channel_id=1, source_target_pairs={{0,2},{1,3},{2,0},{3,1},{4,6},{5,7},{6,4},{7,5},{8,10},{9,11},{10,... | collective-permute-start | bytes 172040 | tf_op jit(solution)/shard_map/ppermute | solution.py:846
  24.2 5.5 %collective-permute-start.12 = (bf16[2,320,128]{2,1,0:T(8,128)(2,1)S(1)}, bf16[2,320,128]{2,1,0:T(8,128)(2,1)S(1)}, u32[]{:S(2)}, u32[]{:S(2)}) collective-permute-start(bf16[2,320,128]{2,1,0:T(8,128)(2,1)S(1)} %get-tuple-element.79.rest_0_), channel_id=1, source_target_pairs={{0,8},{4,12},{8,0},{12,4},{16,24},{20,28},{24,16},{28,20},{1,9},{5... | collective-permute-start | bytes 491528 | tf_op jit(solution)/shard_map/ppermute | solution.py:846
  24.9 5.9 %collective-permute-start.15 = (bf16[2,320,128]{2,1,0:T(8,128)(2,1)S(1)}, bf16[2,320,128]{2,1,0:T(8,128)(2,1)S(1)}, u32[]{:S(2)}, u32[]{:S(2)}) collective-permute-start(bf16[2,320,128]{2,1,0:T(8,128)(2,1)S(1)} %get-tuple-element.81.rest_1_), channel_id=1, source_target_pairs={{0,16},{4,20},{8,24},{12,28},{16,0},{20,4},{24,8},{28,12},{1,17},{... | collective-permute-start | bytes 491528 | tf_op jit(solution)/shard_map/ppermute | solution.py:846
  26.2 4.5 %collective-permute-start.10 = (bf16[2,320,128]{2,1,0:T(8,128)(2,1)S(1)}, bf16[2,320,128]{2,1,0:T(8,128)(2,1)S(1)}, u32[]{:S(2)}, u32[]{:S(2)}) collective-permute-start(bf16[2,320,128]{2,1,0:T(8,128)(2,1)S(1)} %get-tuple-element.79.rest_0_), channel_id=1, source_target_pairs={{0,4},{4,0},{8,12},{12,8},{16,20},{20,16},{24,28},{28,24},{1,5},{5... | collective-permute-start | bytes 491528 | tf_op jit(solution)/shard_map/ppermute | solution.py:846
  26.2 6.8 %collective-permute-start.7 = (bf16[2,320,128]{2,1,0:T(8,128)(2,1)S(1)}, bf16[2,320,128]{2,1,0:T(8,128)(2,1)S(1)}, u32[]{:S(2)}, u32[]{:S(2)}) collective-permute-start(bf16[2,320,128]{2,1,0:T(8,128)(2,1)S(1)} %collective-permute-done.6.rest_8_), channel_id=1, source_target_pairs={{0,8},{4,12},{8,0},{12,4},{16,24},{20,28},{24,16},{28,20},{1,9},{5... | collective-permute-start | bytes 491528 | tf_op jit(solution)/shard_map/ppermute | solution.py:846
  26.8 6.9 %collective-permute-start.9 = (bf16[2,320,128]{2,1,0:T(8,128)(2,1)S(1)}, bf16[2,320,128]{2,1,0:T(8,128)(2,1)S(1)}, u32[]{:S(2)}, u32[]{:S(2)}) collective-permute-start(bf16[2,320,128]{2,1,0:T(8,128)(2,1)S(1)} %collective-permute-done.8.rest_5_), channel_id=1, source_target_pairs={{0,16},{4,20},{8,24},{12,28},{16,0},{20,4},{24,8},{28,12},{1,17},{... | collective-permute-start | bytes 491528 | tf_op jit(solution)/shard_map/ppermute | solution.py:846
  30.7 4.4 %collective-permute-start.16 = (bf16[2,320,128]{2,1,0:T(8,128)(2,1)S(1)}, bf16[2,320,128]{2,1,0:T(8,128)(2,1)S(1)}, u32[]{:S(2)}, u32[]{:S(2)}) collective-permute-start(bf16[2,320,128]{2,1,0:T(8,128)(2,1)S(1)} %collective-permute-done.6.rest_8_), channel_id=1, source_target_pairs={{0,4},{4,0},{8,12},{12,8},{16,20},{20,16},{24,28},{28,24},{1,5},{5... | collective-permute-start | bytes 491528 | tf_op jit(solution)/shard_map/ppermute | solution.py:846
  30.8 5.9 %collective-permute-start.13 = (bf16[2,320,128]{2,1,0:T(8,128)(2,1)S(1)}, bf16[2,320,128]{2,1,0:T(8,128)(2,1)S(1)}, u32[]{:S(2)}, u32[]{:S(2)}) collective-permute-start(bf16[2,320,128]{2,1,0:T(8,128)(2,1)S(1)} %collective-permute-done.12.rest_4_), channel_id=1, source_target_pairs={{0,4},{4,0},{8,12},{12,8},{16,20},{20,16},{24,28},{28,24},{1,5},{5... | collective-permute-start | bytes 491528 | tf_op jit(solution)/shard_map/ppermute | solution.py:846
  33.7 15.8 %collective-permute-start.25 = (bf16[4,224,128]{2,1,0:T(8,128)(2,1)S(1)}, bf16[4,224,128]{2,1,0:T(8,128)(2,1)S(1)}, u32[]{:S(2)}, u32[]{:S(2)}) collective-permute-start(bf16[4,224,128]{2,1,0:T(8,128)(2,1)S(1)} %shard_map.86.rest_0_), channel_id=1, source_target_pairs={{0,24},{4,28},{8,16},{12,20},{16,8},{20,12},{24,0},{28,4},{1,25},{... | collective-permute-start | bytes 688136 | tf_op jit(solution)/shard_map/ppermute | solution.py:846
  35.1 14.7 %collective-permute-start.23 = (bf16[4,224,128]{2,1,0:T(8,128)(2,1)S(1)}, bf16[4,224,128]{2,1,0:T(8,128)(2,1)S(1)}, u32[]{:S(2)}, u32[]{:S(2)}) collective-permute-start(bf16[4,224,128]{2,1,0:T(8,128)(2,1)S(1)} %shard_map.86.rest_0_), channel_id=1, source_target_pairs={{0,16},{4,20},{8,24},{12,28},{16,0},{20,4},{24,8},{28,12},{1,17},{... | collective-permute-start | bytes 688136 | tf_op jit(solution)/shard_map/ppermute | solution.py:846
  36.6 13.4 %collective-permute-start.21 = (bf16[4,224,128]{2,1,0:T(8,128)(2,1)S(1)}, bf16[4,224,128]{2,1,0:T(8,128)(2,1)S(1)}, u32[]{:S(2)}, u32[]{:S(2)}) collective-permute-start(bf16[4,224,128]{2,1,0:T(8,128)(2,1)S(1)} %shard_map.86.rest_0_), channel_id=1, source_target_pairs={{0,8},{4,12},{8,0},{12,4},{16,24},{20,28},{24,16},{28,20},{1,9},{5... | collective-permute-start | bytes 688136 | tf_op jit(solution)/shard_map/ppermute | solution.py:846
  72.1 5.6 %collective-permute-start.27 = (bf16[16,224,128]{2,1,0:T(8,128)(2,1)S(1)}, bf16[16,224,128]{2,1,0:T(8,128)(2,1)S(1)}, u32[]{:S(2)}, u32[]{:S(2)}) collective-permute-start(bf16[16,224,128]{2,1,0:T(8,128)(2,1)S(1)} %get-tuple-element.105), channel_id=1, source_target_pairs={{0,4},{4,0},{8,12},{12,8},{16,20},{20,16},{24,28},{28,24},{1,5},{5... | collective-permute-start | bytes 2752520 | tf_op jit(solution)/shard_map/ppermute | solution.py:846
  78.0 13.2 %collective-permute-start.28 = (bf16[4,224,128]{2,1,0:T(8,128)(2,1)S(1)}, bf16[4,224,128]{2,1,0:T(8,128)(2,1)S(1)}, u32[]{:S(2)}, u32[]{:S(2)}) collective-permute-start(bf16[4,224,128]{2,1,0:T(8,128)(2,1)S(1)} %get-tuple-element.122), channel_id=1, source_target_pairs={{0,8},{4,12},{8,0},{12,4},{16,24},{20,28},{24,16},{28,20},{1,9},{5... | collective-permute-start | bytes 688136 | tf_op jit(solution)/shard_map/ppermute | solution.py:846
  79.4 12.4 %collective-permute-start.29 = (bf16[4,224,128]{2,1,0:T(8,128)(2,1)S(1)}, bf16[4,224,128]{2,1,0:T(8,128)(2,1)S(1)}, u32[]{:S(2)}, u32[]{:S(2)}) collective-permute-start(bf16[4,224,128]{2,1,0:T(8,128)(2,1)S(1)} %get-tuple-element.123), channel_id=1, source_target_pairs={{0,16},{4,20},{8,24},{12,28},{16,0},{20,4},{24,8},{28,12},{1,17},{... | collective-permute-start | bytes 688136 | tf_op jit(solution)/shard_map/ppermute | solution.py:846
  79.9 11.9 %collective-permute-start.30 = (bf16[4,224,128]{2,1,0:T(8,128)(2,1)S(1)}, bf16[4,224,128]{2,1,0:T(8,128)(2,1)S(1)}, u32[]{:S(2)}, u32[]{:S(2)}) collective-permute-start(bf16[4,224,128]{2,1,0:T(8,128)(2,1)S(1)} %get-tuple-element.124), channel_id=1, source_target_pairs={{0,24},{4,28},{8,16},{12,20},{16,8},{20,12},{24,0},{28,4},{1,25},{... | collective-permute-start | bytes 688136 | tf_op jit(solution)/shard_map/ppermute | solution.py:846
  95.3 11.5 %collective-permute-start.35 = (bf16[4,320,128]{2,1,0:T(8,128)(2,1)S(1)}, bf16[4,320,128]{2,1,0:T(8,128)(2,1)S(1)}, u32[]{:S(2)}, u32[]{:S(2)}) collective-permute-start(bf16[4,320,128]{2,1,0:T(8,128)(2,1)S(1)} %get-tuple-element.133), channel_id=1, source_target_pairs={{0,16},{4,20},{8,24},{12,28},{16,0},{20,4},{24,8},{28,12},{1,17},{... | collective-permute-start | bytes 983048 | tf_op jit(solution)/shard_map/ppermute | solution.py:846
  95.8 10.9 %collective-permute-start.36 = (bf16[4,320,128]{2,1,0:T(8,128)(2,1)S(1)}, bf16[4,320,128]{2,1,0:T(8,128)(2,1)S(1)}, u32[]{:S(2)}, u32[]{:S(2)}) collective-permute-start(bf16[4,320,128]{2,1,0:T(8,128)(2,1)S(1)} %get-tuple-element.134), channel_id=1, source_target_pairs={{0,8},{4,12},{8,0},{12,4},{16,24},{20,28},{24,16},{28,20},{1,9},{5... | collective-permute-start | bytes 983048 | tf_op jit(solution)/shard_map/ppermute | solution.py:846
  97.1 4.8 %collective-permute-start.32 = (bf16[224,128]{1,0:T(8,128)(2,1)S(1)}, bf16[224,128]{1,0:T(8,128)(2,1)S(1)}, u32[]{:S(2)}, u32[]{:S(2)}) collective-permute-start(bf16[224,128]{1,0:T(8,128)(2,1)S(1)} %get-tuple-element.128), channel_id=1, source_target_pairs={{0,1},{1,0},{2,3},{3,2},{4,5},{5,4},{6,7},{7,6},{8,9},{9,8},{10,11... | collective-permute-start | bytes 172040 | tf_op jit(solution)/shard_map/ppermute | solution.py:846
  98.1 6.5 %collective-permute-start.33 = (bf16[224,128]{1,0:T(8,128)(2,1)S(1)}, bf16[224,128]{1,0:T(8,128)(2,1)S(1)}, u32[]{:S(2)}, u32[]{:S(2)}) collective-permute-start(bf16[224,128]{1,0:T(8,128)(2,1)S(1)} %get-tuple-element.129), channel_id=1, source_target_pairs={{0,2},{1,3},{2,0},{3,1},{4,6},{5,7},{6,4},{7,5},{8,10},{9,11},{10,... | collective-permute-start | bytes 172040 | tf_op jit(solution)/shard_map/ppermute | solution.py:846
  100.1 6.0 %collective-permute-start.34 = (bf16[224,128]{1,0:T(8,128)(2,1)S(1)}, bf16[224,128]{1,0:T(8,128)(2,1)S(1)}, u32[]{:S(2)}, u32[]{:S(2)}) collective-permute-start(bf16[224,128]{1,0:T(8,128)(2,1)S(1)} %get-tuple-element.130), channel_id=1, source_target_pairs={{0,3},{1,2},{2,1},{3,0},{4,7},{5,6},{6,5},{7,4},{8,11},{9,10},{10,... | collective-permute-start | bytes 172040 | tf_op jit(solution)/shard_map/ppermute | solution.py:846
  106.9 5.4 %collective-permute-start.37 = (bf16[2,320,128]{2,1,0:T(8,128)(2,1)S(1)}, bf16[2,320,128]{2,1,0:T(8,128)(2,1)S(1)}, u32[]{:S(2)}, u32[]{:S(2)}) collective-permute-start(bf16[2,320,128]{2,1,0:T(8,128)(2,1)S(1)} %get-tuple-element.138), channel_id=1, source_target_pairs={{0,8},{4,12},{8,0},{12,4},{16,24},{20,28},{24,16},{28,20},{1,9},{5... | collective-permute-start | bytes 491528 | tf_op jit(solution)/shard_map/ppermute | solution.py:846
  107.8 5.3 %collective-permute-start.38 = (bf16[2,320,128]{2,1,0:T(8,128)(2,1)S(1)}, bf16[2,320,128]{2,1,0:T(8,128)(2,1)S(1)}, u32[]{:S(2)}, u32[]{:S(2)}) collective-permute-start(bf16[2,320,128]{2,1,0:T(8,128)(2,1)S(1)} %get-tuple-element.139), channel_id=1, source_target_pairs={{0,16},{4,20},{8,24},{12,28},{16,0},{20,4},{24,8},{28,12},{1,17},{... | collective-permute-start | bytes 491528 | tf_op jit(solution)/shard_map/ppermute | solution.py:846
  113.2 6.3 %collective-permute-start.39 = (bf16[320,128]{1,0:T(8,128)(2,1)S(1)}, bf16[320,128]{1,0:T(8,128)(2,1)S(1)}, u32[]{:S(2)}, u32[]{:S(2)}) collective-permute-start(bf16[320,128]{1,0:T(8,128)(2,1)S(1)} %get-tuple-element.143), channel_id=1, source_target_pairs={{0,1},{1,0},{2,3},{3,2},{4,5},{5,4},{6,7},{7,6},{8,9},{9,8},{10,11... | collective-permute-start | bytes 245768 | tf_op jit(solution)/shard_map/ppermute | solution.py:846
  113.2 6.2 %collective-permute-start.40 = (bf16[320,128]{1,0:T(8,128)(2,1)S(1)}, bf16[320,128]{1,0:T(8,128)(2,1)S(1)}, u32[]{:S(2)}, u32[]{:S(2)}) collective-permute-start(bf16[320,128]{1,0:T(8,128)(2,1)S(1)} %get-tuple-element.144), channel_id=1, source_target_pairs={{0,2},{1,3},{2,0},{3,1},{4,6},{5,7},{6,4},{7,5},{8,10},{9,11},{10,... | collective-permute-start | bytes 245768 | tf_op jit(solution)/shard_map/ppermute | solution.py:846
  115.2 6.3 %collective-permute-start.41 = (bf16[320,128]{1,0:T(8,128)(2,1)S(1)}, bf16[320,128]{1,0:T(8,128)(2,1)S(1)}, u32[]{:S(2)}, u32[]{:S(2)}) collective-permute-start(bf16[320,128]{1,0:T(8,128)(2,1)S(1)} %get-tuple-element.145), channel_id=1, source_target_pairs={{0,3},{1,2},{2,1},{3,0},{4,7},{5,6},{6,5},{7,4},{8,11},{9,10},{10,... | collective-permute-start | bytes 245768 | tf_op jit(solution)/shard_map/ppermute | solution.py:846
  (14 other events, 61.1 us)

commit v4 on v3

--- a/solution.py
+++ b/solution.py
@@ -252,12 +252,14 @@
     return pl.BlockSpec(memory_space=pltpu.SMEM)
 
 
-def run_kernel(kernel, inputs, out_shape, scratch, limit, flops, scalar=True, spec=None):
+def run_kernel(
+    kernel, inputs, out_shape, scratch, limit, flops, scalar=True, spec=None, out_spec=None
+):
     specs = [spec or full_spec()] * len(inputs)
     if scalar:
         specs[0] = scalar_spec()
     several = isinstance(out_shape, (list, tuple))
-    out_specs = [full_spec()] * len(out_shape) if several else full_spec()
+    out_specs = [full_spec()] * len(out_shape) if several else out_spec or full_spec()
     return pl.pallas_call(
         kernel,
         in_specs=specs,
@@ -590,15 +592,14 @@
             post_grad = norm_backward(
                 out_grad * small_ref[2, e : e + 1, :], normal, scale_ref[e], means_ref[...]
             )
-            post_grad = post_grad.astype(BF16)
-            post_grad_ref[e, now, :] = post_grad
-            g_small_ref[1, e : e + 1, :] += column_sum(post_grad.astype(F32))
+            post_grad_ref[e, now, :] = post_grad.astype(BF16)
+            g_small_ref[1, e : e + 1, :] += column_sum(post_grad)
 
         def active_half(e):
             act_grad = mm_nt(post_grad_ref[e, now, :], w_out_ref[e])
-            pre_grad = (act_grad * slope_ref[:, spot(e)]).astype(BF16)
-            pre_grad_ref[now, spot(e)] = pre_grad
-            g_small_ref[0, e : e + 1, :] += column_sum(pre_grad.astype(F32))
+            pre_grad = act_grad * slope_ref[:, spot(e)]
+            pre_grad_ref[now, spot(e)] = pre_grad.astype(BF16)
+            g_small_ref[0, e : e + 1, :] += column_sum(pre_grad)
 
         in_turn(norm_half, active_half)
         for index in range(3):
@@ -729,15 +730,15 @@
                 normal,
                 scale_ref[e, now, :],
                 means_ref[...],
-            ).astype(BF16)
-            post_grad_ref[e, here, :] = post_grad
-            g_small_ref[1, e : e + 1, :] += column_sum(post_grad.astype(F32))
+            )
+            post_grad_ref[e, here, :] = post_grad.astype(BF16)
+            g_small_ref[1, e : e + 1, :] += column_sum(post_grad)
 
         def active_half(e):
             act_grad = mm_nt(post_grad_ref[e, here, :], w_out_ref[e])
-            pre_grad = (act_grad * slope_ref[e, now, :].astype(F32)).astype(BF16)
-            pre_grad_ref[here, spot(e)] = pre_grad
-            g_small_ref[0, e : e + 1, :] += column_sum(pre_grad.astype(F32))
+            pre_grad = act_grad * slope_ref[e, now, :].astype(F32)
+            pre_grad_ref[here, spot(e)] = pre_grad.astype(BF16)
+            g_small_ref[0, e : e + 1, :] += column_sum(pre_grad)
 
         in_turn(norm_half, active_half)
         level_grad = mm_nt(pre_grad_ref[here, :], w_in_ref[...]) + mm_nt(
@@ -826,19 +827,36 @@
 
 
 def input_kernel(
-    total_rows, grad_a_ref, grad_b_ref, masked_ref, presence_ref, entry_ref, sums_ref, out_ref
+    total_rows,
+    parts,
+    grad_a_ref,
+    grad_b_ref,
+    masked_ref,
+    presence_ref,
+    entry_ref,
+    sums_ref,
+    out_hbm,
+    out_ref,
+    sems,
 ):
-    width = masked_ref.shape[1]
-    mask = spread_presence(presence_ref[...], width)
+    rows, width = masked_ref.shape
     inv_scale = entry_ref[1:2, :]
-    gain = entry_ref[2:3, :]
+    factor = inv_scale * entry_ref[2:3, :]
     cross = sums_ref[0:1, :] * (1.0 / total_rows)
     plain = sums_ref[1:2, :] * (1.0 / total_rows)
-    half = grad_a_ref.shape[0]
-    for part, ref in enumerate((grad_a_ref, grad_b_ref)):
-        now = slice(part * half, (part + 1) * half)
+    each = rows // parts
+    copies = []
+    for part in range(parts):
+        now = pl.ds(part * each, each)
+        ref = grad_a_ref if part < parts // 2 else grad_b_ref
+        grad = ref[pl.ds(part % (parts // 2) * each, each), :]
+        mask = spread_presence(presence_ref[:, now], width)
         normed = (masked_ref[now, :].astype(F32) - entry_ref[0:1, :]) * inv_scale
-        out_ref[now, :] = mask[now] * ((inv_scale * gain) * (ref[...] - plain - normed * cross))
+        out_ref[now, :] = mask * (factor * (grad - plain - normed * cross))
+        copies.append(pltpu.make_async_copy(out_ref.at[now], out_hbm.at[now], sems.at[part]))
+        copies[-1].start()
+    for copy in copies:
+        copy.wait()
 
 
 def xor_permute(value, axis, bit):
@@ -1140,7 +1158,7 @@
             pltpu.VMEM((2 * LANES, 8 * LANES), BF16),
             pltpu.VMEM((2 * H, 2 * LANES), BF16),
         ],
-        32,
+        28,
         rows * 6 * 2 * H * H * 2 * 3,
     )
     def backward(part, *before):
@@ -1270,14 +1288,16 @@
             scalar=True,
         )
 
+    parts = 8 if rows % 1024 == 0 else 2
     input_grad = run_kernel(
-        functools.partial(input_kernel, float(total_rows)),
+        functools.partial(input_kernel, float(total_rows), parts),
         [grad_a, grad_b, masked, fields, entry, sums],
         shape((rows, width), F32),
-        [],
+        [pltpu.VMEM((rows, width), F32), pltpu.SemaphoreType.DMA((parts,))],
         8,
         rows * width * 10,
         scalar=False,
+        out_spec=pl.BlockSpec(memory_space=pltpu.HBM),
     )
     return (towers, input_grad, first_grad.reshape(-1), second_grad.reshape(-1))
 

time: 124 us -> 122 us (0.984)
  local copies, waits for them, and re-layouts: 1.64 us -> 0.01 us
    unnamed x8 -> x4, local copies, waits for them, and re-layouts: 1.64 us -> 0.01 us
where the time goes in v4:
time: 122 us
  Pallas kernels  49.2 us (40%)
  starting transfers between devices  38.9 us (32%)
  waiting for transfers between devices  33 us (27%)
    pallas_call x16, Pallas kernels, run_kernel(): pl.pallas_call(kernel, in_specs=specs, out_specs=out_specs, out_shape=out...  49.2 us
    ppermute x42, starting transfers between devices, xor_permute(): lax.ppermute(value, axis, [(index, index ^ bit) for index in range(size)])  38.9 us
    ppermute x42, waiting for transfers between devices, xor_permute(): lax.ppermute(value, axis, [(index, index ^ bit) for index in range(size)])  33 us
  transfers between devices with their start and end apart: 42, of which 23 were waited for; matrix products, arithmetic and copies ran while one was open for 0% of the time, Pallas kernels for 20%

profile of v4, /device:TPU:0, one launch (start us, length us, event | category | flops | bytes accessed | tf_op | source)
XLA Modules:
  0.0 122.1 jit_solution(9583810508717301873)
XLA Ops:
  0.6 2.1 %shard_map.84 = (bf16[1024,512]{1,0:T(8,128)(2,1)S(1)}, bf16[320,128]{1,0:T(8,128)(2,1)S(1)}, bf16[224,128]{1,0:T(8,128)(2,1)S(1)}) custom-call(s32[1]{0:T(128)} %bitcast.me_ref, bf16[1024,512]{1,0:T(8,128)(2,1)} %features_hbm.1, s32[8,1024]{1,0:T(8,128)} %bitcast.6, bf16[292,128]{1,0:T(8,128)(2,1)} %bitcast.9, bf16[215,128]{1,0:T(8,128)(2,1)} %bitcast.10), custom_call_target="tpu_custom_call" | custom-call | flops 1048576 | bytes 1024 | tf_op jit(solution)/shard_map/pallas_call | solution.py:263
  2.7 3.1 %collective-permute-start = (bf16[320,128]{1,0:T(8,128)(2,1)S(1)}, bf16[320,128]{1,0:T(8,128)(2,1)S(1)}, u32[]{:S(2)}, u32[]{:S(2)}) collective-permute-start(bf16[320,128]{1,0:T(8,128)(2,1)S(1)} %get-tuple-element.78.refs_0_), channel_id=1, source_target_pairs={{0,1},{1,0},{2,3},{3,2},{4,5},{5,4},{6,7},{7,6},{8,9},{9,8},{10,11... | collective-permute-start | bytes 245768 | tf_op jit(solution)/shard_map/ppermute | solution.py:864
  5.8 2.6 %collective-permute-start.1 = (bf16[320,128]{1,0:T(8,128)(2,1)S(1)}, bf16[320,128]{1,0:T(8,128)(2,1)S(1)}, u32[]{:S(2)}, u32[]{:S(2)}) collective-permute-start(bf16[320,128]{1,0:T(8,128)(2,1)S(1)} %get-tuple-element.78.refs_0_), channel_id=1, source_target_pairs={{0,2},{1,3},{2,0},{3,1},{4,6},{5,7},{6,4},{7,5},{8,10},{9,11},{10,... | collective-permute-start | bytes 245768 | tf_op jit(solution)/shard_map/ppermute | solution.py:864
  8.4 6.6 %collective-permute-done.1.refs_2_ = bf16[320,128]{1,0:T(8,128)(2,1)S(1)} collective-permute-done((bf16[320,128]{1,0:T(8,128)(2,1)S(1)}, bf16[320,128]{1,0:T(8,128)(2,1)S(1)}, u32[]{:S(2)}, u32[]{:S(2)}) %collective-permute-start.1) | collective-permute-done | bytes 81952 | tf_op jit(solution)/shard_map/ppermute | solution.py:864
  15.1 1.6 %collective-permute-start.6 = (bf16[2,320,128]{2,1,0:T(8,128)(2,1)S(1)}, bf16[2,320,128]{2,1,0:T(8,128)(2,1)S(1)}, u32[]{:S(2)}, u32[]{:S(2)}) collective-permute-start(bf16[2,320,128]{2,1,0:T(8,128)(2,1)S(1)} %get-tuple-element.79.rest_0_), channel_id=1, source_target_pairs={{0,16},{4,20},{8,24},{12,28},{16,0},{20,4},{24,8},{28,12},{1,17},{... | collective-permute-start | bytes 491528 | tf_op jit(solution)/shard_map/ppermute | solution.py:864
  16.6 1.5 %collective-permute-start.8 = (bf16[2,320,128]{2,1,0:T(8,128)(2,1)S(1)}, bf16[2,320,128]{2,1,0:T(8,128)(2,1)S(1)}, u32[]{:S(2)}, u32[]{:S(2)}) collective-permute-start(bf16[2,320,128]{2,1,0:T(8,128)(2,1)S(1)} %get-tuple-element.81.rest_1_), channel_id=1, source_target_pairs={{0,8},{4,12},{8,0},{12,4},{16,24},{20,28},{24,16},{28,20},{1,9},{5... | collective-permute-start | bytes 491528 | tf_op jit(solution)/shard_map/ppermute | solution.py:864
  18.1 2.5 %collective-permute-start.5 = (bf16[224,128]{1,0:T(8,128)(2,1)S(1)}, bf16[224,128]{1,0:T(8,128)(2,1)S(1)}, u32[]{:S(2)}, u32[]{:S(2)}) collective-permute-start(bf16[224,128]{1,0:T(8,128)(2,1)S(1)} %get-tuple-element.80.refs_0_), channel_id=1, source_target_pairs={{0,3},{1,2},{2,1},{3,0},{4,7},{5,6},{6,5},{7,4},{8,11},{9,10},{10,... | collective-permute-start | bytes 172040 | tf_op jit(solution)/shard_map/ppermute | solution.py:864
  21.1 1.4 %collective-permute-start.4 = (bf16[224,128]{1,0:T(8,128)(2,1)S(1)}, bf16[224,128]{1,0:T(8,128)(2,1)S(1)}, u32[]{:S(2)}, u32[]{:S(2)}) collective-permute-start(bf16[224,128]{1,0:T(8,128)(2,1)S(1)} %get-tuple-element.80.refs_0_), channel_id=1, source_target_pairs={{0,2},{1,3},{2,0},{3,1},{4,6},{5,7},{6,4},{7,5},{8,10},{9,11},{10,... | collective-permute-start | bytes 172040 | tf_op jit(solution)/shard_map/ppermute | solution.py:864
  22.5 1.7 %collective-permute-done.5.refs_3_ = bf16[224,128]{1,0:T(8,128)(2,1)S(1)} collective-permute-done((bf16[224,128]{1,0:T(8,128)(2,1)S(1)}, bf16[224,128]{1,0:T(8,128)(2,1)S(1)}, u32[]{:S(2)}, u32[]{:S(2)}) %collective-permute-start.5) | collective-permute-done | bytes 57376 | tf_op jit(solution)/shard_map/ppermute | solution.py:864
  26.8 1.5 %collective-permute-start.9 = (bf16[2,320,128]{2,1,0:T(8,128)(2,1)S(1)}, bf16[2,320,128]{2,1,0:T(8,128)(2,1)S(1)}, u32[]{:S(2)}, u32[]{:S(2)}) collective-permute-start(bf16[2,320,128]{2,1,0:T(8,128)(2,1)S(1)} %collective-permute-done.8.rest_5_), channel_id=1, source_target_pairs={{0,16},{4,20},{8,24},{12,28},{16,0},{20,4},{24,8},{28,12},{1,17},{... | collective-permute-start | bytes 491528 | tf_op jit(solution)/shard_map/ppermute | solution.py:864
  31.3 1.8 %collective-permute-done.7.rest_12_ = bf16[2,320,128]{2,1,0:T(8,128)(2,1)S(1)} collective-permute-done((bf16[2,320,128]{2,1,0:T(8,128)(2,1)S(1)}, bf16[2,320,128]{2,1,0:T(8,128)(2,1)S(1)}, u32[]{:S(2)}, u32[]{:S(2)}) %collective-permute-start.7) | collective-permute-done | bytes 163872 | tf_op jit(solution)/shard_map/ppermute | solution.py:864
  33.7 1.4 %collective-permute-start.25 = (bf16[4,224,128]{2,1,0:T(8,128)(2,1)S(1)}, bf16[4,224,128]{2,1,0:T(8,128)(2,1)S(1)}, u32[]{:S(2)}, u32[]{:S(2)}) collective-permute-start(bf16[4,224,128]{2,1,0:T(8,128)(2,1)S(1)} %shard_map.86.rest_0_), channel_id=1, source_target_pairs={{0,24},{4,28},{8,16},{12,20},{16,8},{20,12},{24,0},{28,4},{1,25},{... | collective-permute-start | bytes 688136 | tf_op jit(solution)/shard_map/ppermute | solution.py:864
  35.1 1.5 %collective-permute-start.23 = (bf16[4,224,128]{2,1,0:T(8,128)(2,1)S(1)}, bf16[4,224,128]{2,1,0:T(8,128)(2,1)S(1)}, u32[]{:S(2)}, u32[]{:S(2)}) collective-permute-start(bf16[4,224,128]{2,1,0:T(8,128)(2,1)S(1)} %shard_map.86.rest_0_), channel_id=1, source_target_pairs={{0,16},{4,20},{8,24},{12,28},{16,0},{20,4},{24,8},{28,12},{1,17},{... | collective-permute-start | bytes 688136 | tf_op jit(solution)/shard_map/ppermute | solution.py:864
  38.9 8.7 %shard_map.87 = (bf16[1024,512]{1,0:T(8,128)(2,1)S(1)}, bf16[6,1024,256]{2,1,0:T(8,128)(2,1)S(1)}, bf16[6,1024,256]{2,1,0:T(8,128)(2,1)S(1)}, bf16[6,1024,256]{2...) custom-call(s32[1]{0:T(128)} %bitcast.me_ref, ...), custom_call_target="tpu_custom_call" | custom-call | flops 1048576 | bytes 1024 | tf_op jit(solution)/shard_map/pallas_call | solution.py:263
  50.2 20.2 %shard_map.88 = (f32[1024,128]{1,0:T(8,128)}, f32[3,1024,256]{2,1,0:T(8,128)S(1)}, bf16[16,224,128]{2,1,0:T(8,128)(2,1)S(1)}, bf16[16,224,128]{2,1,0:T(8,128)(2,1)S(1)}) custom-call(s32[1]{0:T(128)} %bitcast.me_ref, bf16[3,1024,256]{2,1,0:T(8,128)(2,1)S(1)} %get-tuple-element.84.mixed_ref, bf16[1024,128]{1,0:T(8,128)(2,1)S(1)} %copy-done, ...), custom_call_target="tpu_custom_call" | custom-call | flops 1048576 | bytes 1024 | tf_op jit(solution)/shard_map/pallas_call | solution.py:263
  70.6 5.1 %shard_map.89 = (f32[512,512]{1,0:T(8,128)S(1)}, f32[8,512]{1,0:T(8,128)S(1)}, f32[4,8,256]{2,1,0:T(8,128)S(1)}, bf16[512,128]{1,0:T(8,128)(2,1)S(1)}, bf16[6,51...) custom-call(f32[3,1024,256]{2,1,0:T(8,128)S(1)} %get-tuple-element.92.mixed_grad_ref, ...), custom_call_target="tpu_custom_call" | custom-call | flops 1048576 | bytes 1024 | tf_op jit(solution)/shard_map/pallas_call | solution.py:263
  76.0 1.4 %collective-permute-start.28 = (bf16[4,224,128]{2,1,0:T(8,128)(2,1)S(1)}, bf16[4,224,128]{2,1,0:T(8,128)(2,1)S(1)}, u32[]{:S(2)}, u32[]{:S(2)}) collective-permute-start(bf16[4,224,128]{2,1,0:T(8,128)(2,1)S(1)} %get-tuple-element.122), channel_id=1, source_target_pairs={{0,8},{4,12},{8,0},{12,4},{16,24},{20,28},{24,16},{28,20},{1,9},{5... | collective-permute-start | bytes 688136 | tf_op jit(solution)/shard_map/ppermute | solution.py:864
  77.9 1.6 %collective-permute-start.30 = (bf16[4,224,128]{2,1,0:T(8,128)(2,1)S(1)}, bf16[4,224,128]{2,1,0:T(8,128)(2,1)S(1)}, u32[]{:S(2)}, u32[]{:S(2)}) collective-permute-start(bf16[4,224,128]{2,1,0:T(8,128)(2,1)S(1)} %get-tuple-element.124), channel_id=1, source_target_pairs={{0,24},{4,28},{8,16},{12,20},{16,8},{20,12},{24,0},{28,4},{1,25},{... | collective-permute-start | bytes 688136 | tf_op jit(solution)/shard_map/ppermute | solution.py:864
  79.5 5.4 %shard_map.91 = (f32[512,512]{1,0:T(8,128)S(1)}, f32[8,512]{1,0:T(8,128)S(1)}, f32[4,8,256]{2,1,0:T(8,128)S(1)}, bf16[512,128]{1,0:T(8,128)(2,1)S(1)}, bf16[6,51...) custom-call(f32[3,1024,256]{2,1,0:T(8,128)S(1)} %get-tuple-element.92.mixed_grad_ref, ...), custom_call_target="tpu_custom_call" | custom-call | flops 1048576 | bytes 1024 | tf_op jit(solution)/shard_map/pallas_call | solution.py:263
  84.9 4.0 %shard_map.92 = (bf16[16,320,128]{2,1,0:T(8,128)(2,1)S(1)}, bf16[16,320,128]{2,1,0:T(8,128)(2,1)S(1)}) custom-call(s32[1]{0:T(128)} %bitcast.me_ref, bf16[1024,512]{1,0:T(8,128)(2,1)S(1)} %get-tuple-element.110.level_ref, bf16[6,1024,256]{2,1,0:T(8,128)(2,1)S(1)} %get-tuple-element.111.active_ref, f32[8,512]{1,0:T(8,128)S(1)} %get-tuple-element.112.sums_ref, ...), custom_call_target="tpu_custom_call" | custom-call | flops 1048576 | bytes 1024 | tf_op jit(solution)/shard_map/pallas_call | solution.py:263
  90.0 3.0 %collective-permute-done.31.got_ref = bf16[16,320,128]{2,1,0:T(8,128)(2,1)S(1)} collective-permute-done((bf16[16,320,128]{2,1,0:T(8,128)(2,1)S(1)}, bf16[16,320,128]{2,1,0:T(8,128)(2,1)S(1)}, u32[]{:S(2)}, u32[]{:S(2)}) %collective-permute-start.31) | collective-permute-done | bytes 1310752 | tf_op jit(solution)/shard_map/ppermute | solution.py:864
  96.1 2.0 %collective-permute-start.33 = (bf16[224,128]{1,0:T(8,128)(2,1)S(1)}, bf16[224,128]{1,0:T(8,128)(2,1)S(1)}, u32[]{:S(2)}, u32[]{:S(2)}) collective-permute-start(bf16[224,128]{1,0:T(8,128)(2,1)S(1)} %get-tuple-element.129), channel_id=1, source_target_pairs={{0,2},{1,3},{2,0},{3,1},{4,6},{5,7},{6,4},{7,5},{8,10},{9,11},{10,... | collective-permute-start | bytes 172040 | tf_op jit(solution)/shard_map/ppermute | solution.py:864
  98.1 1.3 %collective-permute-start.34 = (bf16[224,128]{1,0:T(8,128)(2,1)S(1)}, bf16[224,128]{1,0:T(8,128)(2,1)S(1)}, u32[]{:S(2)}, u32[]{:S(2)}) collective-permute-start(bf16[224,128]{1,0:T(8,128)(2,1)S(1)} %get-tuple-element.130), channel_id=1, source_target_pairs={{0,3},{1,2},{2,1},{3,0},{4,7},{5,6},{6,5},{7,4},{8,11},{9,10},{10,... | collective-permute-start | bytes 172040 | tf_op jit(solution)/shard_map/ppermute | solution.py:864
  99.9 2.7 %collective-permute-done.33.two_ref = bf16[224,128]{1,0:T(8,128)(2,1)S(1)} collective-permute-done((bf16[224,128]{1,0:T(8,128)(2,1)S(1)}, bf16[224,128]{1,0:T(8,128)(2,1)S(1)}, u32[]{:S(2)}, u32[]{:S(2)}) %collective-permute-start.33) | collective-permute-done | bytes 57376 | tf_op jit(solution)/shard_map/ppermute | solution.py:864
  102.6 1.5 %collective-permute-done.34.three_ref = bf16[224,128]{1,0:T(8,128)(2,1)S(1)} collective-permute-done((bf16[224,128]{1,0:T(8,128)(2,1)S(1)}, bf16[224,128]{1,0:T(8,128)(2,1)S(1)}, u32[]{:S(2)}, u32[]{:S(2)}) %collective-permute-start.34) | collective-permute-done | bytes 57376 | tf_op jit(solution)/shard_map/ppermute | solution.py:864
  105.8 1.5 %collective-permute-start.38 = (bf16[2,320,128]{2,1,0:T(8,128)(2,1)S(1)}, bf16[2,320,128]{2,1,0:T(8,128)(2,1)S(1)}, u32[]{:S(2)}, u32[]{:S(2)}) collective-permute-start(bf16[2,320,128]{2,1,0:T(8,128)(2,1)S(1)} %get-tuple-element.139), channel_id=1, source_target_pairs={{0,16},{4,20},{8,24},{12,28},{16,0},{20,4},{24,8},{28,12},{1,17},{... | collective-permute-start | bytes 491528 | tf_op jit(solution)/shard_map/ppermute | solution.py:864
  107.3 3.0 %collective-permute-done.37.got_one_ref = bf16[2,320,128]{2,1,0:T(8,128)(2,1)S(1)} collective-permute-done((bf16[2,320,128]{2,1,0:T(8,128)(2,1)S(1)}, bf16[2,320,128]{2,1,0:T(8,128)(2,1)S(1)}, u32[]{:S(2)}, u32[]{:S(2)}) %collective-permute-start.37) | collective-permute-done | bytes 163872 | tf_op jit(solution)/shard_map/ppermute | solution.py:864
  111.2 2.0 %collective-permute-start.40 = (bf16[320,128]{1,0:T(8,128)(2,1)S(1)}, bf16[320,128]{1,0:T(8,128)(2,1)S(1)}, u32[]{:S(2)}, u32[]{:S(2)}) collective-permute-start(bf16[320,128]{1,0:T(8,128)(2,1)S(1)} %get-tuple-element.144), channel_id=1, source_target_pairs={{0,2},{1,3},{2,0},{3,1},{4,6},{5,7},{6,4},{7,5},{8,10},{9,11},{10,... | collective-permute-start | bytes 245768 | tf_op jit(solution)/shard_map/ppermute | solution.py:864
  113.3 2.4 %collective-permute-start.41 = (bf16[320,128]{1,0:T(8,128)(2,1)S(1)}, bf16[320,128]{1,0:T(8,128)(2,1)S(1)}, u32[]{:S(2)}, u32[]{:S(2)}) collective-permute-start(bf16[320,128]{1,0:T(8,128)(2,1)S(1)} %get-tuple-element.145), channel_id=1, source_target_pairs={{0,3},{1,2},{2,1},{3,0},{4,7},{5,6},{6,5},{7,4},{8,11},{9,10},{10,... | collective-permute-start | bytes 245768 | tf_op jit(solution)/shard_map/ppermute | solution.py:864
  115.6 1.8 %collective-permute-done.39.one_ref = bf16[320,128]{1,0:T(8,128)(2,1)S(1)} collective-permute-done((bf16[320,128]{1,0:T(8,128)(2,1)S(1)}, bf16[320,128]{1,0:T(8,128)(2,1)S(1)}, u32[]{:S(2)}, u32[]{:S(2)}) %collective-permute-start.39) | collective-permute-done | bytes 81952 | tf_op jit(solution)/shard_map/ppermute | solution.py:864
  117.4 2.2 %collective-permute-done.41.three_ref = bf16[320,128]{1,0:T(8,128)(2,1)S(1)} collective-permute-done((bf16[320,128]{1,0:T(8,128)(2,1)S(1)}, bf16[320,128]{1,0:T(8,128)(2,1)S(1)}, u32[]{:S(2)}, u32[]{:S(2)}) %collective-permute-start.41) | collective-permute-done | bytes 81952 | tf_op jit(solution)/shard_map/ppermute | solution.py:864
  120.3 1.6 %shard_map.99 = f32[1024,512]{1,0:T(8,128)} custom-call(f32[512,512]{1,0:T(8,128)S(1)} %get-tuple-element.101.grad_a_ref, f32[512,512]{1,0:T(8,128)S(1)} %get-tuple-element.109.grad_b_ref, bf16[1024,512]{1,0:T(8,128)(2,1)S(1)} %get-tuple-element.83.masked_ref, s32[8,1024]{1,0:T(8,128)S(1)} %bitcast.7, f32[8,512]{1,0:T(8,128)S(1)} %get-tuple-element.86.entry_ref, ...), custom_call_target="tpu_custom_call" | custom-call | flops 1048576 | bytes 1024 | tf_op jit(solution)/shard_map/pallas_call | solution.py:263
  (72 shorter events, 20.5 us)
Async XLA Ops:
  2.7 5.7 %collective-permute-start = (bf16[320,128]{1,0:T(8,128)(2,1)S(1)}, bf16[320,128]{1,0:T(8,128)(2,1)S(1)}, u32[]{:S(2)}, u32[]{:S(2)}) collective-permute-start(bf16[320,128]{1,0:T(8,128)(2,1)S(1)} %get-tuple-element.78.refs_0_), channel_id=1, source_target_pairs={{0,1},{1,0},{2,3},{3,2},{4,5},{5,4},{6,7},{7,6},{8,9},{9,8},{10,11... | collective-permute-start | bytes 245768 | tf_op jit(solution)/shard_map/ppermute | solution.py:864
  5.8 9.2 %collective-permute-start.1 = (bf16[320,128]{1,0:T(8,128)(2,1)S(1)}, bf16[320,128]{1,0:T(8,128)(2,1)S(1)}, u32[]{:S(2)}, u32[]{:S(2)}) collective-permute-start(bf16[320,128]{1,0:T(8,128)(2,1)S(1)} %get-tuple-element.78.refs_0_), channel_id=1, source_target_pairs={{0,2},{1,3},{2,0},{3,1},{4,6},{5,7},{6,4},{7,5},{8,10},{9,11},{10,... | collective-permute-start | bytes 245768 | tf_op jit(solution)/shard_map/ppermute | solution.py:864
  8.4 6.6 %collective-permute-start.2 = (bf16[320,128]{1,0:T(8,128)(2,1)S(1)}, bf16[320,128]{1,0:T(8,128)(2,1)S(1)}, u32[]{:S(2)}, u32[]{:S(2)}) collective-permute-start(bf16[320,128]{1,0:T(8,128)(2,1)S(1)} %get-tuple-element.78.refs_0_), channel_id=1, source_target_pairs={{0,3},{1,2},{2,1},{3,0},{4,7},{5,6},{6,5},{7,4},{8,11},{9,10},{10,... | collective-permute-start | bytes 245768 | tf_op jit(solution)/shard_map/ppermute | solution.py:864
  15.1 11.2 %collective-permute-start.6 = (bf16[2,320,128]{2,1,0:T(8,128)(2,1)S(1)}, bf16[2,320,128]{2,1,0:T(8,128)(2,1)S(1)}, u32[]{:S(2)}, u32[]{:S(2)}) collective-permute-start(bf16[2,320,128]{2,1,0:T(8,128)(2,1)S(1)} %get-tuple-element.79.rest_0_), channel_id=1, source_target_pairs={{0,16},{4,20},{8,24},{12,28},{16,0},{20,4},{24,8},{28,12},{1,17},{... | collective-permute-start | bytes 491528 | tf_op jit(solution)/shard_map/ppermute | solution.py:864
  16.6 10.2 %collective-permute-start.8 = (bf16[2,320,128]{2,1,0:T(8,128)(2,1)S(1)}, bf16[2,320,128]{2,1,0:T(8,128)(2,1)S(1)}, u32[]{:S(2)}, u32[]{:S(2)}) collective-permute-start(bf16[2,320,128]{2,1,0:T(8,128)(2,1)S(1)} %get-tuple-element.81.rest_1_), channel_id=1, source_target_pairs={{0,8},{4,12},{8,0},{12,4},{16,24},{20,28},{24,16},{28,20},{1,9},{5... | collective-permute-start | bytes 491528 | tf_op jit(solution)/shard_map/ppermute | solution.py:864
  18.1 6.1 %collective-permute-start.5 = (bf16[224,128]{1,0:T(8,128)(2,1)S(1)}, bf16[224,128]{1,0:T(8,128)(2,1)S(1)}, u32[]{:S(2)}, u32[]{:S(2)}) collective-permute-start(bf16[224,128]{1,0:T(8,128)(2,1)S(1)} %get-tuple-element.80.refs_0_), channel_id=1, source_target_pairs={{0,3},{1,2},{2,1},{3,0},{4,7},{5,6},{6,5},{7,4},{8,11},{9,10},{10,... | collective-permute-start | bytes 172040 | tf_op jit(solution)/shard_map/ppermute | solution.py:864
  20.6 4.3 %collective-permute-start.3 = (bf16[224,128]{1,0:T(8,128)(2,1)S(1)}, bf16[224,128]{1,0:T(8,128)(2,1)S(1)}, u32[]{:S(2)}, u32[]{:S(2)}) collective-permute-start(bf16[224,128]{1,0:T(8,128)(2,1)S(1)} %get-tuple-element.80.refs_0_), channel_id=1, source_target_pairs={{0,1},{1,0},{2,3},{3,2},{4,5},{5,4},{6,7},{7,6},{8,9},{9,8},{10,11... | collective-permute-start | bytes 172040 | tf_op jit(solution)/shard_map/ppermute | solution.py:864
  21.1 5.1 %collective-permute-start.4 = (bf16[224,128]{1,0:T(8,128)(2,1)S(1)}, bf16[224,128]{1,0:T(8,128)(2,1)S(1)}, u32[]{:S(2)}, u32[]{:S(2)}) collective-permute-start(bf16[224,128]{1,0:T(8,128)(2,1)S(1)} %get-tuple-element.80.refs_0_), channel_id=1, source_target_pairs={{0,2},{1,3},{2,0},{3,1},{4,6},{5,7},{6,4},{7,5},{8,10},{9,11},{10,... | collective-permute-start | bytes 172040 | tf_op jit(solution)/shard_map/ppermute | solution.py:864
  24.2 5.5 %collective-permute-start.12 = (bf16[2,320,128]{2,1,0:T(8,128)(2,1)S(1)}, bf16[2,320,128]{2,1,0:T(8,128)(2,1)S(1)}, u32[]{:S(2)}, u32[]{:S(2)}) collective-permute-start(bf16[2,320,128]{2,1,0:T(8,128)(2,1)S(1)} %get-tuple-element.79.rest_0_), channel_id=1, source_target_pairs={{0,8},{4,12},{8,0},{12,4},{16,24},{20,28},{24,16},{28,20},{1,9},{5... | collective-permute-start | bytes 491528 | tf_op jit(solution)/shard_map/ppermute | solution.py:864
  24.9 5.9 %collective-permute-start.15 = (bf16[2,320,128]{2,1,0:T(8,128)(2,1)S(1)}, bf16[2,320,128]{2,1,0:T(8,128)(2,1)S(1)}, u32[]{:S(2)}, u32[]{:S(2)}) collective-permute-start(bf16[2,320,128]{2,1,0:T(8,128)(2,1)S(1)} %get-tuple-element.81.rest_1_), channel_id=1, source_target_pairs={{0,16},{4,20},{8,24},{12,28},{16,0},{20,4},{24,8},{28,12},{1,17},{... | collective-permute-start | bytes 491528 | tf_op jit(solution)/shard_map/ppermute | solution.py:864
  26.2 4.5 %collective-permute-start.10 = (bf16[2,320,128]{2,1,0:T(8,128)(2,1)S(1)}, bf16[2,320,128]{2,1,0:T(8,128)(2,1)S(1)}, u32[]{:S(2)}, u32[]{:S(2)}) collective-permute-start(bf16[2,320,128]{2,1,0:T(8,128)(2,1)S(1)} %get-tuple-element.79.rest_0_), channel_id=1, source_target_pairs={{0,4},{4,0},{8,12},{12,8},{16,20},{20,16},{24,28},{28,24},{1,5},{5... | collective-permute-start | bytes 491528 | tf_op jit(solution)/shard_map/ppermute | solution.py:864
  26.2 6.8 %collective-permute-start.7 = (bf16[2,320,128]{2,1,0:T(8,128)(2,1)S(1)}, bf16[2,320,128]{2,1,0:T(8,128)(2,1)S(1)}, u32[]{:S(2)}, u32[]{:S(2)}) collective-permute-start(bf16[2,320,128]{2,1,0:T(8,128)(2,1)S(1)} %collective-permute-done.6.rest_8_), channel_id=1, source_target_pairs={{0,8},{4,12},{8,0},{12,4},{16,24},{20,28},{24,16},{28,20},{1,9},{5... | collective-permute-start | bytes 491528 | tf_op jit(solution)/shard_map/ppermute | solution.py:864
  26.8 6.9 %collective-permute-start.9 = (bf16[2,320,128]{2,1,0:T(8,128)(2,1)S(1)}, bf16[2,320,128]{2,1,0:T(8,128)(2,1)S(1)}, u32[]{:S(2)}, u32[]{:S(2)}) collective-permute-start(bf16[2,320,128]{2,1,0:T(8,128)(2,1)S(1)} %collective-permute-done.8.rest_5_), channel_id=1, source_target_pairs={{0,16},{4,20},{8,24},{12,28},{16,0},{20,4},{24,8},{28,12},{1,17},{... | collective-permute-start | bytes 491528 | tf_op jit(solution)/shard_map/ppermute | solution.py:864
  30.7 4.4 %collective-permute-start.16 = (bf16[2,320,128]{2,1,0:T(8,128)(2,1)S(1)}, bf16[2,320,128]{2,1,0:T(8,128)(2,1)S(1)}, u32[]{:S(2)}, u32[]{:S(2)}) collective-permute-start(bf16[2,320,128]{2,1,0:T(8,128)(2,1)S(1)} %collective-permute-done.6.rest_8_), channel_id=1, source_target_pairs={{0,4},{4,0},{8,12},{12,8},{16,20},{20,16},{24,28},{28,24},{1,5},{5... | collective-permute-start | bytes 491528 | tf_op jit(solution)/shard_map/ppermute | solution.py:864
  30.8 5.9 %collective-permute-start.13 = (bf16[2,320,128]{2,1,0:T(8,128)(2,1)S(1)}, bf16[2,320,128]{2,1,0:T(8,128)(2,1)S(1)}, u32[]{:S(2)}, u32[]{:S(2)}) collective-permute-start(bf16[2,320,128]{2,1,0:T(8,128)(2,1)S(1)} %collective-permute-done.12.rest_4_), channel_id=1, source_target_pairs={{0,4},{4,0},{8,12},{12,8},{16,20},{20,16},{24,28},{28,24},{1,5},{5... | collective-permute-start | bytes 491528 | tf_op jit(solution)/shard_map/ppermute | solution.py:864
  33.7 14.3 %collective-permute-start.25 = (bf16[4,224,128]{2,1,0:T(8,128)(2,1)S(1)}, bf16[4,224,128]{2,1,0:T(8,128)(2,1)S(1)}, u32[]{:S(2)}, u32[]{:S(2)}) collective-permute-start(bf16[4,224,128]{2,1,0:T(8,128)(2,1)S(1)} %shard_map.86.rest_0_), channel_id=1, source_target_pairs={{0,24},{4,28},{8,16},{12,20},{16,8},{20,12},{24,0},{28,4},{1,25},{... | collective-permute-start | bytes 688136 | tf_op jit(solution)/shard_map/ppermute | solution.py:864
  35.1 13.1 %collective-permute-start.23 = (bf16[4,224,128]{2,1,0:T(8,128)(2,1)S(1)}, bf16[4,224,128]{2,1,0:T(8,128)(2,1)S(1)}, u32[]{:S(2)}, u32[]{:S(2)}) collective-permute-start(bf16[4,224,128]{2,1,0:T(8,128)(2,1)S(1)} %shard_map.86.rest_0_), channel_id=1, source_target_pairs={{0,16},{4,20},{8,24},{12,28},{16,0},{20,4},{24,8},{28,12},{1,17},{... | collective-permute-start | bytes 688136 | tf_op jit(solution)/shard_map/ppermute | solution.py:864
  36.6 11.9 %collective-permute-start.21 = (bf16[4,224,128]{2,1,0:T(8,128)(2,1)S(1)}, bf16[4,224,128]{2,1,0:T(8,128)(2,1)S(1)}, u32[]{:S(2)}, u32[]{:S(2)}) collective-permute-start(bf16[4,224,128]{2,1,0:T(8,128)(2,1)S(1)} %shard_map.86.rest_0_), channel_id=1, source_target_pairs={{0,8},{4,12},{8,0},{12,4},{16,24},{20,28},{24,16},{28,20},{1,9},{5... | collective-permute-start | bytes 688136 | tf_op jit(solution)/shard_map/ppermute | solution.py:864
  70.3 5.4 %collective-permute-start.27 = (bf16[16,224,128]{2,1,0:T(8,128)(2,1)S(1)}, bf16[16,224,128]{2,1,0:T(8,128)(2,1)S(1)}, u32[]{:S(2)}, u32[]{:S(2)}) collective-permute-start(bf16[16,224,128]{2,1,0:T(8,128)(2,1)S(1)} %get-tuple-element.105), channel_id=1, source_target_pairs={{0,4},{4,0},{8,12},{12,8},{16,20},{20,16},{24,28},{28,24},{1,5},{5... | collective-permute-start | bytes 2752520 | tf_op jit(solution)/shard_map/ppermute | solution.py:864
  76.0 12.9 %collective-permute-start.28 = (bf16[4,224,128]{2,1,0:T(8,128)(2,1)S(1)}, bf16[4,224,128]{2,1,0:T(8,128)(2,1)S(1)}, u32[]{:S(2)}, u32[]{:S(2)}) collective-permute-start(bf16[4,224,128]{2,1,0:T(8,128)(2,1)S(1)} %get-tuple-element.122), channel_id=1, source_target_pairs={{0,8},{4,12},{8,0},{12,4},{16,24},{20,28},{24,16},{28,20},{1,9},{5... | collective-permute-start | bytes 688136 | tf_op jit(solution)/shard_map/ppermute | solution.py:864
  77.4 12.4 %collective-permute-start.29 = (bf16[4,224,128]{2,1,0:T(8,128)(2,1)S(1)}, bf16[4,224,128]{2,1,0:T(8,128)(2,1)S(1)}, u32[]{:S(2)}, u32[]{:S(2)}) collective-permute-start(bf16[4,224,128]{2,1,0:T(8,128)(2,1)S(1)} %get-tuple-element.123), channel_id=1, source_target_pairs={{0,16},{4,20},{8,24},{12,28},{16,0},{20,4},{24,8},{28,12},{1,17},{... | collective-permute-start | bytes 688136 | tf_op jit(solution)/shard_map/ppermute | solution.py:864
  77.9 11.9 %collective-permute-start.30 = (bf16[4,224,128]{2,1,0:T(8,128)(2,1)S(1)}, bf16[4,224,128]{2,1,0:T(8,128)(2,1)S(1)}, u32[]{:S(2)}, u32[]{:S(2)}) collective-permute-start(bf16[4,224,128]{2,1,0:T(8,128)(2,1)S(1)} %get-tuple-element.124), channel_id=1, source_target_pairs={{0,24},{4,28},{8,16},{12,20},{16,8},{20,12},{24,0},{28,4},{1,25},{... | collective-permute-start | bytes 688136 | tf_op jit(solution)/shard_map/ppermute | solution.py:864
  93.3 11.5 %collective-permute-start.35 = (bf16[4,320,128]{2,1,0:T(8,128)(2,1)S(1)}, bf16[4,320,128]{2,1,0:T(8,128)(2,1)S(1)}, u32[]{:S(2)}, u32[]{:S(2)}) collective-permute-start(bf16[4,320,128]{2,1,0:T(8,128)(2,1)S(1)} %get-tuple-element.133), channel_id=1, source_target_pairs={{0,16},{4,20},{8,24},{12,28},{16,0},{20,4},{24,8},{28,12},{1,17},{... | collective-permute-start | bytes 983048 | tf_op jit(solution)/shard_map/ppermute | solution.py:864
  93.8 10.9 %collective-permute-start.36 = (bf16[4,320,128]{2,1,0:T(8,128)(2,1)S(1)}, bf16[4,320,128]{2,1,0:T(8,128)(2,1)S(1)}, u32[]{:S(2)}, u32[]{:S(2)}) collective-permute-start(bf16[4,320,128]{2,1,0:T(8,128)(2,1)S(1)} %get-tuple-element.134), channel_id=1, source_target_pairs={{0,8},{4,12},{8,0},{12,4},{16,24},{20,28},{24,16},{28,20},{1,9},{5... | collective-permute-start | bytes 983048 | tf_op jit(solution)/shard_map/ppermute | solution.py:864
  95.1 4.8 %collective-permute-start.32 = (bf16[224,128]{1,0:T(8,128)(2,1)S(1)}, bf16[224,128]{1,0:T(8,128)(2,1)S(1)}, u32[]{:S(2)}, u32[]{:S(2)}) collective-permute-start(bf16[224,128]{1,0:T(8,128)(2,1)S(1)} %get-tuple-element.128), channel_id=1, source_target_pairs={{0,1},{1,0},{2,3},{3,2},{4,5},{5,4},{6,7},{7,6},{8,9},{9,8},{10,11... | collective-permute-start | bytes 172040 | tf_op jit(solution)/shard_map/ppermute | solution.py:864
  96.1 6.5 %collective-permute-start.33 = (bf16[224,128]{1,0:T(8,128)(2,1)S(1)}, bf16[224,128]{1,0:T(8,128)(2,1)S(1)}, u32[]{:S(2)}, u32[]{:S(2)}) collective-permute-start(bf16[224,128]{1,0:T(8,128)(2,1)S(1)} %get-tuple-element.129), channel_id=1, source_target_pairs={{0,2},{1,3},{2,0},{3,1},{4,6},{5,7},{6,4},{7,5},{8,10},{9,11},{10,... | collective-permute-start | bytes 172040 | tf_op jit(solution)/shard_map/ppermute | solution.py:864
  98.1 6.0 %collective-permute-start.34 = (bf16[224,128]{1,0:T(8,128)(2,1)S(1)}, bf16[224,128]{1,0:T(8,128)(2,1)S(1)}, u32[]{:S(2)}, u32[]{:S(2)}) collective-permute-start(bf16[224,128]{1,0:T(8,128)(2,1)S(1)} %get-tuple-element.130), channel_id=1, source_target_pairs={{0,3},{1,2},{2,1},{3,0},{4,7},{5,6},{6,5},{7,4},{8,11},{9,10},{10,... | collective-permute-start | bytes 172040 | tf_op jit(solution)/shard_map/ppermute | solution.py:864
  104.9 5.4 %collective-permute-start.37 = (bf16[2,320,128]{2,1,0:T(8,128)(2,1)S(1)}, bf16[2,320,128]{2,1,0:T(8,128)(2,1)S(1)}, u32[]{:S(2)}, u32[]{:S(2)}) collective-permute-start(bf16[2,320,128]{2,1,0:T(8,128)(2,1)S(1)} %get-tuple-element.138), channel_id=1, source_target_pairs={{0,8},{4,12},{8,0},{12,4},{16,24},{20,28},{24,16},{28,20},{1,9},{5... | collective-permute-start | bytes 491528 | tf_op jit(solution)/shard_map/ppermute | solution.py:864
  105.8 5.3 %collective-permute-start.38 = (bf16[2,320,128]{2,1,0:T(8,128)(2,1)S(1)}, bf16[2,320,128]{2,1,0:T(8,128)(2,1)S(1)}, u32[]{:S(2)}, u32[]{:S(2)}) collective-permute-start(bf16[2,320,128]{2,1,0:T(8,128)(2,1)S(1)} %get-tuple-element.139), channel_id=1, source_target_pairs={{0,16},{4,20},{8,24},{12,28},{16,0},{20,4},{24,8},{28,12},{1,17},{... | collective-permute-start | bytes 491528 | tf_op jit(solution)/shard_map/ppermute | solution.py:864
  111.2 6.3 %collective-permute-start.39 = (bf16[320,128]{1,0:T(8,128)(2,1)S(1)}, bf16[320,128]{1,0:T(8,128)(2,1)S(1)}, u32[]{:S(2)}, u32[]{:S(2)}) collective-permute-start(bf16[320,128]{1,0:T(8,128)(2,1)S(1)} %get-tuple-element.143), channel_id=1, source_target_pairs={{0,1},{1,0},{2,3},{3,2},{4,5},{5,4},{6,7},{7,6},{8,9},{9,8},{10,11... | collective-permute-start | bytes 245768 | tf_op jit(solution)/shard_map/ppermute | solution.py:864
  111.2 6.2 %collective-permute-start.40 = (bf16[320,128]{1,0:T(8,128)(2,1)S(1)}, bf16[320,128]{1,0:T(8,128)(2,1)S(1)}, u32[]{:S(2)}, u32[]{:S(2)}) collective-permute-start(bf16[320,128]{1,0:T(8,128)(2,1)S(1)} %get-tuple-element.144), channel_id=1, source_target_pairs={{0,2},{1,3},{2,0},{3,1},{4,6},{5,7},{6,4},{7,5},{8,10},{9,11},{10,... | collective-permute-start | bytes 245768 | tf_op jit(solution)/shard_map/ppermute | solution.py:864
  113.3 6.3 %collective-permute-start.41 = (bf16[320,128]{1,0:T(8,128)(2,1)S(1)}, bf16[320,128]{1,0:T(8,128)(2,1)S(1)}, u32[]{:S(2)}, u32[]{:S(2)}) collective-permute-start(bf16[320,128]{1,0:T(8,128)(2,1)S(1)} %get-tuple-element.145), channel_id=1, source_target_pairs={{0,3},{1,2},{2,1},{3,0},{4,7},{5,6},{6,5},{7,4},{8,11},{9,10},{10,... | collective-permute-start | bytes 245768 | tf_op jit(solution)/shard_map/ppermute | solution.py:864
  (12 other events, 52.3 us)

commit v5 on v4

--- a/solution.py
+++ b/solution.py
@@ -350,11 +350,11 @@
 
 
 def in_turn(first, second):
-    for e in range(7):
+    for e in range(8):
         if e < 6:
             first(e)
-        if e > 0:
-            second(e - 1)
+        if e > 1:
+            second(e - 2)
 
 
 def spot(e):
@@ -514,7 +514,7 @@
             tower_tmp_ref[pl.ds(task * TOWER1 + half, TOWER1 // 2, stride=2), :] = jnp.concatenate(
                 pair, axis=1
             )
-    tower_out_ref[...] = tower_tmp_ref[...].astype(BF16)
+    tower_out_ref[...] = tower_tmp_ref[: 2 * TOWER1, :].astype(BF16)
     tower_small_ref[0:1, :] = from_lanes(flat_ref[pl.ds(where_row["tower_in_bias"], 2), :])
     tower_small_ref[1:2, :LANES] = flat_ref[pl.ds(where_row["tower_out_bias"], 1), :]
     g_small_ref[...] = jnp.zeros(g_small_ref.shape, F32)
@@ -630,7 +630,7 @@
     back = ((shift_a == shift_b + 4) & (shift_b < 4)).astype(F32).astype(BF16)
     tables = [mm_tn(mixed_ref[task], logit_ref[task]) for task in range(2)]
     tables[1] = mm(tables[1].astype(BF16), back)
-    g_tower_out_ref[...] = mm_tn(tower_active_ref[...], cotangent_ref[...])
+    g_tower_out_ref[: 2 * TOWER1, :] = mm_tn(tower_active_ref[...], cotangent_ref[...])
     for task in range(2):
         flat_ref[pl.ds(where_row["gate"] + task * gate_rows, gate_rows), :] = rows_from_table(
             tables[task], gate_rows, 4
@@ -1108,7 +1108,7 @@
             shape((8, width), F32),
         ],
         [
-            pltpu.VMEM((count * chunks[0], LANES), F32),
+            pltpu.VMEM((up(count * chunks[0], 8) + 16, LANES), F32),
             pltpu.VMEM((count, extra, LANES), F32),
             pltpu.VMEM((6, big, H), F32),
             pltpu.VMEM((big, 14 * LANES), F32),
@@ -1130,17 +1130,17 @@
         ]
         + [shape((count // outs, blocks[1], LANES), BF16)] * outs,
         [
-            pltpu.VMEM((count * chunks[1], LANES), F32),
+            pltpu.VMEM((up(count * chunks[1], 8) + 16, LANES), F32),
             pltpu.VMEM((H, 6 * H), BF16),
             pltpu.VMEM((6, H, H), BF16),
             pltpu.VMEM((4, 8, H), F32),
             pltpu.VMEM((H, LANES), BF16),
             pltpu.VMEM((2, H, TOWER1), BF16),
             pltpu.VMEM((2 * TOWER1, LANES), BF16),
-            pltpu.VMEM((2 * TOWER1, LANES), F32),
+            pltpu.VMEM((2 * TOWER1 + 16, LANES), F32),
             pltpu.VMEM((8, 2 * TOWER1), F32),
             pltpu.VMEM((4, 8, H), F32),
-            pltpu.VMEM((2 * TOWER1, LANES), F32),
+            pltpu.VMEM((2 * TOWER1 + 16, LANES), F32),
             pltpu.VMEM((8, 2 * TOWER1), F32),
             pltpu.VMEM((6, rows, H), BF16),
             pltpu.VMEM((tile, 6 * H), F32),
@@ -1222,7 +1222,7 @@
             pre_b,
         ],
         [shape((count // outs, blocks[0], LANES), BF16)] * outs,
-        [pltpu.VMEM((count * chunks[0], LANES), F32)],
+        [pltpu.VMEM((up(count * chunks[0], 8) + 16, LANES), F32)],
         12,
         rows * 6 * (width + H) * H * 2,
     )

time: 122 us -> 122 us (level)
  transfers between devices with their start and end apart: 42 -> 42, of which waited for: 23 -> 23; matrix products, arithmetic and copies ran while one was open for 0% -> 0% of each run, Pallas kernels for 20% -> 19%
where the time goes in v5:
time: 122 us
  Pallas kernels  48.6 us (40%)
  starting transfers between devices  38.9 us (32%)
  waiting for transfers between devices  33.1 us (27%)
    pallas_call x16, Pallas kernels, run_kernel(): pl.pallas_call(kernel, in_specs=specs, out_specs=out_specs, out_shape=out...  48.6 us
    ppermute x42, starting transfers between devices, xor_permute(): lax.ppermute(value, axis, [(index, index ^ bit) for index in range(size)])  38.9 us
    ppermute x42, waiting for transfers between devices, xor_permute(): lax.ppermute(value, axis, [(index, index ^ bit) for index in range(size)])  33.1 us
  transfers between devices with their start and end apart: 42, of which 23 were waited for; matrix products, arithmetic and copies ran while one was open for 0% of the time, Pallas kernels for 19%

profile of v5, /device:TPU:0, one launch (start us, length us, event | category | flops | bytes accessed | tf_op | source)
XLA Modules:
  0.0 121.6 jit_solution(6166554882378967823)
XLA Ops:
  0.6 2.1 %shard_map.84 = (bf16[1024,512]{1,0:T(8,128)(2,1)S(1)}, bf16[320,128]{1,0:T(8,128)(2,1)S(1)}, bf16[224,128]{1,0:T(8,128)(2,1)S(1)}) custom-call(s32[1]{0:T(128)} %bitcast.me_ref, bf16[1024,512]{1,0:T(8,128)(2,1)} %features_hbm.1, s32[8,1024]{1,0:T(8,128)} %bitcast.6, bf16[292,128]{1,0:T(8,128)(2,1)} %bitcast.9, bf16[215,128]{1,0:T(8,128)(2,1)} %bitcast.10), custom_call_target="tpu_custom_call" | custom-call | flops 1048576 | bytes 1024 | tf_op jit(solution)/shard_map/pallas_call | solution.py:263
  2.7 3.1 %collective-permute-start = (bf16[320,128]{1,0:T(8,128)(2,1)S(1)}, bf16[320,128]{1,0:T(8,128)(2,1)S(1)}, u32[]{:S(2)}, u32[]{:S(2)}) collective-permute-start(bf16[320,128]{1,0:T(8,128)(2,1)S(1)} %get-tuple-element.78.refs_0_), channel_id=1, source_target_pairs={{0,1},{1,0},{2,3},{3,2},{4,5},{5,4},{6,7},{7,6},{8,9},{9,8},{10,11... | collective-permute-start | bytes 245768 | tf_op jit(solution)/shard_map/ppermute | solution.py:864
  5.8 2.6 %collective-permute-start.1 = (bf16[320,128]{1,0:T(8,128)(2,1)S(1)}, bf16[320,128]{1,0:T(8,128)(2,1)S(1)}, u32[]{:S(2)}, u32[]{:S(2)}) collective-permute-start(bf16[320,128]{1,0:T(8,128)(2,1)S(1)} %get-tuple-element.78.refs_0_), channel_id=1, source_target_pairs={{0,2},{1,3},{2,0},{3,1},{4,6},{5,7},{6,4},{7,5},{8,10},{9,11},{10,... | collective-permute-start | bytes 245768 | tf_op jit(solution)/shard_map/ppermute | solution.py:864
  8.4 6.6 %collective-permute-done.1.refs_2_ = bf16[320,128]{1,0:T(8,128)(2,1)S(1)} collective-permute-done((bf16[320,128]{1,0:T(8,128)(2,1)S(1)}, bf16[320,128]{1,0:T(8,128)(2,1)S(1)}, u32[]{:S(2)}, u32[]{:S(2)}) %collective-permute-start.1) | collective-permute-done | bytes 81952 | tf_op jit(solution)/shard_map/ppermute | solution.py:864
  15.1 1.6 %collective-permute-start.6 = (bf16[2,320,128]{2,1,0:T(8,128)(2,1)S(1)}, bf16[2,320,128]{2,1,0:T(8,128)(2,1)S(1)}, u32[]{:S(2)}, u32[]{:S(2)}) collective-permute-start(bf16[2,320,128]{2,1,0:T(8,128)(2,1)S(1)} %get-tuple-element.79.rest_0_), channel_id=1, source_target_pairs={{0,16},{4,20},{8,24},{12,28},{16,0},{20,4},{24,8},{28,12},{1,17},{... | collective-permute-start | bytes 491528 | tf_op jit(solution)/shard_map/ppermute | solution.py:864
  16.6 1.5 %collective-permute-start.8 = (bf16[2,320,128]{2,1,0:T(8,128)(2,1)S(1)}, bf16[2,320,128]{2,1,0:T(8,128)(2,1)S(1)}, u32[]{:S(2)}, u32[]{:S(2)}) collective-permute-start(bf16[2,320,128]{2,1,0:T(8,128)(2,1)S(1)} %get-tuple-element.81.rest_1_), channel_id=1, source_target_pairs={{0,8},{4,12},{8,0},{12,4},{16,24},{20,28},{24,16},{28,20},{1,9},{5... | collective-permute-start | bytes 491528 | tf_op jit(solution)/shard_map/ppermute | solution.py:864
  18.1 2.5 %collective-permute-start.5 = (bf16[224,128]{1,0:T(8,128)(2,1)S(1)}, bf16[224,128]{1,0:T(8,128)(2,1)S(1)}, u32[]{:S(2)}, u32[]{:S(2)}) collective-permute-start(bf16[224,128]{1,0:T(8,128)(2,1)S(1)} %get-tuple-element.80.refs_0_), channel_id=1, source_target_pairs={{0,3},{1,2},{2,1},{3,0},{4,7},{5,6},{6,5},{7,4},{8,11},{9,10},{10,... | collective-permute-start | bytes 172040 | tf_op jit(solution)/shard_map/ppermute | solution.py:864
  21.1 1.4 %collective-permute-start.4 = (bf16[224,128]{1,0:T(8,128)(2,1)S(1)}, bf16[224,128]{1,0:T(8,128)(2,1)S(1)}, u32[]{:S(2)}, u32[]{:S(2)}) collective-permute-start(bf16[224,128]{1,0:T(8,128)(2,1)S(1)} %get-tuple-element.80.refs_0_), channel_id=1, source_target_pairs={{0,2},{1,3},{2,0},{3,1},{4,6},{5,7},{6,4},{7,5},{8,10},{9,11},{10,... | collective-permute-start | bytes 172040 | tf_op jit(solution)/shard_map/ppermute | solution.py:864
  22.5 1.7 %collective-permute-done.5.refs_3_ = bf16[224,128]{1,0:T(8,128)(2,1)S(1)} collective-permute-done((bf16[224,128]{1,0:T(8,128)(2,1)S(1)}, bf16[224,128]{1,0:T(8,128)(2,1)S(1)}, u32[]{:S(2)}, u32[]{:S(2)}) %collective-permute-start.5) | collective-permute-done | bytes 57376 | tf_op jit(solution)/shard_map/ppermute | solution.py:864
  26.8 1.5 %collective-permute-start.9 = (bf16[2,320,128]{2,1,0:T(8,128)(2,1)S(1)}, bf16[2,320,128]{2,1,0:T(8,128)(2,1)S(1)}, u32[]{:S(2)}, u32[]{:S(2)}) collective-permute-start(bf16[2,320,128]{2,1,0:T(8,128)(2,1)S(1)} %collective-permute-done.8.rest_5_), channel_id=1, source_target_pairs={{0,16},{4,20},{8,24},{12,28},{16,0},{20,4},{24,8},{28,12},{1,17},{... | collective-permute-start | bytes 491528 | tf_op jit(solution)/shard_map/ppermute | solution.py:864
  31.3 1.8 %collective-permute-done.7.rest_12_ = bf16[2,320,128]{2,1,0:T(8,128)(2,1)S(1)} collective-permute-done((bf16[2,320,128]{2,1,0:T(8,128)(2,1)S(1)}, bf16[2,320,128]{2,1,0:T(8,128)(2,1)S(1)}, u32[]{:S(2)}, u32[]{:S(2)}) %collective-permute-start.7) | collective-permute-done | bytes 163872 | tf_op jit(solution)/shard_map/ppermute | solution.py:864
  33.7 1.4 %collective-permute-start.25 = (bf16[4,224,128]{2,1,0:T(8,128)(2,1)S(1)}, bf16[4,224,128]{2,1,0:T(8,128)(2,1)S(1)}, u32[]{:S(2)}, u32[]{:S(2)}) collective-permute-start(bf16[4,224,128]{2,1,0:T(8,128)(2,1)S(1)} %shard_map.86.rest_0_), channel_id=1, source_target_pairs={{0,24},{4,28},{8,16},{12,20},{16,8},{20,12},{24,0},{28,4},{1,25},{... | collective-permute-start | bytes 688136 | tf_op jit(solution)/shard_map/ppermute | solution.py:864
  35.1 1.5 %collective-permute-start.23 = (bf16[4,224,128]{2,1,0:T(8,128)(2,1)S(1)}, bf16[4,224,128]{2,1,0:T(8,128)(2,1)S(1)}, u32[]{:S(2)}, u32[]{:S(2)}) collective-permute-start(bf16[4,224,128]{2,1,0:T(8,128)(2,1)S(1)} %shard_map.86.rest_0_), channel_id=1, source_target_pairs={{0,16},{4,20},{8,24},{12,28},{16,0},{20,4},{24,8},{28,12},{1,17},{... | collective-permute-start | bytes 688136 | tf_op jit(solution)/shard_map/ppermute | solution.py:864
  38.9 8.5 %shard_map.87 = (bf16[1024,512]{1,0:T(8,128)(2,1)S(1)}, bf16[6,1024,256]{2,1,0:T(8,128)(2,1)S(1)}, bf16[6,1024,256]{2,1,0:T(8,128)(2,1)S(1)}, bf16[6,1024,256]{2...) custom-call(s32[1]{0:T(128)} %bitcast.me_ref, ...), custom_call_target="tpu_custom_call" | custom-call | flops 1048576 | bytes 1024 | tf_op jit(solution)/shard_map/pallas_call | solution.py:263
  49.9 20.0 %shard_map.88 = (f32[1024,128]{1,0:T(8,128)}, f32[3,1024,256]{2,1,0:T(8,128)S(1)}, bf16[16,224,128]{2,1,0:T(8,128)(2,1)S(1)}, bf16[16,224,128]{2,1,0:T(8,128)(2,1)S(1)}) custom-call(s32[1]{0:T(128)} %bitcast.me_ref, bf16[3,1024,256]{2,1,0:T(8,128)(2,1)S(1)} %get-tuple-element.84.mixed_ref, bf16[1024,128]{1,0:T(8,128)(2,1)S(1)} %copy-done, ...), custom_call_target="tpu_custom_call" | custom-call | flops 1048576 | bytes 1024 | tf_op jit(solution)/shard_map/pallas_call | solution.py:263
  70.2 5.0 %shard_map.89 = (f32[512,512]{1,0:T(8,128)S(1)}, f32[8,512]{1,0:T(8,128)S(1)}, f32[4,8,256]{2,1,0:T(8,128)S(1)}, bf16[512,128]{1,0:T(8,128)(2,1)S(1)}, bf16[6,51...) custom-call(f32[3,1024,256]{2,1,0:T(8,128)S(1)} %get-tuple-element.92.mixed_grad_ref, ...), custom_call_target="tpu_custom_call" | custom-call | flops 1048576 | bytes 1024 | tf_op jit(solution)/shard_map/pallas_call | solution.py:263
  75.4 1.4 %collective-permute-start.28 = (bf16[4,224,128]{2,1,0:T(8,128)(2,1)S(1)}, bf16[4,224,128]{2,1,0:T(8,128)(2,1)S(1)}, u32[]{:S(2)}, u32[]{:S(2)}) collective-permute-start(bf16[4,224,128]{2,1,0:T(8,128)(2,1)S(1)} %get-tuple-element.122), channel_id=1, source_target_pairs={{0,8},{4,12},{8,0},{12,4},{16,24},{20,28},{24,16},{28,20},{1,9},{5... | collective-permute-start | bytes 688136 | tf_op jit(solution)/shard_map/ppermute | solution.py:864
  77.4 1.6 %collective-permute-start.30 = (bf16[4,224,128]{2,1,0:T(8,128)(2,1)S(1)}, bf16[4,224,128]{2,1,0:T(8,128)(2,1)S(1)}, u32[]{:S(2)}, u32[]{:S(2)}) collective-permute-start(bf16[4,224,128]{2,1,0:T(8,128)(2,1)S(1)} %get-tuple-element.124), channel_id=1, source_target_pairs={{0,24},{4,28},{8,16},{12,20},{16,8},{20,12},{24,0},{28,4},{1,25},{... | collective-permute-start | bytes 688136 | tf_op jit(solution)/shard_map/ppermute | solution.py:864
  79.0 5.2 %shard_map.91 = (f32[512,512]{1,0:T(8,128)S(1)}, f32[8,512]{1,0:T(8,128)S(1)}, f32[4,8,256]{2,1,0:T(8,128)S(1)}, bf16[512,128]{1,0:T(8,128)(2,1)S(1)}, bf16[6,51...) custom-call(f32[3,1024,256]{2,1,0:T(8,128)S(1)} %get-tuple-element.92.mixed_grad_ref, ...), custom_call_target="tpu_custom_call" | custom-call | flops 1048576 | bytes 1024 | tf_op jit(solution)/shard_map/pallas_call | solution.py:263
  84.2 4.0 %shard_map.92 = (bf16[16,320,128]{2,1,0:T(8,128)(2,1)S(1)}, bf16[16,320,128]{2,1,0:T(8,128)(2,1)S(1)}) custom-call(s32[1]{0:T(128)} %bitcast.me_ref, bf16[1024,512]{1,0:T(8,128)(2,1)S(1)} %get-tuple-element.110.level_ref, bf16[6,1024,256]{2,1,0:T(8,128)(2,1)S(1)} %get-tuple-element.111.active_ref, f32[8,512]{1,0:T(8,128)S(1)} %get-tuple-element.112.sums_ref, ...), custom_call_target="tpu_custom_call" | custom-call | flops 1048576 | bytes 1024 | tf_op jit(solution)/shard_map/pallas_call | solution.py:263
  89.4 3.0 %collective-permute-done.31.got_ref = bf16[16,320,128]{2,1,0:T(8,128)(2,1)S(1)} collective-permute-done((bf16[16,320,128]{2,1,0:T(8,128)(2,1)S(1)}, bf16[16,320,128]{2,1,0:T(8,128)(2,1)S(1)}, u32[]{:S(2)}, u32[]{:S(2)}) %collective-permute-start.31) | collective-permute-done | bytes 1310752 | tf_op jit(solution)/shard_map/ppermute | solution.py:864
  95.6 2.0 %collective-permute-start.33 = (bf16[224,128]{1,0:T(8,128)(2,1)S(1)}, bf16[224,128]{1,0:T(8,128)(2,1)S(1)}, u32[]{:S(2)}, u32[]{:S(2)}) collective-permute-start(bf16[224,128]{1,0:T(8,128)(2,1)S(1)} %get-tuple-element.129), channel_id=1, source_target_pairs={{0,2},{1,3},{2,0},{3,1},{4,6},{5,7},{6,4},{7,5},{8,10},{9,11},{10,... | collective-permute-start | bytes 172040 | tf_op jit(solution)/shard_map/ppermute | solution.py:864
  97.6 1.3 %collective-permute-start.34 = (bf16[224,128]{1,0:T(8,128)(2,1)S(1)}, bf16[224,128]{1,0:T(8,128)(2,1)S(1)}, u32[]{:S(2)}, u32[]{:S(2)}) collective-permute-start(bf16[224,128]{1,0:T(8,128)(2,1)S(1)} %get-tuple-element.130), channel_id=1, source_target_pairs={{0,3},{1,2},{2,1},{3,0},{4,7},{5,6},{6,5},{7,4},{8,11},{9,10},{10,... | collective-permute-start | bytes 172040 | tf_op jit(solution)/shard_map/ppermute | solution.py:864
  99.3 2.7 %collective-permute-done.33.two_ref = bf16[224,128]{1,0:T(8,128)(2,1)S(1)} collective-permute-done((bf16[224,128]{1,0:T(8,128)(2,1)S(1)}, bf16[224,128]{1,0:T(8,128)(2,1)S(1)}, u32[]{:S(2)}, u32[]{:S(2)}) %collective-permute-start.33) | collective-permute-done | bytes 57376 | tf_op jit(solution)/shard_map/ppermute | solution.py:864
  102.1 1.5 %collective-permute-done.34.three_ref = bf16[224,128]{1,0:T(8,128)(2,1)S(1)} collective-permute-done((bf16[224,128]{1,0:T(8,128)(2,1)S(1)}, bf16[224,128]{1,0:T(8,128)(2,1)S(1)}, u32[]{:S(2)}, u32[]{:S(2)}) %collective-permute-start.34) | collective-permute-done | bytes 57376 | tf_op jit(solution)/shard_map/ppermute | solution.py:864
  105.3 1.5 %collective-permute-start.38 = (bf16[2,320,128]{2,1,0:T(8,128)(2,1)S(1)}, bf16[2,320,128]{2,1,0:T(8,128)(2,1)S(1)}, u32[]{:S(2)}, u32[]{:S(2)}) collective-permute-start(bf16[2,320,128]{2,1,0:T(8,128)(2,1)S(1)} %get-tuple-element.139), channel_id=1, source_target_pairs={{0,16},{4,20},{8,24},{12,28},{16,0},{20,4},{24,8},{28,12},{1,17},{... | collective-permute-start | bytes 491528 | tf_op jit(solution)/shard_map/ppermute | solution.py:864
  106.8 3.0 %collective-permute-done.37.got_one_ref = bf16[2,320,128]{2,1,0:T(8,128)(2,1)S(1)} collective-permute-done((bf16[2,320,128]{2,1,0:T(8,128)(2,1)S(1)}, bf16[2,320,128]{2,1,0:T(8,128)(2,1)S(1)}, u32[]{:S(2)}, u32[]{:S(2)}) %collective-permute-start.37) | collective-permute-done | bytes 163872 | tf_op jit(solution)/shard_map/ppermute | solution.py:864
  110.7 2.0 %collective-permute-start.40 = (bf16[320,128]{1,0:T(8,128)(2,1)S(1)}, bf16[320,128]{1,0:T(8,128)(2,1)S(1)}, u32[]{:S(2)}, u32[]{:S(2)}) collective-permute-start(bf16[320,128]{1,0:T(8,128)(2,1)S(1)} %get-tuple-element.144), channel_id=1, source_target_pairs={{0,2},{1,3},{2,0},{3,1},{4,6},{5,7},{6,4},{7,5},{8,10},{9,11},{10,... | collective-permute-start | bytes 245768 | tf_op jit(solution)/shard_map/ppermute | solution.py:864
  112.7 2.4 %collective-permute-start.41 = (bf16[320,128]{1,0:T(8,128)(2,1)S(1)}, bf16[320,128]{1,0:T(8,128)(2,1)S(1)}, u32[]{:S(2)}, u32[]{:S(2)}) collective-permute-start(bf16[320,128]{1,0:T(8,128)(2,1)S(1)} %get-tuple-element.145), channel_id=1, source_target_pairs={{0,3},{1,2},{2,1},{3,0},{4,7},{5,6},{6,5},{7,4},{8,11},{9,10},{10,... | collective-permute-start | bytes 245768 | tf_op jit(solution)/shard_map/ppermute | solution.py:864
  115.1 1.8 %collective-permute-done.39.one_ref = bf16[320,128]{1,0:T(8,128)(2,1)S(1)} collective-permute-done((bf16[320,128]{1,0:T(8,128)(2,1)S(1)}, bf16[320,128]{1,0:T(8,128)(2,1)S(1)}, u32[]{:S(2)}, u32[]{:S(2)}) %collective-permute-start.39) | collective-permute-done | bytes 81952 | tf_op jit(solution)/shard_map/ppermute | solution.py:864
  116.9 2.2 %collective-permute-done.41.three_ref = bf16[320,128]{1,0:T(8,128)(2,1)S(1)} collective-permute-done((bf16[320,128]{1,0:T(8,128)(2,1)S(1)}, bf16[320,128]{1,0:T(8,128)(2,1)S(1)}, u32[]{:S(2)}, u32[]{:S(2)}) %collective-permute-start.41) | collective-permute-done | bytes 81952 | tf_op jit(solution)/shard_map/ppermute | solution.py:864
  119.8 1.6 %shard_map.99 = f32[1024,512]{1,0:T(8,128)} custom-call(f32[512,512]{1,0:T(8,128)S(1)} %get-tuple-element.101.grad_a_ref, f32[512,512]{1,0:T(8,128)S(1)} %get-tuple-element.109.grad_b_ref, bf16[1024,512]{1,0:T(8,128)(2,1)S(1)} %get-tuple-element.83.masked_ref, s32[8,1024]{1,0:T(8,128)S(1)} %bitcast.7, f32[8,512]{1,0:T(8,128)S(1)} %get-tuple-element.86.entry_ref, ...), custom_call_target="tpu_custom_call" | custom-call | flops 1048576 | bytes 1024 | tf_op jit(solution)/shard_map/pallas_call | solution.py:263
  (72 shorter events, 20.6 us)
Async XLA Ops:
  2.7 5.7 %collective-permute-start = (bf16[320,128]{1,0:T(8,128)(2,1)S(1)}, bf16[320,128]{1,0:T(8,128)(2,1)S(1)}, u32[]{:S(2)}, u32[]{:S(2)}) collective-permute-start(bf16[320,128]{1,0:T(8,128)(2,1)S(1)} %get-tuple-element.78.refs_0_), channel_id=1, source_target_pairs={{0,1},{1,0},{2,3},{3,2},{4,5},{5,4},{6,7},{7,6},{8,9},{9,8},{10,11... | collective-permute-start | bytes 245768 | tf_op jit(solution)/shard_map/ppermute | solution.py:864
  5.8 9.2 %collective-permute-start.1 = (bf16[320,128]{1,0:T(8,128)(2,1)S(1)}, bf16[320,128]{1,0:T(8,128)(2,1)S(1)}, u32[]{:S(2)}, u32[]{:S(2)}) collective-permute-start(bf16[320,128]{1,0:T(8,128)(2,1)S(1)} %get-tuple-element.78.refs_0_), channel_id=1, source_target_pairs={{0,2},{1,3},{2,0},{3,1},{4,6},{5,7},{6,4},{7,5},{8,10},{9,11},{10,... | collective-permute-start | bytes 245768 | tf_op jit(solution)/shard_map/ppermute | solution.py:864
  8.4 6.6 %collective-permute-start.2 = (bf16[320,128]{1,0:T(8,128)(2,1)S(1)}, bf16[320,128]{1,0:T(8,128)(2,1)S(1)}, u32[]{:S(2)}, u32[]{:S(2)}) collective-permute-start(bf16[320,128]{1,0:T(8,128)(2,1)S(1)} %get-tuple-element.78.refs_0_), channel_id=1, source_target_pairs={{0,3},{1,2},{2,1},{3,0},{4,7},{5,6},{6,5},{7,4},{8,11},{9,10},{10,... | collective-permute-start | bytes 245768 | tf_op jit(solution)/shard_map/ppermute | solution.py:864
  15.1 11.2 %collective-permute-start.6 = (bf16[2,320,128]{2,1,0:T(8,128)(2,1)S(1)}, bf16[2,320,128]{2,1,0:T(8,128)(2,1)S(1)}, u32[]{:S(2)}, u32[]{:S(2)}) collective-permute-start(bf16[2,320,128]{2,1,0:T(8,128)(2,1)S(1)} %get-tuple-element.79.rest_0_), channel_id=1, source_target_pairs={{0,16},{4,20},{8,24},{12,28},{16,0},{20,4},{24,8},{28,12},{1,17},{... | collective-permute-start | bytes 491528 | tf_op jit(solution)/shard_map/ppermute | solution.py:864
  16.6 10.2 %collective-permute-start.8 = (bf16[2,320,128]{2,1,0:T(8,128)(2,1)S(1)}, bf16[2,320,128]{2,1,0:T(8,128)(2,1)S(1)}, u32[]{:S(2)}, u32[]{:S(2)}) collective-permute-start(bf16[2,320,128]{2,1,0:T(8,128)(2,1)S(1)} %get-tuple-element.81.rest_1_), channel_id=1, source_target_pairs={{0,8},{4,12},{8,0},{12,4},{16,24},{20,28},{24,16},{28,20},{1,9},{5... | collective-permute-start | bytes 491528 | tf_op jit(solution)/shard_map/ppermute | solution.py:864
  18.1 6.1 %collective-permute-start.5 = (bf16[224,128]{1,0:T(8,128)(2,1)S(1)}, bf16[224,128]{1,0:T(8,128)(2,1)S(1)}, u32[]{:S(2)}, u32[]{:S(2)}) collective-permute-start(bf16[224,128]{1,0:T(8,128)(2,1)S(1)} %get-tuple-element.80.refs_0_), channel_id=1, source_target_pairs={{0,3},{1,2},{2,1},{3,0},{4,7},{5,6},{6,5},{7,4},{8,11},{9,10},{10,... | collective-permute-start | bytes 172040 | tf_op jit(solution)/shard_map/ppermute | solution.py:864
  20.6 4.3 %collective-permute-start.3 = (bf16[224,128]{1,0:T(8,128)(2,1)S(1)}, bf16[224,128]{1,0:T(8,128)(2,1)S(1)}, u32[]{:S(2)}, u32[]{:S(2)}) collective-permute-start(bf16[224,128]{1,0:T(8,128)(2,1)S(1)} %get-tuple-element.80.refs_0_), channel_id=1, source_target_pairs={{0,1},{1,0},{2,3},{3,2},{4,5},{5,4},{6,7},{7,6},{8,9},{9,8},{10,11... | collective-permute-start | bytes 172040 | tf_op jit(solution)/shard_map/ppermute | solution.py:864
  21.1 5.1 %collective-permute-start.4 = (bf16[224,128]{1,0:T(8,128)(2,1)S(1)}, bf16[224,128]{1,0:T(8,128)(2,1)S(1)}, u32[]{:S(2)}, u32[]{:S(2)}) collective-permute-start(bf16[224,128]{1,0:T(8,128)(2,1)S(1)} %get-tuple-element.80.refs_0_), channel_id=1, source_target_pairs={{0,2},{1,3},{2,0},{3,1},{4,6},{5,7},{6,4},{7,5},{8,10},{9,11},{10,... | collective-permute-start | bytes 172040 | tf_op jit(solution)/shard_map/ppermute | solution.py:864
  24.2 5.5 %collective-permute-start.12 = (bf16[2,320,128]{2,1,0:T(8,128)(2,1)S(1)}, bf16[2,320,128]{2,1,0:T(8,128)(2,1)S(1)}, u32[]{:S(2)}, u32[]{:S(2)}) collective-permute-start(bf16[2,320,128]{2,1,0:T(8,128)(2,1)S(1)} %get-tuple-element.79.rest_0_), channel_id=1, source_target_pairs={{0,8},{4,12},{8,0},{12,4},{16,24},{20,28},{24,16},{28,20},{1,9},{5... | collective-permute-start | bytes 491528 | tf_op jit(solution)/shard_map/ppermute | solution.py:864
  24.9 5.9 %collective-permute-start.15 = (bf16[2,320,128]{2,1,0:T(8,128)(2,1)S(1)}, bf16[2,320,128]{2,1,0:T(8,128)(2,1)S(1)}, u32[]{:S(2)}, u32[]{:S(2)}) collective-permute-start(bf16[2,320,128]{2,1,0:T(8,128)(2,1)S(1)} %get-tuple-element.81.rest_1_), channel_id=1, source_target_pairs={{0,16},{4,20},{8,24},{12,28},{16,0},{20,4},{24,8},{28,12},{1,17},{... | collective-permute-start | bytes 491528 | tf_op jit(solution)/shard_map/ppermute | solution.py:864
  26.2 4.5 %collective-permute-start.10 = (bf16[2,320,128]{2,1,0:T(8,128)(2,1)S(1)}, bf16[2,320,128]{2,1,0:T(8,128)(2,1)S(1)}, u32[]{:S(2)}, u32[]{:S(2)}) collective-permute-start(bf16[2,320,128]{2,1,0:T(8,128)(2,1)S(1)} %get-tuple-element.79.rest_0_), channel_id=1, source_target_pairs={{0,4},{4,0},{8,12},{12,8},{16,20},{20,16},{24,28},{28,24},{1,5},{5... | collective-permute-start | bytes 491528 | tf_op jit(solution)/shard_map/ppermute | solution.py:864
  26.2 6.8 %collective-permute-start.7 = (bf16[2,320,128]{2,1,0:T(8,128)(2,1)S(1)}, bf16[2,320,128]{2,1,0:T(8,128)(2,1)S(1)}, u32[]{:S(2)}, u32[]{:S(2)}) collective-permute-start(bf16[2,320,128]{2,1,0:T(8,128)(2,1)S(1)} %collective-permute-done.6.rest_8_), channel_id=1, source_target_pairs={{0,8},{4,12},{8,0},{12,4},{16,24},{20,28},{24,16},{28,20},{1,9},{5... | collective-permute-start | bytes 491528 | tf_op jit(solution)/shard_map/ppermute | solution.py:864
  26.8 6.9 %collective-permute-start.9 = (bf16[2,320,128]{2,1,0:T(8,128)(2,1)S(1)}, bf16[2,320,128]{2,1,0:T(8,128)(2,1)S(1)}, u32[]{:S(2)}, u32[]{:S(2)}) collective-permute-start(bf16[2,320,128]{2,1,0:T(8,128)(2,1)S(1)} %collective-permute-done.8.rest_5_), channel_id=1, source_target_pairs={{0,16},{4,20},{8,24},{12,28},{16,0},{20,4},{24,8},{28,12},{1,17},{... | collective-permute-start | bytes 491528 | tf_op jit(solution)/shard_map/ppermute | solution.py:864
  30.7 4.4 %collective-permute-start.16 = (bf16[2,320,128]{2,1,0:T(8,128)(2,1)S(1)}, bf16[2,320,128]{2,1,0:T(8,128)(2,1)S(1)}, u32[]{:S(2)}, u32[]{:S(2)}) collective-permute-start(bf16[2,320,128]{2,1,0:T(8,128)(2,1)S(1)} %collective-permute-done.6.rest_8_), channel_id=1, source_target_pairs={{0,4},{4,0},{8,12},{12,8},{16,20},{20,16},{24,28},{28,24},{1,5},{5... | collective-permute-start | bytes 491528 | tf_op jit(solution)/shard_map/ppermute | solution.py:864
  30.8 5.9 %collective-permute-start.13 = (bf16[2,320,128]{2,1,0:T(8,128)(2,1)S(1)}, bf16[2,320,128]{2,1,0:T(8,128)(2,1)S(1)}, u32[]{:S(2)}, u32[]{:S(2)}) collective-permute-start(bf16[2,320,128]{2,1,0:T(8,128)(2,1)S(1)} %collective-permute-done.12.rest_4_), channel_id=1, source_target_pairs={{0,4},{4,0},{8,12},{12,8},{16,20},{20,16},{24,28},{28,24},{1,5},{5... | collective-permute-start | bytes 491528 | tf_op jit(solution)/shard_map/ppermute | solution.py:864
  33.7 14.0 %collective-permute-start.25 = (bf16[4,224,128]{2,1,0:T(8,128)(2,1)S(1)}, bf16[4,224,128]{2,1,0:T(8,128)(2,1)S(1)}, u32[]{:S(2)}, u32[]{:S(2)}) collective-permute-start(bf16[4,224,128]{2,1,0:T(8,128)(2,1)S(1)} %shard_map.86.rest_0_), channel_id=1, source_target_pairs={{0,24},{4,28},{8,16},{12,20},{16,8},{20,12},{24,0},{28,4},{1,25},{... | collective-permute-start | bytes 688136 | tf_op jit(solution)/shard_map/ppermute | solution.py:864
  35.1 12.9 %collective-permute-start.23 = (bf16[4,224,128]{2,1,0:T(8,128)(2,1)S(1)}, bf16[4,224,128]{2,1,0:T(8,128)(2,1)S(1)}, u32[]{:S(2)}, u32[]{:S(2)}) collective-permute-start(bf16[4,224,128]{2,1,0:T(8,128)(2,1)S(1)} %shard_map.86.rest_0_), channel_id=1, source_target_pairs={{0,16},{4,20},{8,24},{12,28},{16,0},{20,4},{24,8},{28,12},{1,17},{... | collective-permute-start | bytes 688136 | tf_op jit(solution)/shard_map/ppermute | solution.py:864
  36.6 11.6 %collective-permute-start.21 = (bf16[4,224,128]{2,1,0:T(8,128)(2,1)S(1)}, bf16[4,224,128]{2,1,0:T(8,128)(2,1)S(1)}, u32[]{:S(2)}, u32[]{:S(2)}) collective-permute-start(bf16[4,224,128]{2,1,0:T(8,128)(2,1)S(1)} %shard_map.86.rest_0_), channel_id=1, source_target_pairs={{0,8},{4,12},{8,0},{12,4},{16,24},{20,28},{24,16},{28,20},{1,9},{5... | collective-permute-start | bytes 688136 | tf_op jit(solution)/shard_map/ppermute | solution.py:864
  69.9 5.3 %collective-permute-start.27 = (bf16[16,224,128]{2,1,0:T(8,128)(2,1)S(1)}, bf16[16,224,128]{2,1,0:T(8,128)(2,1)S(1)}, u32[]{:S(2)}, u32[]{:S(2)}) collective-permute-start(bf16[16,224,128]{2,1,0:T(8,128)(2,1)S(1)} %get-tuple-element.105), channel_id=1, source_target_pairs={{0,4},{4,0},{8,12},{12,8},{16,20},{20,16},{24,28},{28,24},{1,5},{5... | collective-permute-start | bytes 2752520 | tf_op jit(solution)/shard_map/ppermute | solution.py:864
  75.4 12.8 %collective-permute-start.28 = (bf16[4,224,128]{2,1,0:T(8,128)(2,1)S(1)}, bf16[4,224,128]{2,1,0:T(8,128)(2,1)S(1)}, u32[]{:S(2)}, u32[]{:S(2)}) collective-permute-start(bf16[4,224,128]{2,1,0:T(8,128)(2,1)S(1)} %get-tuple-element.122), channel_id=1, source_target_pairs={{0,8},{4,12},{8,0},{12,4},{16,24},{20,28},{24,16},{28,20},{1,9},{5... | collective-permute-start | bytes 688136 | tf_op jit(solution)/shard_map/ppermute | solution.py:864
  76.9 12.4 %collective-permute-start.29 = (bf16[4,224,128]{2,1,0:T(8,128)(2,1)S(1)}, bf16[4,224,128]{2,1,0:T(8,128)(2,1)S(1)}, u32[]{:S(2)}, u32[]{:S(2)}) collective-permute-start(bf16[4,224,128]{2,1,0:T(8,128)(2,1)S(1)} %get-tuple-element.123), channel_id=1, source_target_pairs={{0,16},{4,20},{8,24},{12,28},{16,0},{20,4},{24,8},{28,12},{1,17},{... | collective-permute-start | bytes 688136 | tf_op jit(solution)/shard_map/ppermute | solution.py:864
  77.4 11.9 %collective-permute-start.30 = (bf16[4,224,128]{2,1,0:T(8,128)(2,1)S(1)}, bf16[4,224,128]{2,1,0:T(8,128)(2,1)S(1)}, u32[]{:S(2)}, u32[]{:S(2)}) collective-permute-start(bf16[4,224,128]{2,1,0:T(8,128)(2,1)S(1)} %get-tuple-element.124), channel_id=1, source_target_pairs={{0,24},{4,28},{8,16},{12,20},{16,8},{20,12},{24,0},{28,4},{1,25},{... | collective-permute-start | bytes 688136 | tf_op jit(solution)/shard_map/ppermute | solution.py:864
  92.8 11.5 %collective-permute-start.35 = (bf16[4,320,128]{2,1,0:T(8,128)(2,1)S(1)}, bf16[4,320,128]{2,1,0:T(8,128)(2,1)S(1)}, u32[]{:S(2)}, u32[]{:S(2)}) collective-permute-start(bf16[4,320,128]{2,1,0:T(8,128)(2,1)S(1)} %get-tuple-element.133), channel_id=1, source_target_pairs={{0,16},{4,20},{8,24},{12,28},{16,0},{20,4},{24,8},{28,12},{1,17},{... | collective-permute-start | bytes 983048 | tf_op jit(solution)/shard_map/ppermute | solution.py:864
  93.3 10.9 %collective-permute-start.36 = (bf16[4,320,128]{2,1,0:T(8,128)(2,1)S(1)}, bf16[4,320,128]{2,1,0:T(8,128)(2,1)S(1)}, u32[]{:S(2)}, u32[]{:S(2)}) collective-permute-start(bf16[4,320,128]{2,1,0:T(8,128)(2,1)S(1)} %get-tuple-element.134), channel_id=1, source_target_pairs={{0,8},{4,12},{8,0},{12,4},{16,24},{20,28},{24,16},{28,20},{1,9},{5... | collective-permute-start | bytes 983048 | tf_op jit(solution)/shard_map/ppermute | solution.py:864
  94.6 4.8 %collective-permute-start.32 = (bf16[224,128]{1,0:T(8,128)(2,1)S(1)}, bf16[224,128]{1,0:T(8,128)(2,1)S(1)}, u32[]{:S(2)}, u32[]{:S(2)}) collective-permute-start(bf16[224,128]{1,0:T(8,128)(2,1)S(1)} %get-tuple-element.128), channel_id=1, source_target_pairs={{0,1},{1,0},{2,3},{3,2},{4,5},{5,4},{6,7},{7,6},{8,9},{9,8},{10,11... | collective-permute-start | bytes 172040 | tf_op jit(solution)/shard_map/ppermute | solution.py:864
  95.6 6.5 %collective-permute-start.33 = (bf16[224,128]{1,0:T(8,128)(2,1)S(1)}, bf16[224,128]{1,0:T(8,128)(2,1)S(1)}, u32[]{:S(2)}, u32[]{:S(2)}) collective-permute-start(bf16[224,128]{1,0:T(8,128)(2,1)S(1)} %get-tuple-element.129), channel_id=1, source_target_pairs={{0,2},{1,3},{2,0},{3,1},{4,6},{5,7},{6,4},{7,5},{8,10},{9,11},{10,... | collective-permute-start | bytes 172040 | tf_op jit(solution)/shard_map/ppermute | solution.py:864
  97.6 6.0 %collective-permute-start.34 = (bf16[224,128]{1,0:T(8,128)(2,1)S(1)}, bf16[224,128]{1,0:T(8,128)(2,1)S(1)}, u32[]{:S(2)}, u32[]{:S(2)}) collective-permute-start(bf16[224,128]{1,0:T(8,128)(2,1)S(1)} %get-tuple-element.130), channel_id=1, source_target_pairs={{0,3},{1,2},{2,1},{3,0},{4,7},{5,6},{6,5},{7,4},{8,11},{9,10},{10,... | collective-permute-start | bytes 172040 | tf_op jit(solution)/shard_map/ppermute | solution.py:864
  104.4 5.4 %collective-permute-start.37 = (bf16[2,320,128]{2,1,0:T(8,128)(2,1)S(1)}, bf16[2,320,128]{2,1,0:T(8,128)(2,1)S(1)}, u32[]{:S(2)}, u32[]{:S(2)}) collective-permute-start(bf16[2,320,128]{2,1,0:T(8,128)(2,1)S(1)} %get-tuple-element.138), channel_id=1, source_target_pairs={{0,8},{4,12},{8,0},{12,4},{16,24},{20,28},{24,16},{28,20},{1,9},{5... | collective-permute-start | bytes 491528 | tf_op jit(solution)/shard_map/ppermute | solution.py:864
  105.3 5.3 %collective-permute-start.38 = (bf16[2,320,128]{2,1,0:T(8,128)(2,1)S(1)}, bf16[2,320,128]{2,1,0:T(8,128)(2,1)S(1)}, u32[]{:S(2)}, u32[]{:S(2)}) collective-permute-start(bf16[2,320,128]{2,1,0:T(8,128)(2,1)S(1)} %get-tuple-element.139), channel_id=1, source_target_pairs={{0,16},{4,20},{8,24},{12,28},{16,0},{20,4},{24,8},{28,12},{1,17},{... | collective-permute-start | bytes 491528 | tf_op jit(solution)/shard_map/ppermute | solution.py:864
  110.7 6.3 %collective-permute-start.39 = (bf16[320,128]{1,0:T(8,128)(2,1)S(1)}, bf16[320,128]{1,0:T(8,128)(2,1)S(1)}, u32[]{:S(2)}, u32[]{:S(2)}) collective-permute-start(bf16[320,128]{1,0:T(8,128)(2,1)S(1)} %get-tuple-element.143), channel_id=1, source_target_pairs={{0,1},{1,0},{2,3},{3,2},{4,5},{5,4},{6,7},{7,6},{8,9},{9,8},{10,11... | collective-permute-start | bytes 245768 | tf_op jit(solution)/shard_map/ppermute | solution.py:864
  110.7 6.2 %collective-permute-start.40 = (bf16[320,128]{1,0:T(8,128)(2,1)S(1)}, bf16[320,128]{1,0:T(8,128)(2,1)S(1)}, u32[]{:S(2)}, u32[]{:S(2)}) collective-permute-start(bf16[320,128]{1,0:T(8,128)(2,1)S(1)} %get-tuple-element.144), channel_id=1, source_target_pairs={{0,2},{1,3},{2,0},{3,1},{4,6},{5,7},{6,4},{7,5},{8,10},{9,11},{10,... | collective-permute-start | bytes 245768 | tf_op jit(solution)/shard_map/ppermute | solution.py:864
  112.7 6.3 %collective-permute-start.41 = (bf16[320,128]{1,0:T(8,128)(2,1)S(1)}, bf16[320,128]{1,0:T(8,128)(2,1)S(1)}, u32[]{:S(2)}, u32[]{:S(2)}) collective-permute-start(bf16[320,128]{1,0:T(8,128)(2,1)S(1)} %get-tuple-element.145), channel_id=1, source_target_pairs={{0,3},{1,2},{2,1},{3,0},{4,7},{5,6},{6,5},{7,4},{8,11},{9,10},{10,... | collective-permute-start | bytes 245768 | tf_op jit(solution)/shard_map/ppermute | solution.py:864
  (12 other events, 52.1 us)

commit v6 on v5

--- a/solution.py
+++ b/solution.py
@@ -848,8 +848,9 @@
     copies = []
     for part in range(parts):
         now = pl.ds(part * each, each)
-        ref = grad_a_ref if part < parts // 2 else grad_b_ref
-        grad = ref[pl.ds(part % (parts // 2) * each, each), :]
+        first = grad_a_ref.shape[0] // each
+        ref = grad_a_ref if part < first else grad_b_ref
+        grad = ref[pl.ds((part if part < first else part - first) * each, each), :]
         mask = spread_presence(presence_ref[:, now], width)
         normed = (masked_ref[now, :].astype(F32) - entry_ref[0:1, :]) * inv_scale
         out_ref[now, :] = mask * (factor * (grad - plain - normed * cross))
@@ -1041,7 +1042,7 @@
     total_rows = rows * devices_all
     cube = hypercube_ok()
     tile = math.gcd(rows, 256)
-    half = rows // 2
+    sizes = (rows // 4, rows - rows // 4)
     big = math.gcd(rows, 512)
     me = lax.axis_index(AXES).astype(jnp.int32).reshape(1)
     chunks = [first_params.shape[0] // LANES, second_params.shape[0] // LANES]
@@ -1163,7 +1164,7 @@
     )
     def backward(part, *before):
         return run_kernel(
-            functools.partial(level_one_backward, math.gcd(big, half), part * half),
+            functools.partial(level_one_backward, math.gcd(big, sizes[part]), part * sizes[0]),
             [
                 mixed_grad,
                 masked,
@@ -1179,15 +1180,15 @@
                 *before,
             ],
             [
-                shape((half, width), F32),
+                shape((sizes[part], width), F32),
                 shape((8, width), F32),
                 shape((4, 8, H), F32),
-                shape((half, LANES), BF16),
-                shape((6, half, H), BF16),
-                shape((half, 6 * H), BF16),
+                shape((sizes[part], LANES), BF16),
+                shape((6, sizes[part], H), BF16),
+                shape((sizes[part], 6 * H), BF16),
             ],
             [
-                pltpu.VMEM((math.gcd(big, half), 14 * LANES), F32),
+                pltpu.VMEM((math.gcd(big, sizes[part]), 14 * LANES), F32),
                 pltpu.VMEM((2 * LANES, 14 * LANES), BF16),
                 pltpu.VMEM((2 * H, 2 * LANES), BF16),
             ],
@@ -1288,7 +1289,7 @@
             scalar=True,
         )
 
-    parts = 8 if rows % 1024 == 0 else 2
+    parts = 8 if rows % 1024 == 0 else 4
     input_grad = run_kernel(
         functools.partial(input_kernel, float(total_rows), parts),
         [grad_a, grad_b, masked, fields, entry, sums],

time: 122 us -> 121 us (level)
  transfers between devices with their start and end apart: 42 -> 42, of which waited for: 23 -> 22; matrix products, arithmetic and copies ran while one was open for 0% -> 0% of each run, Pallas kernels for 19% -> 19%
where the time goes in v6:
time: 121 us
  Pallas kernels  48.7 us (40%)
  starting transfers between devices  38.8 us (32%)
  waiting for transfers between devices  32.6 us (27%)
    pallas_call x16, Pallas kernels, run_kernel(): pl.pallas_call(kernel, in_specs=specs, out_specs=out_specs, out_shape=out...  48.7 us
    ppermute x42, starting transfers between devices, xor_permute(): lax.ppermute(value, axis, [(index, index ^ bit) for index in range(size)])  38.8 us
    ppermute x42, waiting for transfers between devices, xor_permute(): lax.ppermute(value, axis, [(index, index ^ bit) for index in range(size)])  32.6 us
  transfers between devices with their start and end apart: 42, of which 22 were waited for; matrix products, arithmetic and copies ran while one was open for 0% of the time, Pallas kernels for 19%

profile of v6, /device:TPU:0, one launch (start us, length us, event | category | flops | bytes accessed | tf_op | source)
XLA Modules:
  0.0 121.1 jit_solution(14392789386648291530)
XLA Ops:
  0.6 2.1 %shard_map.84 = (bf16[1024,512]{1,0:T(8,128)(2,1)S(1)}, bf16[320,128]{1,0:T(8,128)(2,1)S(1)}, bf16[224,128]{1,0:T(8,128)(2,1)S(1)}) custom-call(s32[1]{0:T(128)} %bitcast.me_ref, bf16[1024,512]{1,0:T(8,128)(2,1)} %features_hbm.1, s32[8,1024]{1,0:T(8,128)} %bitcast.6, bf16[292,128]{1,0:T(8,128)(2,1)} %bitcast.9, bf16[215,128]{1,0:T(8,128)(2,1)} %bitcast.10), custom_call_target="tpu_custom_call" | custom-call | flops 1048576 | bytes 1024 | tf_op jit(solution)/shard_map/pallas_call | solution.py:263
  2.8 3.1 %collective-permute-start = (bf16[320,128]{1,0:T(8,128)(2,1)S(1)}, bf16[320,128]{1,0:T(8,128)(2,1)S(1)}, u32[]{:S(2)}, u32[]{:S(2)}) collective-permute-start(bf16[320,128]{1,0:T(8,128)(2,1)S(1)} %get-tuple-element.78.refs_0_), channel_id=1, source_target_pairs={{0,1},{1,0},{2,3},{3,2},{4,5},{5,4},{6,7},{7,6},{8,9},{9,8},{10,11... | collective-permute-start | bytes 245768 | tf_op jit(solution)/shard_map/ppermute | solution.py:865
  5.8 2.6 %collective-permute-start.1 = (bf16[320,128]{1,0:T(8,128)(2,1)S(1)}, bf16[320,128]{1,0:T(8,128)(2,1)S(1)}, u32[]{:S(2)}, u32[]{:S(2)}) collective-permute-start(bf16[320,128]{1,0:T(8,128)(2,1)S(1)} %get-tuple-element.78.refs_0_), channel_id=1, source_target_pairs={{0,2},{1,3},{2,0},{3,1},{4,6},{5,7},{6,4},{7,5},{8,10},{9,11},{10,... | collective-permute-start | bytes 245768 | tf_op jit(solution)/shard_map/ppermute | solution.py:865
  8.4 6.6 %collective-permute-done.1.refs_2_ = bf16[320,128]{1,0:T(8,128)(2,1)S(1)} collective-permute-done((bf16[320,128]{1,0:T(8,128)(2,1)S(1)}, bf16[320,128]{1,0:T(8,128)(2,1)S(1)}, u32[]{:S(2)}, u32[]{:S(2)}) %collective-permute-start.1) | collective-permute-done | bytes 81952 | tf_op jit(solution)/shard_map/ppermute | solution.py:865
  15.1 1.6 %collective-permute-start.6 = (bf16[2,320,128]{2,1,0:T(8,128)(2,1)S(1)}, bf16[2,320,128]{2,1,0:T(8,128)(2,1)S(1)}, u32[]{:S(2)}, u32[]{:S(2)}) collective-permute-start(bf16[2,320,128]{2,1,0:T(8,128)(2,1)S(1)} %get-tuple-element.79.rest_0_), channel_id=1, source_target_pairs={{0,16},{4,20},{8,24},{12,28},{16,0},{20,4},{24,8},{28,12},{1,17},{... | collective-permute-start | bytes 491528 | tf_op jit(solution)/shard_map/ppermute | solution.py:865
  16.6 1.5 %collective-permute-start.8 = (bf16[2,320,128]{2,1,0:T(8,128)(2,1)S(1)}, bf16[2,320,128]{2,1,0:T(8,128)(2,1)S(1)}, u32[]{:S(2)}, u32[]{:S(2)}) collective-permute-start(bf16[2,320,128]{2,1,0:T(8,128)(2,1)S(1)} %get-tuple-element.81.rest_1_), channel_id=1, source_target_pairs={{0,8},{4,12},{8,0},{12,4},{16,24},{20,28},{24,16},{28,20},{1,9},{5... | collective-permute-start | bytes 491528 | tf_op jit(solution)/shard_map/ppermute | solution.py:865
  18.1 2.5 %collective-permute-start.5 = (bf16[224,128]{1,0:T(8,128)(2,1)S(1)}, bf16[224,128]{1,0:T(8,128)(2,1)S(1)}, u32[]{:S(2)}, u32[]{:S(2)}) collective-permute-start(bf16[224,128]{1,0:T(8,128)(2,1)S(1)} %get-tuple-element.80.refs_0_), channel_id=1, source_target_pairs={{0,3},{1,2},{2,1},{3,0},{4,7},{5,6},{6,5},{7,4},{8,11},{9,10},{10,... | collective-permute-start | bytes 172040 | tf_op jit(solution)/shard_map/ppermute | solution.py:865
  21.2 1.4 %collective-permute-start.4 = (bf16[224,128]{1,0:T(8,128)(2,1)S(1)}, bf16[224,128]{1,0:T(8,128)(2,1)S(1)}, u32[]{:S(2)}, u32[]{:S(2)}) collective-permute-start(bf16[224,128]{1,0:T(8,128)(2,1)S(1)} %get-tuple-element.80.refs_0_), channel_id=1, source_target_pairs={{0,2},{1,3},{2,0},{3,1},{4,6},{5,7},{6,4},{7,5},{8,10},{9,11},{10,... | collective-permute-start | bytes 172040 | tf_op jit(solution)/shard_map/ppermute | solution.py:865
  22.5 1.7 %collective-permute-done.5.refs_3_ = bf16[224,128]{1,0:T(8,128)(2,1)S(1)} collective-permute-done((bf16[224,128]{1,0:T(8,128)(2,1)S(1)}, bf16[224,128]{1,0:T(8,128)(2,1)S(1)}, u32[]{:S(2)}, u32[]{:S(2)}) %collective-permute-start.5) | collective-permute-done | bytes 57376 | tf_op jit(solution)/shard_map/ppermute | solution.py:865
  26.8 1.5 %collective-permute-start.9 = (bf16[2,320,128]{2,1,0:T(8,128)(2,1)S(1)}, bf16[2,320,128]{2,1,0:T(8,128)(2,1)S(1)}, u32[]{:S(2)}, u32[]{:S(2)}) collective-permute-start(bf16[2,320,128]{2,1,0:T(8,128)(2,1)S(1)} %collective-permute-done.8.rest_5_), channel_id=1, source_target_pairs={{0,16},{4,20},{8,24},{12,28},{16,0},{20,4},{24,8},{28,12},{1,17},{... | collective-permute-start | bytes 491528 | tf_op jit(solution)/shard_map/ppermute | solution.py:865
  28.4 1.3 %collective-permute-done.12.rest_4_ = bf16[2,320,128]{2,1,0:T(8,128)(2,1)S(1)} collective-permute-done((bf16[2,320,128]{2,1,0:T(8,128)(2,1)S(1)}, bf16[2,320,128]{2,1,0:T(8,128)(2,1)S(1)}, u32[]{:S(2)}, u32[]{:S(2)}) %collective-permute-start.12) | collective-permute-done | bytes 163872 | tf_op jit(solution)/shard_map/ppermute | solution.py:865
  31.3 1.8 %collective-permute-done.7.rest_12_ = bf16[2,320,128]{2,1,0:T(8,128)(2,1)S(1)} collective-permute-done((bf16[2,320,128]{2,1,0:T(8,128)(2,1)S(1)}, bf16[2,320,128]{2,1,0:T(8,128)(2,1)S(1)}, u32[]{:S(2)}, u32[]{:S(2)}) %collective-permute-start.7) | collective-permute-done | bytes 163872 | tf_op jit(solution)/shard_map/ppermute | solution.py:865
  33.7 1.4 %collective-permute-start.25 = (bf16[4,224,128]{2,1,0:T(8,128)(2,1)S(1)}, bf16[4,224,128]{2,1,0:T(8,128)(2,1)S(1)}, u32[]{:S(2)}, u32[]{:S(2)}) collective-permute-start(bf16[4,224,128]{2,1,0:T(8,128)(2,1)S(1)} %shard_map.86.rest_0_), channel_id=1, source_target_pairs={{0,24},{4,28},{8,16},{12,20},{16,8},{20,12},{24,0},{28,4},{1,25},{... | collective-permute-start | bytes 688136 | tf_op jit(solution)/shard_map/ppermute | solution.py:865
  35.1 1.5 %collective-permute-start.23 = (bf16[4,224,128]{2,1,0:T(8,128)(2,1)S(1)}, bf16[4,224,128]{2,1,0:T(8,128)(2,1)S(1)}, u32[]{:S(2)}, u32[]{:S(2)}) collective-permute-start(bf16[4,224,128]{2,1,0:T(8,128)(2,1)S(1)} %shard_map.86.rest_0_), channel_id=1, source_target_pairs={{0,16},{4,20},{8,24},{12,28},{16,0},{20,4},{24,8},{28,12},{1,17},{... | collective-permute-start | bytes 688136 | tf_op jit(solution)/shard_map/ppermute | solution.py:865
  38.9 8.4 %shard_map.87 = (bf16[1024,512]{1,0:T(8,128)(2,1)S(1)}, bf16[6,1024,256]{2,1,0:T(8,128)(2,1)S(1)}, bf16[6,1024,256]{2,1,0:T(8,128)(2,1)S(1)}, bf16[6,1024,256]{2...) custom-call(s32[1]{0:T(128)} %bitcast.me_ref, ...), custom_call_target="tpu_custom_call" | custom-call | flops 1048576 | bytes 1024 | tf_op jit(solution)/shard_map/pallas_call | solution.py:263
  49.8 20.0 %shard_map.88 = (f32[1024,128]{1,0:T(8,128)}, f32[3,1024,256]{2,1,0:T(8,128)S(1)}, bf16[16,224,128]{2,1,0:T(8,128)(2,1)S(1)}, bf16[16,224,128]{2,1,0:T(8,128)(2,1)S(1)}) custom-call(s32[1]{0:T(128)} %bitcast.me_ref, bf16[3,1024,256]{2,1,0:T(8,128)(2,1)S(1)} %get-tuple-element.84.mixed_ref, bf16[1024,128]{1,0:T(8,128)(2,1)S(1)} %copy-done, ...), custom_call_target="tpu_custom_call" | custom-call | flops 1048576 | bytes 1024 | tf_op jit(solution)/shard_map/pallas_call | solution.py:263
  70.1 2.5 %shard_map.89 = (f32[256,512]{1,0:T(8,128)S(1)}, f32[8,512]{1,0:T(8,128)S(1)}, f32[4,8,256]{2,1,0:T(8,128)S(1)}, bf16[256,128]{1,0:T(8,128)(2,1)S(1)}, bf16[6,25...) custom-call(f32[3,1024,256]{2,1,0:T(8,128)S(1)} %get-tuple-element.92.mixed_grad_ref, ...), custom_call_target="tpu_custom_call" | custom-call | flops 1048576 | bytes 1024 | tf_op jit(solution)/shard_map/pallas_call | solution.py:263
  72.9 1.4 %collective-permute-start.28 = (bf16[4,224,128]{2,1,0:T(8,128)(2,1)S(1)}, bf16[4,224,128]{2,1,0:T(8,128)(2,1)S(1)}, u32[]{:S(2)}, u32[]{:S(2)}) collective-permute-start(bf16[4,224,128]{2,1,0:T(8,128)(2,1)S(1)} %get-tuple-element.122), channel_id=1, source_target_pairs={{0,8},{4,12},{8,0},{12,4},{16,24},{20,28},{24,16},{28,20},{1,9},{5... | collective-permute-start | bytes 688136 | tf_op jit(solution)/shard_map/ppermute | solution.py:865
  74.9 1.6 %collective-permute-start.30 = (bf16[4,224,128]{2,1,0:T(8,128)(2,1)S(1)}, bf16[4,224,128]{2,1,0:T(8,128)(2,1)S(1)}, u32[]{:S(2)}, u32[]{:S(2)}) collective-permute-start(bf16[4,224,128]{2,1,0:T(8,128)(2,1)S(1)} %get-tuple-element.124), channel_id=1, source_target_pairs={{0,24},{4,28},{8,16},{12,20},{16,8},{20,12},{24,0},{28,4},{1,25},{... | collective-permute-start | bytes 688136 | tf_op jit(solution)/shard_map/ppermute | solution.py:865
  76.5 7.8 %shard_map.91 = (f32[768,512]{1,0:T(8,128)S(1)}, f32[8,512]{1,0:T(8,128)S(1)}, f32[4,8,256]{2,1,0:T(8,128)S(1)}, bf16[768,128]{1,0:T(8,128)(2,1)S(1)}, bf16[6,76...) custom-call(f32[3,1024,256]{2,1,0:T(8,128)S(1)} %get-tuple-element.92.mixed_grad_ref, ...), custom_call_target="tpu_custom_call" | custom-call | flops 1048576 | bytes 1024 | tf_op jit(solution)/shard_map/pallas_call | solution.py:263
  84.3 4.0 %shard_map.92 = (bf16[16,320,128]{2,1,0:T(8,128)(2,1)S(1)}, bf16[16,320,128]{2,1,0:T(8,128)(2,1)S(1)}) custom-call(s32[1]{0:T(128)} %bitcast.me_ref, bf16[1024,512]{1,0:T(8,128)(2,1)S(1)} %get-tuple-element.110.level_ref, bf16[6,1024,256]{2,1,0:T(8,128)(2,1)S(1)} %get-tuple-element.111.active_ref, f32[8,512]{1,0:T(8,128)S(1)} %get-tuple-element.112.sums_ref, ...), custom_call_target="tpu_custom_call" | custom-call | flops 1048576 | bytes 1024 | tf_op jit(solution)/shard_map/pallas_call | solution.py:263
  88.5 3.0 %collective-permute-done.31.got_ref = bf16[16,320,128]{2,1,0:T(8,128)(2,1)S(1)} collective-permute-done((bf16[16,320,128]{2,1,0:T(8,128)(2,1)S(1)}, bf16[16,320,128]{2,1,0:T(8,128)(2,1)S(1)}, u32[]{:S(2)}, u32[]{:S(2)}) %collective-permute-start.31) | collective-permute-done | bytes 1310752 | tf_op jit(solution)/shard_map/ppermute | solution.py:865
  94.8 2.0 %collective-permute-start.33 = (bf16[224,128]{1,0:T(8,128)(2,1)S(1)}, bf16[224,128]{1,0:T(8,128)(2,1)S(1)}, u32[]{:S(2)}, u32[]{:S(2)}) collective-permute-start(bf16[224,128]{1,0:T(8,128)(2,1)S(1)} %get-tuple-element.129), channel_id=1, source_target_pairs={{0,2},{1,3},{2,0},{3,1},{4,6},{5,7},{6,4},{7,5},{8,10},{9,11},{10,... | collective-permute-start | bytes 172040 | tf_op jit(solution)/shard_map/ppermute | solution.py:865
  96.8 1.3 %collective-permute-start.34 = (bf16[224,128]{1,0:T(8,128)(2,1)S(1)}, bf16[224,128]{1,0:T(8,128)(2,1)S(1)}, u32[]{:S(2)}, u32[]{:S(2)}) collective-permute-start(bf16[224,128]{1,0:T(8,128)(2,1)S(1)} %get-tuple-element.130), channel_id=1, source_target_pairs={{0,3},{1,2},{2,1},{3,0},{4,7},{5,6},{6,5},{7,4},{8,11},{9,10},{10,... | collective-permute-start | bytes 172040 | tf_op jit(solution)/shard_map/ppermute | solution.py:865
  98.6 2.7 %collective-permute-done.33.two_ref = bf16[224,128]{1,0:T(8,128)(2,1)S(1)} collective-permute-done((bf16[224,128]{1,0:T(8,128)(2,1)S(1)}, bf16[224,128]{1,0:T(8,128)(2,1)S(1)}, u32[]{:S(2)}, u32[]{:S(2)}) %collective-permute-start.33) | collective-permute-done | bytes 57376 | tf_op jit(solution)/shard_map/ppermute | solution.py:865
  101.3 1.5 %collective-permute-done.34.three_ref = bf16[224,128]{1,0:T(8,128)(2,1)S(1)} collective-permute-done((bf16[224,128]{1,0:T(8,128)(2,1)S(1)}, bf16[224,128]{1,0:T(8,128)(2,1)S(1)}, u32[]{:S(2)}, u32[]{:S(2)}) %collective-permute-start.34) | collective-permute-done | bytes 57376 | tf_op jit(solution)/shard_map/ppermute | solution.py:865
  105.8 3.3 %collective-permute-done.37.got_one_ref = bf16[2,320,128]{2,1,0:T(8,128)(2,1)S(1)} collective-permute-done((bf16[2,320,128]{2,1,0:T(8,128)(2,1)S(1)}, bf16[2,320,128]{2,1,0:T(8,128)(2,1)S(1)}, u32[]{:S(2)}, u32[]{:S(2)}) %collective-permute-start.37) | collective-permute-done | bytes 163872 | tf_op jit(solution)/shard_map/ppermute | solution.py:865
  110.2 2.0 %collective-permute-start.40 = (bf16[320,128]{1,0:T(8,128)(2,1)S(1)}, bf16[320,128]{1,0:T(8,128)(2,1)S(1)}, u32[]{:S(2)}, u32[]{:S(2)}) collective-permute-start(bf16[320,128]{1,0:T(8,128)(2,1)S(1)} %get-tuple-element.144), channel_id=1, source_target_pairs={{0,2},{1,3},{2,0},{3,1},{4,6},{5,7},{6,4},{7,5},{8,10},{9,11},{10,... | collective-permute-start | bytes 245768 | tf_op jit(solution)/shard_map/ppermute | solution.py:865
  112.2 2.4 %collective-permute-start.41 = (bf16[320,128]{1,0:T(8,128)(2,1)S(1)}, bf16[320,128]{1,0:T(8,128)(2,1)S(1)}, u32[]{:S(2)}, u32[]{:S(2)}) collective-permute-start(bf16[320,128]{1,0:T(8,128)(2,1)S(1)} %get-tuple-element.145), channel_id=1, source_target_pairs={{0,3},{1,2},{2,1},{3,0},{4,7},{5,6},{6,5},{7,4},{8,11},{9,10},{10,... | collective-permute-start | bytes 245768 | tf_op jit(solution)/shard_map/ppermute | solution.py:865
  114.6 1.8 %collective-permute-done.39.one_ref = bf16[320,128]{1,0:T(8,128)(2,1)S(1)} collective-permute-done((bf16[320,128]{1,0:T(8,128)(2,1)S(1)}, bf16[320,128]{1,0:T(8,128)(2,1)S(1)}, u32[]{:S(2)}, u32[]{:S(2)}) %collective-permute-start.39) | collective-permute-done | bytes 81952 | tf_op jit(solution)/shard_map/ppermute | solution.py:865
  116.4 2.2 %collective-permute-done.41.three_ref = bf16[320,128]{1,0:T(8,128)(2,1)S(1)} collective-permute-done((bf16[320,128]{1,0:T(8,128)(2,1)S(1)}, bf16[320,128]{1,0:T(8,128)(2,1)S(1)}, u32[]{:S(2)}, u32[]{:S(2)}) %collective-permute-start.41) | collective-permute-done | bytes 81952 | tf_op jit(solution)/shard_map/ppermute | solution.py:865
  119.3 1.6 %shard_map.99 = f32[1024,512]{1,0:T(8,128)} custom-call(f32[256,512]{1,0:T(8,128)S(1)} %get-tuple-element.101.grad_a_ref, f32[768,512]{1,0:T(8,128)S(1)} %get-tuple-element.109.grad_b_ref, bf16[1024,512]{1,0:T(8,128)(2,1)S(1)} %get-tuple-element.83.masked_ref, s32[8,1024]{1,0:T(8,128)S(1)} %bitcast.7, f32[8,512]{1,0:T(8,128)S(1)} %get-tuple-element.86.entry_ref, ...), custom_call_target="tpu_custom_call" | custom-call | flops 1048576 | bytes 1024 | tf_op jit(solution)/shard_map/pallas_call | solution.py:263
  (72 shorter events, 20.0 us)
Async XLA Ops:
  2.8 5.7 %collective-permute-start = (bf16[320,128]{1,0:T(8,128)(2,1)S(1)}, bf16[320,128]{1,0:T(8,128)(2,1)S(1)}, u32[]{:S(2)}, u32[]{:S(2)}) collective-permute-start(bf16[320,128]{1,0:T(8,128)(2,1)S(1)} %get-tuple-element.78.refs_0_), channel_id=1, source_target_pairs={{0,1},{1,0},{2,3},{3,2},{4,5},{5,4},{6,7},{7,6},{8,9},{9,8},{10,11... | collective-permute-start | bytes 245768 | tf_op jit(solution)/shard_map/ppermute | solution.py:865
  5.8 9.2 %collective-permute-start.1 = (bf16[320,128]{1,0:T(8,128)(2,1)S(1)}, bf16[320,128]{1,0:T(8,128)(2,1)S(1)}, u32[]{:S(2)}, u32[]{:S(2)}) collective-permute-start(bf16[320,128]{1,0:T(8,128)(2,1)S(1)} %get-tuple-element.78.refs_0_), channel_id=1, source_target_pairs={{0,2},{1,3},{2,0},{3,1},{4,6},{5,7},{6,4},{7,5},{8,10},{9,11},{10,... | collective-permute-start | bytes 245768 | tf_op jit(solution)/shard_map/ppermute | solution.py:865
  8.4 6.6 %collective-permute-start.2 = (bf16[320,128]{1,0:T(8,128)(2,1)S(1)}, bf16[320,128]{1,0:T(8,128)(2,1)S(1)}, u32[]{:S(2)}, u32[]{:S(2)}) collective-permute-start(bf16[320,128]{1,0:T(8,128)(2,1)S(1)} %get-tuple-element.78.refs_0_), channel_id=1, source_target_pairs={{0,3},{1,2},{2,1},{3,0},{4,7},{5,6},{6,5},{7,4},{8,11},{9,10},{10,... | collective-permute-start | bytes 245768 | tf_op jit(solution)/shard_map/ppermute | solution.py:865
  15.1 11.2 %collective-permute-start.6 = (bf16[2,320,128]{2,1,0:T(8,128)(2,1)S(1)}, bf16[2,320,128]{2,1,0:T(8,128)(2,1)S(1)}, u32[]{:S(2)}, u32[]{:S(2)}) collective-permute-start(bf16[2,320,128]{2,1,0:T(8,128)(2,1)S(1)} %get-tuple-element.79.rest_0_), channel_id=1, source_target_pairs={{0,16},{4,20},{8,24},{12,28},{16,0},{20,4},{24,8},{28,12},{1,17},{... | collective-permute-start | bytes 491528 | tf_op jit(solution)/shard_map/ppermute | solution.py:865
  16.6 10.2 %collective-permute-start.8 = (bf16[2,320,128]{2,1,0:T(8,128)(2,1)S(1)}, bf16[2,320,128]{2,1,0:T(8,128)(2,1)S(1)}, u32[]{:S(2)}, u32[]{:S(2)}) collective-permute-start(bf16[2,320,128]{2,1,0:T(8,128)(2,1)S(1)} %get-tuple-element.81.rest_1_), channel_id=1, source_target_pairs={{0,8},{4,12},{8,0},{12,4},{16,24},{20,28},{24,16},{28,20},{1,9},{5... | collective-permute-start | bytes 491528 | tf_op jit(solution)/shard_map/ppermute | solution.py:865
  18.1 6.1 %collective-permute-start.5 = (bf16[224,128]{1,0:T(8,128)(2,1)S(1)}, bf16[224,128]{1,0:T(8,128)(2,1)S(1)}, u32[]{:S(2)}, u32[]{:S(2)}) collective-permute-start(bf16[224,128]{1,0:T(8,128)(2,1)S(1)} %get-tuple-element.80.refs_0_), channel_id=1, source_target_pairs={{0,3},{1,2},{2,1},{3,0},{4,7},{5,6},{6,5},{7,4},{8,11},{9,10},{10,... | collective-permute-start | bytes 172040 | tf_op jit(solution)/shard_map/ppermute | solution.py:865
  20.6 4.3 %collective-permute-start.3 = (bf16[224,128]{1,0:T(8,128)(2,1)S(1)}, bf16[224,128]{1,0:T(8,128)(2,1)S(1)}, u32[]{:S(2)}, u32[]{:S(2)}) collective-permute-start(bf16[224,128]{1,0:T(8,128)(2,1)S(1)} %get-tuple-element.80.refs_0_), channel_id=1, source_target_pairs={{0,1},{1,0},{2,3},{3,2},{4,5},{5,4},{6,7},{7,6},{8,9},{9,8},{10,11... | collective-permute-start | bytes 172040 | tf_op jit(solution)/shard_map/ppermute | solution.py:865
  21.2 5.1 %collective-permute-start.4 = (bf16[224,128]{1,0:T(8,128)(2,1)S(1)}, bf16[224,128]{1,0:T(8,128)(2,1)S(1)}, u32[]{:S(2)}, u32[]{:S(2)}) collective-permute-start(bf16[224,128]{1,0:T(8,128)(2,1)S(1)} %get-tuple-element.80.refs_0_), channel_id=1, source_target_pairs={{0,2},{1,3},{2,0},{3,1},{4,6},{5,7},{6,4},{7,5},{8,10},{9,11},{10,... | collective-permute-start | bytes 172040 | tf_op jit(solution)/shard_map/ppermute | solution.py:865
  24.2 5.5 %collective-permute-start.12 = (bf16[2,320,128]{2,1,0:T(8,128)(2,1)S(1)}, bf16[2,320,128]{2,1,0:T(8,128)(2,1)S(1)}, u32[]{:S(2)}, u32[]{:S(2)}) collective-permute-start(bf16[2,320,128]{2,1,0:T(8,128)(2,1)S(1)} %get-tuple-element.79.rest_0_), channel_id=1, source_target_pairs={{0,8},{4,12},{8,0},{12,4},{16,24},{20,28},{24,16},{28,20},{1,9},{5... | collective-permute-start | bytes 491528 | tf_op jit(solution)/shard_map/ppermute | solution.py:865
  24.9 5.9 %collective-permute-start.15 = (bf16[2,320,128]{2,1,0:T(8,128)(2,1)S(1)}, bf16[2,320,128]{2,1,0:T(8,128)(2,1)S(1)}, u32[]{:S(2)}, u32[]{:S(2)}) collective-permute-start(bf16[2,320,128]{2,1,0:T(8,128)(2,1)S(1)} %get-tuple-element.81.rest_1_), channel_id=1, source_target_pairs={{0,16},{4,20},{8,24},{12,28},{16,0},{20,4},{24,8},{28,12},{1,17},{... | collective-permute-start | bytes 491528 | tf_op jit(solution)/shard_map/ppermute | solution.py:865
  26.2 4.5 %collective-permute-start.10 = (bf16[2,320,128]{2,1,0:T(8,128)(2,1)S(1)}, bf16[2,320,128]{2,1,0:T(8,128)(2,1)S(1)}, u32[]{:S(2)}, u32[]{:S(2)}) collective-permute-start(bf16[2,320,128]{2,1,0:T(8,128)(2,1)S(1)} %get-tuple-element.79.rest_0_), channel_id=1, source_target_pairs={{0,4},{4,0},{8,12},{12,8},{16,20},{20,16},{24,28},{28,24},{1,5},{5... | collective-permute-start | bytes 491528 | tf_op jit(solution)/shard_map/ppermute | solution.py:865
  26.2 6.8 %collective-permute-start.7 = (bf16[2,320,128]{2,1,0:T(8,128)(2,1)S(1)}, bf16[2,320,128]{2,1,0:T(8,128)(2,1)S(1)}, u32[]{:S(2)}, u32[]{:S(2)}) collective-permute-start(bf16[2,320,128]{2,1,0:T(8,128)(2,1)S(1)} %collective-permute-done.6.rest_8_), channel_id=1, source_target_pairs={{0,8},{4,12},{8,0},{12,4},{16,24},{20,28},{24,16},{28,20},{1,9},{5... | collective-permute-start | bytes 491528 | tf_op jit(solution)/shard_map/ppermute | solution.py:865
  26.8 6.9 %collective-permute-start.9 = (bf16[2,320,128]{2,1,0:T(8,128)(2,1)S(1)}, bf16[2,320,128]{2,1,0:T(8,128)(2,1)S(1)}, u32[]{:S(2)}, u32[]{:S(2)}) collective-permute-start(bf16[2,320,128]{2,1,0:T(8,128)(2,1)S(1)} %collective-permute-done.8.rest_5_), channel_id=1, source_target_pairs={{0,16},{4,20},{8,24},{12,28},{16,0},{20,4},{24,8},{28,12},{1,17},{... | collective-permute-start | bytes 491528 | tf_op jit(solution)/shard_map/ppermute | solution.py:865
  30.8 4.4 %collective-permute-start.16 = (bf16[2,320,128]{2,1,0:T(8,128)(2,1)S(1)}, bf16[2,320,128]{2,1,0:T(8,128)(2,1)S(1)}, u32[]{:S(2)}, u32[]{:S(2)}) collective-permute-start(bf16[2,320,128]{2,1,0:T(8,128)(2,1)S(1)} %collective-permute-done.6.rest_8_), channel_id=1, source_target_pairs={{0,4},{4,0},{8,12},{12,8},{16,20},{20,16},{24,28},{28,24},{1,5},{5... | collective-permute-start | bytes 491528 | tf_op jit(solution)/shard_map/ppermute | solution.py:865
  30.8 5.9 %collective-permute-start.13 = (bf16[2,320,128]{2,1,0:T(8,128)(2,1)S(1)}, bf16[2,320,128]{2,1,0:T(8,128)(2,1)S(1)}, u32[]{:S(2)}, u32[]{:S(2)}) collective-permute-start(bf16[2,320,128]{2,1,0:T(8,128)(2,1)S(1)} %collective-permute-done.12.rest_4_), channel_id=1, source_target_pairs={{0,4},{4,0},{8,12},{12,8},{16,20},{20,16},{24,28},{28,24},{1,5},{5... | collective-permute-start | bytes 491528 | tf_op jit(solution)/shard_map/ppermute | solution.py:865
  33.0 4.3 %collective-permute-start.14 = (bf16[2,320,128]{2,1,0:T(8,128)(2,1)S(1)}, bf16[2,320,128]{2,1,0:T(8,128)(2,1)S(1)}, u32[]{:S(2)}, u32[]{:S(2)}) collective-permute-start(bf16[2,320,128]{2,1,0:T(8,128)(2,1)S(1)} %collective-permute-done.8.rest_5_), channel_id=1, source_target_pairs={{0,4},{4,0},{8,12},{12,8},{16,20},{20,16},{24,28},{28,24},{1,5},{5... | collective-permute-start | bytes 491528 | tf_op jit(solution)/shard_map/ppermute | solution.py:865
  33.7 13.9 %collective-permute-start.25 = (bf16[4,224,128]{2,1,0:T(8,128)(2,1)S(1)}, bf16[4,224,128]{2,1,0:T(8,128)(2,1)S(1)}, u32[]{:S(2)}, u32[]{:S(2)}) collective-permute-start(bf16[4,224,128]{2,1,0:T(8,128)(2,1)S(1)} %shard_map.86.rest_0_), channel_id=1, source_target_pairs={{0,24},{4,28},{8,16},{12,20},{16,8},{20,12},{24,0},{28,4},{1,25},{... | collective-permute-start | bytes 688136 | tf_op jit(solution)/shard_map/ppermute | solution.py:865
  35.1 12.8 %collective-permute-start.23 = (bf16[4,224,128]{2,1,0:T(8,128)(2,1)S(1)}, bf16[4,224,128]{2,1,0:T(8,128)(2,1)S(1)}, u32[]{:S(2)}, u32[]{:S(2)}) collective-permute-start(bf16[4,224,128]{2,1,0:T(8,128)(2,1)S(1)} %shard_map.86.rest_0_), channel_id=1, source_target_pairs={{0,16},{4,20},{8,24},{12,28},{16,0},{20,4},{24,8},{28,12},{1,17},{... | collective-permute-start | bytes 688136 | tf_op jit(solution)/shard_map/ppermute | solution.py:865
  36.6 11.5 %collective-permute-start.21 = (bf16[4,224,128]{2,1,0:T(8,128)(2,1)S(1)}, bf16[4,224,128]{2,1,0:T(8,128)(2,1)S(1)}, u32[]{:S(2)}, u32[]{:S(2)}) collective-permute-start(bf16[4,224,128]{2,1,0:T(8,128)(2,1)S(1)} %shard_map.86.rest_0_), channel_id=1, source_target_pairs={{0,8},{4,12},{8,0},{12,4},{16,24},{20,28},{24,16},{28,20},{1,9},{5... | collective-permute-start | bytes 688136 | tf_op jit(solution)/shard_map/ppermute | solution.py:865
  72.9 15.4 %collective-permute-start.28 = (bf16[4,224,128]{2,1,0:T(8,128)(2,1)S(1)}, bf16[4,224,128]{2,1,0:T(8,128)(2,1)S(1)}, u32[]{:S(2)}, u32[]{:S(2)}) collective-permute-start(bf16[4,224,128]{2,1,0:T(8,128)(2,1)S(1)} %get-tuple-element.122), channel_id=1, source_target_pairs={{0,8},{4,12},{8,0},{12,4},{16,24},{20,28},{24,16},{28,20},{1,9},{5... | collective-permute-start | bytes 688136 | tf_op jit(solution)/shard_map/ppermute | solution.py:865
  74.4 13.9 %collective-permute-start.29 = (bf16[4,224,128]{2,1,0:T(8,128)(2,1)S(1)}, bf16[4,224,128]{2,1,0:T(8,128)(2,1)S(1)}, u32[]{:S(2)}, u32[]{:S(2)}) collective-permute-start(bf16[4,224,128]{2,1,0:T(8,128)(2,1)S(1)} %get-tuple-element.123), channel_id=1, source_target_pairs={{0,16},{4,20},{8,24},{12,28},{16,0},{20,4},{24,8},{28,12},{1,17},{... | collective-permute-start | bytes 688136 | tf_op jit(solution)/shard_map/ppermute | solution.py:865
  74.9 13.4 %collective-permute-start.30 = (bf16[4,224,128]{2,1,0:T(8,128)(2,1)S(1)}, bf16[4,224,128]{2,1,0:T(8,128)(2,1)S(1)}, u32[]{:S(2)}, u32[]{:S(2)}) collective-permute-start(bf16[4,224,128]{2,1,0:T(8,128)(2,1)S(1)} %get-tuple-element.124), channel_id=1, source_target_pairs={{0,24},{4,28},{8,16},{12,20},{16,8},{20,12},{24,0},{28,4},{1,25},{... | collective-permute-start | bytes 688136 | tf_op jit(solution)/shard_map/ppermute | solution.py:865
  91.8 11.6 %collective-permute-start.35 = (bf16[4,320,128]{2,1,0:T(8,128)(2,1)S(1)}, bf16[4,320,128]{2,1,0:T(8,128)(2,1)S(1)}, u32[]{:S(2)}, u32[]{:S(2)}) collective-permute-start(bf16[4,320,128]{2,1,0:T(8,128)(2,1)S(1)} %get-tuple-element.133), channel_id=1, source_target_pairs={{0,16},{4,20},{8,24},{12,28},{16,0},{20,4},{24,8},{28,12},{1,17},{... | collective-permute-start | bytes 983048 | tf_op jit(solution)/shard_map/ppermute | solution.py:865
  92.8 10.7 %collective-permute-start.36 = (bf16[4,320,128]{2,1,0:T(8,128)(2,1)S(1)}, bf16[4,320,128]{2,1,0:T(8,128)(2,1)S(1)}, u32[]{:S(2)}, u32[]{:S(2)}) collective-permute-start(bf16[4,320,128]{2,1,0:T(8,128)(2,1)S(1)} %get-tuple-element.134), channel_id=1, source_target_pairs={{0,8},{4,12},{8,0},{12,4},{16,24},{20,28},{24,16},{28,20},{1,9},{5... | collective-permute-start | bytes 983048 | tf_op jit(solution)/shard_map/ppermute | solution.py:865
  93.8 4.8 %collective-permute-start.32 = (bf16[224,128]{1,0:T(8,128)(2,1)S(1)}, bf16[224,128]{1,0:T(8,128)(2,1)S(1)}, u32[]{:S(2)}, u32[]{:S(2)}) collective-permute-start(bf16[224,128]{1,0:T(8,128)(2,1)S(1)} %get-tuple-element.128), channel_id=1, source_target_pairs={{0,1},{1,0},{2,3},{3,2},{4,5},{5,4},{6,7},{7,6},{8,9},{9,8},{10,11... | collective-permute-start | bytes 172040 | tf_op jit(solution)/shard_map/ppermute | solution.py:865
  94.8 6.5 %collective-permute-start.33 = (bf16[224,128]{1,0:T(8,128)(2,1)S(1)}, bf16[224,128]{1,0:T(8,128)(2,1)S(1)}, u32[]{:S(2)}, u32[]{:S(2)}) collective-permute-start(bf16[224,128]{1,0:T(8,128)(2,1)S(1)} %get-tuple-element.129), channel_id=1, source_target_pairs={{0,2},{1,3},{2,0},{3,1},{4,6},{5,7},{6,4},{7,5},{8,10},{9,11},{10,... | collective-permute-start | bytes 172040 | tf_op jit(solution)/shard_map/ppermute | solution.py:865
  96.8 6.0 %collective-permute-start.34 = (bf16[224,128]{1,0:T(8,128)(2,1)S(1)}, bf16[224,128]{1,0:T(8,128)(2,1)S(1)}, u32[]{:S(2)}, u32[]{:S(2)}) collective-permute-start(bf16[224,128]{1,0:T(8,128)(2,1)S(1)} %get-tuple-element.130), channel_id=1, source_target_pairs={{0,3},{1,2},{2,1},{3,0},{4,7},{5,6},{6,5},{7,4},{8,11},{9,10},{10,... | collective-permute-start | bytes 172040 | tf_op jit(solution)/shard_map/ppermute | solution.py:865
  103.6 5.4 %collective-permute-start.37 = (bf16[2,320,128]{2,1,0:T(8,128)(2,1)S(1)}, bf16[2,320,128]{2,1,0:T(8,128)(2,1)S(1)}, u32[]{:S(2)}, u32[]{:S(2)}) collective-permute-start(bf16[2,320,128]{2,1,0:T(8,128)(2,1)S(1)} %get-tuple-element.138), channel_id=1, source_target_pairs={{0,8},{4,12},{8,0},{12,4},{16,24},{20,28},{24,16},{28,20},{1,9},{5... | collective-permute-start | bytes 491528 | tf_op jit(solution)/shard_map/ppermute | solution.py:865
  104.8 5.3 %collective-permute-start.38 = (bf16[2,320,128]{2,1,0:T(8,128)(2,1)S(1)}, bf16[2,320,128]{2,1,0:T(8,128)(2,1)S(1)}, u32[]{:S(2)}, u32[]{:S(2)}) collective-permute-start(bf16[2,320,128]{2,1,0:T(8,128)(2,1)S(1)} %get-tuple-element.139), channel_id=1, source_target_pairs={{0,16},{4,20},{8,24},{12,28},{16,0},{20,4},{24,8},{28,12},{1,17},{... | collective-permute-start | bytes 491528 | tf_op jit(solution)/shard_map/ppermute | solution.py:865
  110.2 6.2 %collective-permute-start.39 = (bf16[320,128]{1,0:T(8,128)(2,1)S(1)}, bf16[320,128]{1,0:T(8,128)(2,1)S(1)}, u32[]{:S(2)}, u32[]{:S(2)}) collective-permute-start(bf16[320,128]{1,0:T(8,128)(2,1)S(1)} %get-tuple-element.143), channel_id=1, source_target_pairs={{0,1},{1,0},{2,3},{3,2},{4,5},{5,4},{6,7},{7,6},{8,9},{9,8},{10,11... | collective-permute-start | bytes 245768 | tf_op jit(solution)/shard_map/ppermute | solution.py:865
  110.2 6.2 %collective-permute-start.40 = (bf16[320,128]{1,0:T(8,128)(2,1)S(1)}, bf16[320,128]{1,0:T(8,128)(2,1)S(1)}, u32[]{:S(2)}, u32[]{:S(2)}) collective-permute-start(bf16[320,128]{1,0:T(8,128)(2,1)S(1)} %get-tuple-element.144), channel_id=1, source_target_pairs={{0,2},{1,3},{2,0},{3,1},{4,6},{5,7},{6,4},{7,5},{8,10},{9,11},{10,... | collective-permute-start | bytes 245768 | tf_op jit(solution)/shard_map/ppermute | solution.py:865
  112.2 6.3 %collective-permute-start.41 = (bf16[320,128]{1,0:T(8,128)(2,1)S(1)}, bf16[320,128]{1,0:T(8,128)(2,1)S(1)}, u32[]{:S(2)}, u32[]{:S(2)}) collective-permute-start(bf16[320,128]{1,0:T(8,128)(2,1)S(1)} %get-tuple-element.145), channel_id=1, source_target_pairs={{0,3},{1,2},{2,1},{3,0},{4,7},{5,6},{6,5},{7,4},{8,11},{9,10},{10,... | collective-permute-start | bytes 245768 | tf_op jit(solution)/shard_map/ppermute | solution.py:865
  (12 other events, 97.6 us)
